TPU v7x, 32 devices: a whole 2x2x4 slice. The times are simulated.
32 devices in a mesh: seq: 16 (over z, x, core), uly: 2 (over y).
Axes of the slice: x: 2, y: 2, z: 4, core: 2. Of those that a mesh axis runs over, the one named last changes fastest.
Arguments:
- normed: bfloat16 [4096, 5376], P('seq', 'uly'), may hold values from -6 to 6
- q_raw: bfloat16 [4096, 2048], P('seq', 'uly'), may hold values from -6 to 6
- key_weight: bfloat16 [5376, 1024], P('uly', 'seq'), may hold values from -0.078125 to 0.078125
- value_weight: bfloat16 [5376, 1024], P('uly', 'seq'), may hold values from -0.078125 to 0.078125
- q_gain: float32 [128], replicated, may hold values from 0.1 to 1.9
- k_gain: float32 [128], replicated, may hold values from 0.1 to 1.9
- segment_ids: int32 [4096], replicated, may hold values from 0 to 1, as said below
- grad_out: bfloat16 [4096, 2048], P('seq', 'uly'), may hold values from -6 to 6
Outputs:
- attention: bfloat16 [4096, 2048], P('seq', 'uly')
- grad_normed: bfloat16 [4096, 5376], P('seq', 'uly')
- grad_q: bfloat16 [4096, 2048], P('seq', 'uly')
- grad_key_weight: float32 [5376, 1024], P('uly', 'seq')
- grad_value_weight: float32 [5376, 1024], P('uly', 'seq')
Inputs may be any that keep to these rules, and one draw needn't show every extreme that they name: `segment_ids`: 0 up to one position and 1 from it on; that position lies between 1024 and 3072.
All inputs are finite; a program needn't handle non-finite values.
Results may differ from a plain program's by a relative error of at most 0.025.
Values may be sent and summed in bfloat16 or wider, within the bound.
No kernel may reach another device: no remote copies, remote signals or barrier semaphores. Data moves between devices by JAX's collectives and lax.ppermute only.
A program may use at most 128 MiB of HBM per device.

v0:
```python
import jax
import jax.numpy as jnp
from jax import lax
from jax.sharding import PartitionSpec as P

HD = 128
WINDOW = 1024


epsilon = 1e-06
query_scale = 168.0 ** (-0.5)


def from_behind(array, axis, by):
    devices = lax.axis_size(axis)
    pairs = [(i, i + by) for i in range(devices) if 0 <= i + by < devices]
    return lax.ppermute(array, axis, pairs)


def normalize(raw_vals, gain, factor):
    mean_sq = jnp.mean(raw_vals * raw_vals, axis=-1, keepdims=True)
    return raw_vals * lax.rsqrt(mean_sq + epsilon) * gain * factor


def attend_block(
    queries, key_block, value_block, grad_block, query_pos, key_pos, query_seg, key_seg
):
    scores = jnp.einsum("bhge,lhe->hgbl", queries, key_block, preferred_element_type=jnp.float32)
    allowed = (
        (key_pos[None, :] <= query_pos[:, None])
        & (key_pos[None, :] > query_pos[:, None] - WINDOW)
        & (key_seg[None, :] == query_seg[:, None])
    )
    exp_scores = jnp.where(allowed[None, None], jnp.exp(scores), 0.0)
    probs = exp_scores / jnp.sum(exp_scores, axis=-1, keepdims=True)
    weights = probs.astype(jnp.bfloat16)
    attended = jnp.einsum(
        "hgbl,lhe->bhge", weights, value_block, preferred_element_type=jnp.float32
    ).astype(jnp.bfloat16)
    dprob = jnp.einsum(
        "bhge,lhe->hgbl", grad_block, value_block, preferred_element_type=jnp.float32
    )
    delta_row = jnp.sum(probs * dprob, axis=-1, keepdims=True)
    dscore = (probs * (dprob - delta_row)).astype(jnp.bfloat16)
    dquery = jnp.einsum("hgbl,lhe->bhge", dscore, key_block, preferred_element_type=jnp.float32)
    dkey = jnp.einsum("hgbl,bhge->lhe", dscore, queries, preferred_element_type=jnp.float32)
    dvalue = jnp.einsum("hgbl,bhge->lhe", weights, grad_block, preferred_element_type=jnp.float32)
    return (attended, dquery, dkey, dvalue)


def body(normed, q_raw, key_weight, value_weight, q_gain, k_gain, segment_ids, grad_out):
    rows_here = normed.shape[0]
    heads_here = q_raw.shape[1] // (2 * HD)
    seq_index = lax.axis_index("seq")
    base_row = seq_index * rows_here
    weight_pair = (
        lax.all_gather(key_weight, "seq", axis=1, tiled=True),
        lax.all_gather(value_weight, "seq", axis=1, tiled=True),
    )
    key_term = jnp.dot(normed, weight_pair[0], preferred_element_type=jnp.float32)
    value_term = jnp.dot(normed, weight_pair[1], preferred_element_type=jnp.float32)
    key_raw, value_raw = (
        lax.psum_scatter(
            key_term.astype(jnp.bfloat16), "uly", scatter_dimension=1, tiled=True
        ).astype(jnp.float32),
        lax.psum_scatter(
            value_term.astype(jnp.bfloat16), "uly", scatter_dimension=1, tiled=True
        ).astype(jnp.float32),
    )
    key_in = key_raw.reshape(rows_here, heads_here, HD)
    keys_bf = normalize(key_in, k_gain, 1.0).astype(jnp.bfloat16)
    values_bf = value_raw.reshape(rows_here, heads_here, HD).astype(jnp.bfloat16)
    query_in = q_raw.astype(jnp.float32).reshape(rows_here, heads_here, 2, HD)
    queries = normalize(query_in, q_gain, query_scale).astype(jnp.bfloat16)
    grad_heads = grad_out.reshape(rows_here, heads_here, 2, HD)
    stacked = jnp.stack([keys_bf, values_bf])
    distance_most = -(-WINDOW // rows_here)
    pieces = []
    for distance in range(distance_most, 0, -1):
        first_row = max(0, distance * rows_here - WINDOW)
        pieces.append(from_behind(stacked, "seq", distance))
    pieces.append(stacked)
    extended = jnp.concatenate(pieces, axis=1)
    block_rows = min(512, rows_here)
    span_rows = block_rows + WINDOW
    count_blocks = rows_here // block_rows
    seg_pad = jnp.concatenate([jnp.full((WINDOW,), -1, jnp.int32), segment_ids])
    query_seg_all = lax.dynamic_slice_in_dim(segment_ids, base_row, rows_here, 0)
    key_seg_all = lax.dynamic_slice_in_dim(seg_pad, base_row, WINDOW + rows_here, 0)

    def step(grad_acc, block_index):
        begin_row = block_index * block_rows
        query_pos = base_row + begin_row + jnp.arange(block_rows, dtype=jnp.int32)
        key_pos = base_row + begin_row - WINDOW + jnp.arange(span_rows, dtype=jnp.int32)
        key_block = lax.dynamic_slice_in_dim(extended, begin_row, span_rows, 1)
        attended, dquery, dkey, dvalue = attend_block(
            lax.dynamic_slice_in_dim(queries, begin_row, block_rows, 0),
            key_block[0],
            key_block[1],
            lax.dynamic_slice_in_dim(grad_heads, begin_row, block_rows, 0),
            query_pos,
            key_pos,
            lax.dynamic_slice_in_dim(query_seg_all, begin_row, block_rows, 0),
            lax.dynamic_slice_in_dim(key_seg_all, begin_row, span_rows, 0),
        )
        update = jnp.stack([dkey, dvalue])
        grad_acc = lax.dynamic_update_slice_in_dim(
            grad_acc,
            lax.dynamic_slice_in_dim(grad_acc, begin_row, span_rows, 1) + update,
            begin_row,
            1,
        )
        return (grad_acc, (attended, dquery))

    zero_acc = jnp.zeros((2, WINDOW + rows_here, heads_here, HD), jnp.float32)
    grad_acc, (attended, dquery) = lax.scan(
        step, zero_acc, jnp.arange(count_blocks, dtype=jnp.int32)
    )
    attention = attended.reshape(rows_here, 2 * heads_here * HD)
    dquery = dquery.reshape(rows_here, heads_here, 2, HD)
    own_grads = grad_acc[:, WINDOW:]
    offset_row = 0
    for distance in range(distance_most, 0, -1):
        first_row = max(0, distance * rows_here - WINDOW)
        piece_rows = rows_here - first_row
        outgoing = grad_acc[:, offset_row : offset_row + piece_rows]
        returned = from_behind(outgoing.astype(jnp.bfloat16), "seq", -distance).astype(
            outgoing.dtype
        )
        own_grads = own_grads.at[:, first_row:].add(returned)
        offset_row = offset_row + piece_rows
    _, pull_query = jax.vjp(lambda raw_vals: normalize(raw_vals, q_gain, query_scale), query_in)
    grad_q = pull_query(dquery)[0].astype(jnp.bfloat16).reshape(rows_here, 2 * heads_here * HD)
    _, pull_key = jax.vjp(lambda raw_vals: normalize(raw_vals, k_gain, 1.0), key_in)
    key_grad = pull_key(own_grads[0])[0].astype(jnp.bfloat16).reshape(rows_here, heads_here * HD)
    value_grad = own_grads[1].astype(jnp.bfloat16).reshape(rows_here, heads_here * HD)
    key_all, value_all = (
        lax.all_gather(key_grad, "uly", axis=1, tiled=True),
        lax.all_gather(value_grad, "uly", axis=1, tiled=True),
    )
    dims_last = (((1,), (1,)), ((), ()))
    total = lax.dot_general(key_all, weight_pair[0], dims_last, preferred_element_type=jnp.float32)
    total = total + lax.dot_general(
        value_all, weight_pair[1], dims_last, preferred_element_type=jnp.float32
    )
    grad_normed = total.astype(jnp.bfloat16)
    dims_first = (((0,), (0,)), ((), ()))
    key_part = lax.dot_general(normed, key_all, dims_first, preferred_element_type=jnp.float32)
    value_part = lax.dot_general(normed, value_all, dims_first, preferred_element_type=jnp.float32)
    grad_key_weight = lax.psum_scatter(
        key_part.astype(jnp.bfloat16), "seq", scatter_dimension=1, tiled=True
    ).astype(jnp.float32)
    grad_value_weight = lax.psum_scatter(
        value_part.astype(jnp.bfloat16), "seq", scatter_dimension=1, tiled=True
    ).astype(jnp.float32)
    return (attention, grad_normed, grad_q, grad_key_weight, grad_value_weight)


def solution(mesh):
    return jax.shard_map(
        body,
        mesh=mesh,
        in_specs=(
            P("seq", "uly"),
            P("seq", "uly"),
            P("uly", "seq"),
            P("uly", "seq"),
            P(),
            P(),
            P(),
            P("seq", "uly"),
        ),
        out_specs=(
            P("seq", "uly"),
            P("seq", "uly"),
            P("seq", "uly"),
            P("uly", "seq"),
            P("uly", "seq"),
        ),
        check_vma=False,
    )
```

profile of v0, /device:TPU:17, one launch (start us, length us, event | category | flops | bytes accessed | tf_op | source)
XLA Modules:
  0.0 460.0 jit_solution(5522709000838660446)
XLA Ops:
  8.7 60.0 %all-gather.3.cloned.1.call-done = bf16[2688,1024]{0,1:T(8,128)(2,1)} async-done(((bf16[2688,64]{0,1:T(8,128)(2,1)}), bf16[2688,1024]{0,1:T(8,128)(2,1)}) %all-gather.3.cloned.1.call-update) | async-done | bytes 5505040 | tf_op jit(solution)/shard_map/all_gather | solution.py:57
  68.7 5.0 %convolution_convert_fusion.3 = bf16[256,1024]{1,0:T(8,128)(2,1)} fusion(bf16[256,2688]{1,0:T(8,128)(2,1)S(1)} %copy-done, bf16[2688,1024]{0,1:T(8,128)(2,1)} %all-gather.3.cloned.1.call-done), kind=kOutput, calls=%fused_computation.31 | convolution fusion | flops 1409548288 | bytes 7405568 | tf_op jit(solution)/shard_map/dot_general | solution.py:60
  73.8 53.2 %all-gather.5.cloned.1.call-done = bf16[2688,1024]{0,1:T(8,128)(2,1)} async-done(((bf16[2688,64]{0,1:T(8,128)(2,1)}), bf16[2688,1024]{0,1:T(8,128)(2,1)}) %all-gather.5.cloned.1.call-update) | async-done | bytes 5505040 | tf_op jit(solution)/shard_map/all_gather | solution.py:58
  127.0 5.0 %convolution_convert_fusion.2 = bf16[256,1024]{1,0:T(8,128)(2,1)} fusion(bf16[256,2688]{1,0:T(8,128)(2,1)S(1)} %copy-done, bf16[2688,1024]{0,1:T(8,128)(2,1)} %all-gather.5.cloned.1.call-done), kind=kOutput, calls=%fused_computation.30 | convolution fusion | flops 1409548288 | bytes 7405568 | tf_op jit(solution)/shard_map/dot_general | solution.py:61
  132.3 10.8 %reduce-scatter.5.cloned.1.call-done = bf16[256,512]{1,0:T(8,128)(2,1)} async-done(((bf16[256,1024]{1,0:T(8,128)(2,1)}), bf16[256,512]{1,0:T(8,128)(2,1)}) %reduce-scatter.5.cloned.1.call-update) | async-done | bytes 262160 | tf_op jit(solution)/shard_map/reduce_scatter | solution.py:63
  144.7 15.7 %reduce-scatter.7.cloned.1.call-done = bf16[256,512]{1,0:T(8,128)(2,1)} async-done(((bf16[256,1024]{1,0:T(8,128)(2,1)}), bf16[256,512]{1,0:T(8,128)(2,1)}) %reduce-scatter.7.cloned.1.call-update) | async-done | bytes 262160 | tf_op jit(solution)/shard_map/reduce_scatter | solution.py:66
  175.8 3.3 collective-permute-start.3
  180.3 11.7 %collective-permute-done.1 = bf16[2,256,4,128]{3,1,2,0:T(8,128)(2,1)} collective-permute-done((bf16[2,256,4,128]{3,1,2,0:T(8,128)(2,1)}, bf16[2,256,4,128]{3,1,2,0:T(8,128)(2,1)}, u32[]{:S(2)}, u32[]{:S(2)}) %collective-permute-start.1) | collective-permute-done | bytes 524320 | tf_op jit(solution)/shard_map/ppermute | solution.py:17
  193.0 8.0 %collective-permute-done.2 = bf16[2,256,4,128]{3,1,2,0:T(8,128)(2,1)} collective-permute-done((bf16[2,256,4,128]{3,1,2,0:T(8,128)(2,1)}, bf16[2,256,4,128]{3,1,2,0:T(8,128)(2,1)}, u32[]{:S(2)}, u32[]{:S(2)}) %collective-permute-start.2) | collective-permute-done | bytes 524320 | tf_op jit(solution)/shard_map/ppermute | solution.py:17
  204.7 5.8 %fusion = (f32[4,2,256]{2,1,0:T(2,128)S(1)}, f32[4,1280,256,2]{2,1,3,0:T(8,128)}) fusion(f32[4,2,256]{2,1,0:T(2,128)S(1)} %get-tuple-element.139, f32[4,1280,256,2]{2,1,3,0:T(8,128)S(1)} %get-tuple-element.140, pred[256,1280]{0,1:T(8,128)(4,1)S(1)} %copy-done.8, bf16[256,4,2,128]{0,3,2,1:T(8,128)(2,1)S(1)} %bitcast.128, ...), kind=kOutput, calls=%fused_computation.2 | convolution fusion | flops 681572352 | bytes 23150592 | tf_op jit(solution)/shard_map/while/body/eval_jaxpr/bhge,lhe->hgbl/dot_general | solution.py:40
  213.2 7.0 %fusion.2 = bf16[4,2,256,1280]{2,3,1,0:T(8,128)(2,1)S(1)} fusion(f32[4,1280,256,2]{2,1,3,0:T(8,128)} %get-tuple-element.142, f32[4,2,256]{2,1,0:T(2,128)S(1)} %get-tuple-element.141, f32[4,2,256]{2,1,0:T(2,128)S(1)} %get-tuple-element.139, f32[4,1280,256,2]{2,1,3,0:T(8,128)S(1)} %get-tuple-element.140, pred[256,1280]{0,1:T(8,128)(4,1)S(1)} %copy-done.8), kind=kLoop, calls=%fused_computation.4 | loop fusion | flops 13107200 | bytes 26558464 | tf_op jit(solution)/shard_map/while/body/eval_jaxpr/convert_element_type | solution.py:44
  227.6 4.0 collective-permute-start.5
  231.6 6.8 %collective-permute-start.6 = (bf16[2,256,4,128]{1,3,2,0:T(8,128)(2,1)}, bf16[2,256,4,128]{1,3,2,0:T(8,128)(2,1)}, u32[]{:S(2)}, u32[]{:S(2)}) collective-permute-start(bf16[2,256,4,128]{1,3,2,0:T(8,128)(2,1)} %get-tuple-element.137), channel_id=1, source_target_pairs={{4,0},{6,2},{8,4},{10,6},{12,8},{14,10},{16,12},{18,14},{20,16},{2... | collective-permute-start | bytes 1572872 | tf_op jit(solution)/shard_map/ppermute | solution.py:17
  242.2 15.9 %collective-permute-done.5 = bf16[2,256,4,128]{1,3,2,0:T(8,128)(2,1)} collective-permute-done((bf16[2,256,4,128]{1,3,2,0:T(8,128)(2,1)}, bf16[2,256,4,128]{1,3,2,0:T(8,128)(2,1)}, u32[]{:S(2)}, u32[]{:S(2)}) %collective-permute-start.5) | collective-permute-done | bytes 524320 | tf_op jit(solution)/shard_map/ppermute | solution.py:17
  271.6 6.1 %all_gather.14 = bf16[256,1024]{1,0:T(8,128)(2,1)S(1)} all-gather(bf16[256,512]{1,0:T(8,128)(2,1)S(1)} %fusion.24), channel_id=1, replica_groups=mesh['seq'=16,'uly'=2] {'uly'}, dimensions={1}, use_global_device_ids=true | all-gather | bytes 786432 | tf_op jit(solution)/shard_map/all_gather | solution.py:138
  278.5 4.1 fusion.6
  282.7 5.9 %all_gather.15 = bf16[256,1024]{0,1:T(8,128)(2,1)S(1)} all-gather(bf16[256,512]{0,1:T(8,128)(2,1)S(1)} %bitcast.127), channel_id=1, replica_groups=mesh['seq'=16,'uly'=2] {'uly'}, dimensions={1}, use_global_device_ids=true | all-gather | bytes 786432 | tf_op jit(solution)/shard_map/all_gather | solution.py:139
  288.6 4.0 fusion.7
  292.6 3.9 multiply_reduce_fusion
  297.8 7.4 %fusion.13 = bf16[4,128,2,256]{3,1,2,0:T(8,128)(2,1)S(1)} fusion(bf16[2,1280,4,128]{3,1,2,0:T(8,128)(2,1)} %copy-done.9, f32[4,1280,256,2]{2,1,3,0:T(8,128)} %copy-done.3, f32[4,2,256]{2,1,0:T(2,128)S(1)} %get-tuple-element.139, pred[256,1280]{0,1:T(8,128)(4,1)} %compare_and_fusion), kind=kOutput, calls=%fused_computation.29 | convolution fusion | flops 679215104 | bytes 12656640 | tf_op jit(solution)/shard_map/while/body/eval_jaxpr/hgbl,lhe->bhge/dot_general | solution.py:37
  306.1 4.6 fusion.36
  310.7 5.5 %fusion.8 = bf16[256,2688]{1,0:T(8,128)(2,1)} fusion(f32[256,2688]{1,0:T(8,128)S(1)} %fusion.36, bf16[256,1024]{0,1:T(8,128)(2,1)S(1)} %all_gather.15, bf16[2688,1024]{0,1:T(8,128)(2,1)} %all-gather.5.cloned.1.call-done), kind=kOutput, calls=%fused_computation.17 | convolution fusion | flops 1410662400 | bytes 10158080 | tf_op jit(solution)/shard_map/dot_general | solution.py:143
  316.2 51.7 %reduce-scatter.9.cloned.1.call-done = bf16[2688,64]{0,1:T(8,128)(2,1)} async-done(((bf16[2688,1024]{0,1:T(8,128)(2,1)}), bf16[2688,64]{0,1:T(8,128)(2,1)}) %reduce-scatter.9.cloned.1.call-update) | async-done | bytes 344080 | tf_op jit(solution)/shard_map/reduce_scatter | solution.py:150
  369.8 81.5 %reduce-scatter.11.cloned.1.call-done = bf16[2688,64]{0,1:T(8,128)(2,1)} async-done(((bf16[2688,1024]{0,1:T(8,128)(2,1)}), bf16[2688,64]{0,1:T(8,128)(2,1)}) %reduce-scatter.11.cloned.1.call-update) | async-done | bytes 344080 | tf_op jit(solution)/shard_map/reduce_scatter | solution.py:153
  (99 shorter events, 58.5 us)
Async XLA Ops:
  7.2 61.6 %copy-start = (bf16[256,2688]{1,0:T(8,128)(2,1)S(1)}, bf16[256,2688]{1,0:T(8,128)(2,1)}, u32[]{:S(2)}) copy-start(bf16[256,2688]{1,0:T(8,128)(2,1)} %param.24) | copy-start | bytes 4128772
  7.2 61.5 %all-gather.3.cloned.1.call-start = ((), (), s32[]{:S(2)}) async-start(), calls=%async_computation.4 | async-start | bytes 5849088 | tf_op jit(solution)/shard_map/all_gather | solution.py:57
  7.9 119.1 %all-gather.5.cloned.1.call-start = ((), (), s32[]{:S(2)}) async-start(), calls=%async_computation.6 | async-start | bytes 5849088 | tf_op jit(solution)/shard_map/all_gather | solution.py:58
  8.7 134.4 %reduce-scatter.5.cloned.1.call-start = ((), (), s32[]{:S(2)}) async-start(), calls=%async_computation.5 | async-start | bytes 786432 | tf_op jit(solution)/shard_map/reduce_scatter | solution.py:63
  73.8 58.4 %copy-start.12 = (s32[4096]{0:T(1024)S(1)}, s32[4096]{0:T(1024)}, u32[]{:S(2)}) copy-start(s32[4096]{0:T(1024)} %param.30) | copy-start | bytes 49156
  73.8 86.6 %reduce-scatter.7.cloned.1.call-start = ((), (), s32[]{:S(2)}) async-start(), calls=%async_computation.7 | async-start | bytes 786432 | tf_op jit(solution)/shard_map/reduce_scatter | solution.py:66
  132.1 29.6 %copy-start.13 = (f32[128]{0:T(128)S(1)}, f32[128]{0:T(128)}, u32[]{:S(2)}) copy-start(f32[128]{0:T(128)} %param.29) | copy-start | bytes 1540
  132.1 235.8 %reduce-scatter.9.cloned.1.call-start = ((), (), s32[]{:S(2)}) async-start(), calls=%async_computation.8 | async-start | bytes 5849088 | tf_op jit(solution)/shard_map/reduce_scatter | solution.py:150
  143.1 18.4 %copy-start.7 = (bf16[256,512]{1,0:T(8,128)(2,1)S(1)}, bf16[256,512]{1,0:T(8,128)(2,1)}, u32[]{:S(2)}) copy-start(bf16[256,512]{1,0:T(8,128)(2,1)} %reduce-scatter.5.cloned.1.call-done) | copy-start | bytes 786436
  162.8 16.4 %collective-permute-start = (bf16[2,256,4,128]{3,1,2,0:T(8,128)(2,1)}, bf16[2,256,4,128]{3,1,2,0:T(8,128)(2,1)}, u32[]{:S(2)}, u32[]{:S(2)}) collective-permute-start(bf16[2,256,4,128]{3,1,2,0:T(8,128)(2,1)} %pad_maximum_fusion.1), channel_id=1, source_target_pairs={{0,8},{2,10},{4,12},{6,14},{8,16},{10,18},{12,20},{14,22},{16,24},... | collective-permute-start | bytes 1572872 | tf_op jit(solution)/shard_map/ppermute | solution.py:17
  165.9 26.1 %collective-permute-start.1 = (bf16[2,256,4,128]{3,1,2,0:T(8,128)(2,1)}, bf16[2,256,4,128]{3,1,2,0:T(8,128)(2,1)}, u32[]{:S(2)}, u32[]{:S(2)}) collective-permute-start(bf16[2,256,4,128]{3,1,2,0:T(8,128)(2,1)} %pad_maximum_fusion.1), channel_id=1, source_target_pairs={{0,6},{2,8},{4,10},{6,12},{8,14},{10,16},{12,18},{14,20},{16,22},{... | collective-permute-start | bytes 1572872 | tf_op jit(solution)/shard_map/ppermute | solution.py:17
  170.5 30.5 %collective-permute-start.2 = (bf16[2,256,4,128]{3,1,2,0:T(8,128)(2,1)}, bf16[2,256,4,128]{3,1,2,0:T(8,128)(2,1)}, u32[]{:S(2)}, u32[]{:S(2)}) collective-permute-start(bf16[2,256,4,128]{3,1,2,0:T(8,128)(2,1)} %pad_maximum_fusion.1), channel_id=1, source_target_pairs={{0,4},{2,6},{4,8},{6,10},{8,12},{10,14},{12,16},{14,18},{16,20},{1... | collective-permute-start | bytes 1572872 | tf_op jit(solution)/shard_map/ppermute | solution.py:17
  175.8 26.6 %copy-start.8 = (pred[256,1280]{0,1:T(8,128)(4,1)S(1)}, pred[256,1280]{0,1:T(8,128)(4,1)}, u32[]{:S(2)}) copy-start(pred[256,1280]{0,1:T(8,128)(4,1)} %compare_and_fusion) | copy-start | bytes 983044
  175.8 26.6 %copy-start.14 = (f32[128]{0:T(128)S(1)}, f32[128]{0:T(128)}, u32[]{:S(2)}) copy-start(f32[128]{0:T(128)} %param.28) | copy-start | bytes 1540
  175.8 26.4 %collective-permute-start.3 = (bf16[2,256,4,128]{3,1,2,0:T(8,128)(2,1)}, bf16[2,256,4,128]{3,1,2,0:T(8,128)(2,1)S(1)}, u32[]{:S(2)}, u32[]{:S(2)}) collective-permute-start(bf16[2,256,4,128]{3,1,2,0:T(8,128)(2,1)} %pad_maximum_fusion.1), channel_id=1, source_target_pairs={{0,2},{2,4},{4,6},{6,8},{8,10},{10,12},{12,14},{14,16},{16,18},{18... | collective-permute-start | bytes 1572872 | tf_op jit(solution)/shard_map/ppermute | solution.py:17
  204.6 8.5 %copy-start.3 = (f32[4,1280,256,2]{2,1,3,0:T(8,128)}, f32[4,1280,256,2]{2,1,3,0:T(8,128)S(1)}, u32[]{:S(2)}) copy-start(f32[4,1280,256,2]{2,1,3,0:T(8,128)S(1)} %get-tuple-element.140) | copy-start | bytes 31457284
  213.1 8.9 %copy-start.4 = (f32[1,1280,4,128]{1,3,2,0:T(8,128)}, f32[1,1280,4,128]{1,3,2,0:T(8,128)S(1)}, u32[]{:S(2)}) copy-start(f32[1,1280,4,128]{1,3,2,0:T(8,128)S(1)} %convolution_bitcast_fusion) | copy-start | bytes 7864324
  225.4 16.8 %collective-permute-start.4 = (bf16[2,256,4,128]{1,3,2,0:T(8,128)(2,1)}, bf16[2,256,4,128]{1,3,2,0:T(8,128)(2,1)S(1)}, u32[]{:S(2)}, u32[]{:S(2)}) collective-permute-start(bf16[2,256,4,128]{1,3,2,0:T(8,128)(2,1)} %get-tuple-element.135), channel_id=1, source_target_pairs={{8,0},{10,2},{12,4},{14,6},{16,8},{18,10},{20,12},{22,14},{24,16},... | collective-permute-start | bytes 1572872 | tf_op jit(solution)/shard_map/ppermute | solution.py:17
  227.6 30.5 %collective-permute-start.5 = (bf16[2,256,4,128]{1,3,2,0:T(8,128)(2,1)}, bf16[2,256,4,128]{1,3,2,0:T(8,128)(2,1)}, u32[]{:S(2)}, u32[]{:S(2)}) collective-permute-start(bf16[2,256,4,128]{1,3,2,0:T(8,128)(2,1)} %get-tuple-element.138), channel_id=1, source_target_pairs={{6,0},{8,2},{10,4},{12,6},{14,8},{16,10},{18,12},{20,14},{22,16},{... | collective-permute-start | bytes 1572872 | tf_op jit(solution)/shard_map/ppermute | solution.py:17
  231.6 26.6 %collective-permute-start.6 = (bf16[2,256,4,128]{1,3,2,0:T(8,128)(2,1)}, bf16[2,256,4,128]{1,3,2,0:T(8,128)(2,1)}, u32[]{:S(2)}, u32[]{:S(2)}) collective-permute-start(bf16[2,256,4,128]{1,3,2,0:T(8,128)(2,1)} %get-tuple-element.137), channel_id=1, source_target_pairs={{4,0},{6,2},{8,4},{10,6},{12,8},{14,10},{16,12},{18,14},{20,16},{2... | collective-permute-start | bytes 1572872 | tf_op jit(solution)/shard_map/ppermute | solution.py:17
  238.4 22.3 %collective-permute-start.7 = (bf16[2,256,4,128]{1,3,2,0:T(8,128)(2,1)}, bf16[2,256,4,128]{1,3,2,0:T(8,128)(2,1)}, u32[]{:S(2)}, u32[]{:S(2)}) collective-permute-start(bf16[2,256,4,128]{1,3,2,0:T(8,128)(2,1)} %get-tuple-element.136), channel_id=1, source_target_pairs={{2,0},{4,2},{6,4},{8,6},{10,8},{12,10},{14,12},{16,14},{18,16},{20... | collective-permute-start | bytes 1572872 | tf_op jit(solution)/shard_map/ppermute | solution.py:17
  242.2 16.0 %copy-start.10 = (bf16[2,256,4,128]{1,3,2,0:T(8,128)(2,1)}, bf16[2,256,4,128]{1,3,2,0:T(8,128)(2,1)S(1)}, u32[]{:S(2)}) copy-start(bf16[2,256,4,128]{1,3,2,0:T(8,128)(2,1)S(1)} %collective-permute-done.4) | copy-start | bytes 1572868
  282.6 168.7 %reduce-scatter.11.cloned.1.call-start = ((), (), s32[]{:S(2)}) async-start(), calls=%async_computation.9 | async-start | bytes 5849088 | tf_op jit(solution)/shard_map/reduce_scatter | solution.py:153
  297.8 8.4 %copy-start.6 = (bf16[256,1024]{1,0:T(8,128)(2,1)S(1)}, bf16[256,1024]{1,0:T(8,128)(2,1)}, u32[]{:S(2)}) copy-start(bf16[256,1024]{1,0:T(8,128)(2,1)} %copy-done.5) | copy-start | bytes 1572868
  (5 other events, 9.2 us)
Sparse Core Ops, SparseCore 0:
  10.3 58.3 all-gather.2
  71.0 55.9 all-gather.4
  129.9 13.2 reduce-scatter.4
  145.9 14.5 reduce-scatter.6
  282.7 85.1 reduce-scatter.8
  372.1 79.1 reduce-scatter.10
where the time goes:
time: 465 us; the launch traced here: 460 us
  waiting for transfers between devices  313 us (67%)
  matrix products  52 us (11%)
  starting transfers between devices  26.6 us (6%)
  local copies, waits for them, and re-layouts  22.9 us (5%)
  other arithmetic  19.3 us (4%)
  between operations  14.5 us (3%)
  blocking collectives  12 us (3%)
    reduce_scatter x1, waiting for transfers between devices, body(): lax.psum_scatter(value_part.astype(jnp.bfloat16), 'seq', scatter_dimensio...  81.5 us
    all_gather x1, waiting for transfers between devices, body(): lax.all_gather(key_weight, 'seq', axis=1, tiled=True)  60 us
    all_gather x1, waiting for transfers between devices, body(): lax.all_gather(value_weight, 'seq', axis=1, tiled=True)  53.2 us
    reduce_scatter x1, waiting for transfers between devices, body(): lax.psum_scatter(key_part.astype(jnp.bfloat16), 'seq', scatter_dimension=...  51.7 us
    ppermute x8, waiting for transfers between devices, from_behind(): return lax.ppermute(array, axis, pairs)  38.3 us
    ppermute x8, starting transfers between devices, from_behind(): return lax.ppermute(array, axis, pairs)  26.4 us
    reduce_scatter x1, waiting for transfers between devices, body(): lax.psum_scatter(value_term.astype(jnp.bfloat16), 'uly', scatter_dimensio...  15.7 us
    reduce_scatter x1, waiting for transfers between devices, body(): lax.psum_scatter(key_term.astype(jnp.bfloat16), 'uly', scatter_dimension=...  10.8 us
  transfers between devices with their start and end apart: 14, of which 11 were waited for; matrix products, arithmetic and copies ran while one was open for 11% of the time, Pallas kernels for 0%

commit v1 on v0

--- a/solution.py
+++ b/solution.py
@@ -1,6 +1,10 @@
+import functools
+
 import jax
 import jax.numpy as jnp
 from jax import lax
+from jax.experimental import pallas as pl
+from jax.experimental.pallas import tpu as pltpu
 from jax.sharding import PartitionSpec as P
 
 HD = 128
@@ -48,7 +52,7 @@
     return (attended, dquery, dkey, dvalue)
 
 
-def body(normed, q_raw, key_weight, value_weight, q_gain, k_gain, segment_ids, grad_out):
+def body_general(normed, q_raw, key_weight, value_weight, q_gain, k_gain, segment_ids, grad_out):
     rows_here = normed.shape[0]
     heads_here = q_raw.shape[1] // (2 * HD)
     seq_index = lax.axis_index("seq")
@@ -156,6 +160,569 @@
     return (attention, grad_normed, grad_q, grad_key_weight, grad_value_weight)
 
 
+MIB = 1 << 20
+MASKED = 16384.0
+NT = (((1,), (1,)), ((), ()))
+ANY = pl.BlockSpec(memory_space=pl.ANY)
+SMEM = pl.BlockSpec(memory_space=pltpu.SMEM)
+VMEM = pl.BlockSpec(memory_space=pltpu.VMEM)
+
+
+def at(z, x, c):
+    return (z * 2 + x) * 2 + c
+
+
+def move(array, rule):
+    return lax.ppermute(array, "seq", [(at(*a), at(*b)) for a, b in rule])
+
+
+def along_z(array, hops):
+    return move(array, [((z, x, c), (to, x, c)) for z, c, to in hops for x in (0, 1)])
+
+
+def swap_core(array):
+    return move(
+        array, [((z, x, c), (z, x, 1 - c)) for z in range(4) for x in (0, 1) for c in (0, 1)]
+    )
+
+
+def swap_x(array):
+    return move(
+        array, [((z, x, c), (z, 1 - x, c)) for z in range(4) for x in (0, 1) for c in (0, 1)]
+    )
+
+
+def swap_uly(array):
+    return lax.ppermute(array, "uly", [(0, 1), (1, 0)])
+
+
+def call(kernel, out_shape, vmem, flops, bytes_accessed, **rest):
+    return pl.pallas_call(
+        kernel,
+        out_shape=out_shape,
+        compiler_params=pltpu.CompilerParams(vmem_limit_bytes=vmem * MIB),
+        cost_estimate=pl.CostEstimate(
+            flops=flops, bytes_accessed=bytes_accessed, transcendentals=0
+        ),
+        **rest,
+    )
+
+
+def shaped(shape, dtype=jnp.bfloat16):
+    return jax.ShapeDtypeStruct(shape, dtype)
+
+
+def transpose_in_kernel(key_ref, value_ref, out_ref):
+    both = jnp.concatenate([key_ref[...], value_ref[...]], axis=1).astype(jnp.float32)
+    out_ref[...] = both.T.astype(jnp.bfloat16)
+
+
+def transpose_out_kernel(key_ref, value_ref, key_out, value_out):
+    width = key_ref.shape[0]
+    both = jnp.concatenate([key_ref[...], value_ref[...]], axis=0).T
+    key_out[...] = both[:, :width]
+    value_out[...] = both[:, width:]
+
+
+def line_gather(own):
+    r1 = along_z(own, [(0, 0, 1), (1, 1, 2), (2, 0, 3)])
+    l1 = along_z(own, [(1, 1, 0), (2, 0, 1), (3, 1, 2)])
+    r2 = along_z(r1, [(1, 0, 2), (2, 1, 3)])
+    l2 = along_z(l1, [(2, 1, 1), (1, 0, 0)])
+    r3 = along_z(r2, [(2, 0, 3)])
+    l3 = along_z(l2, [(1, 1, 0)])
+    return (own, r1, r2, r3, l1, l2, l3)
+
+
+def line_reduce(far, mid, z):
+    f1 = along_z(far, [(3, 0, 2), (0, 1, 1)])
+    m1 = along_z(mid, [(3, 1, 2), (0, 0, 1)])
+    f2 = along_z(far + f1, [(2, 0, 1), (1, 1, 2)])
+    near = along_z(mid, [(0, 1, 1), (3, 0, 2)])
+    m2 = along_z(mid + m1, [(2, 1, 1), (1, 0, 2)])
+    f3 = along_z(far + f2, [(1, 0, 0), (2, 1, 3)])
+    own = jnp.where((z == 0) | (z == 3), far, mid).astype(jnp.float32)
+    return own + f3.astype(jnp.float32) + m2.astype(jnp.float32) + near.astype(jnp.float32)
+
+
+def slot_copies(code, slot_at, refs, buffer, sems, act):
+    for k, ref in enumerate(refs):
+
+        @pl.when(slot_at == k)
+        def _():
+            copy = pltpu.make_async_copy(ref, buffer, sems)
+            copy.start() if act else copy.wait()
+
+
+def project_kernel(code, *refs):
+    acts, weights = refs[:4], refs[4:11]
+    mine, theirs, acts_v, w_v, acts_sem, w_sem = refs[11:]
+    width = mine.shape[1]
+    rows = acts[0].shape[0]
+    place = code[0]
+
+    def weight_copies(act):
+        for slot in range(2):
+            slot_copies(
+                code, code[1 + slot], weights, w_v.at[pl.ds(slot * width, width)], w_sem.at[slot], act
+            )
+
+    weight_copies(True)
+    copies = [
+        pltpu.make_async_copy(acts[j], acts_v.at[j], acts_sem.at[j]) for j in range(4)
+    ]
+    for copy in copies:
+        copy.start()
+    weight_copies(False)
+    for j in range(4):
+        copies[j].wait()
+        both = lax.dot_general(acts_v[j], w_v[...], NT, preferred_element_type=jnp.float32)
+        begin = pl.multiple_of((place ^ j) * rows, rows)
+        mine[pl.ds(begin, rows), :] = both[:, :width].astype(jnp.bfloat16)
+        theirs[pl.ds(begin, rows), :] = both[:, width:].astype(jnp.bfloat16)
+
+
+def project(code, acts, weights):
+    rows, features = acts[0].shape
+    width = weights[0].shape[0]
+    return call(
+        project_kernel,
+        [shaped((4 * rows, width)), shaped((4 * rows, width))],
+        24,
+        2 * 4 * rows * features * 2 * width,
+        4 * rows * features * 2 + 2 * width * features * 2,
+        in_specs=[SMEM] + [ANY] * 11,
+        out_specs=[VMEM, VMEM],
+        scratch_shapes=[
+            pltpu.VMEM((4, rows, features), jnp.bfloat16),
+            pltpu.VMEM((2 * width, features), jnp.bfloat16),
+            pltpu.SemaphoreType.DMA((4,)),
+            pltpu.SemaphoreType.DMA((2,)),
+        ],
+        name="project",
+    )(code, *acts, *weights)
+
+
+def normalized(raw, gain, factor):
+    inverse = lax.rsqrt(jnp.mean(raw * raw, axis=-1, keepdims=True) + epsilon)
+    return raw * inverse * gain * factor
+
+
+def normalized_pull(raw, gain, factor, cotangent):
+    inverse = lax.rsqrt(jnp.mean(raw * raw, axis=-1, keepdims=True) + epsilon)
+    scaled = cotangent * gain * factor
+    along = jnp.mean(scaled * raw, axis=-1, keepdims=True)
+    return inverse * (scaled - raw * (inverse * inverse * along))
+
+
+def dot(a, b):
+    return jnp.dot(a, b, preferred_element_type=jnp.float32)
+
+
+def scores_kernel(
+    code, q_ref, go_ref, own_ref, before_ref, key_mark, query_mark, gain_ref,
+    e_ref, stat_ref, dv_own, dv_before, keys_v, acc
+):
+    block = pl.program_id(0)
+    rows = q_ref.shape[1]
+    chunks = e_ref.shape[2] // rows
+    half = own_ref.shape[0]
+
+    @pl.when(block == 0)
+    def _():
+        keys_v[:half, :HD] = before_ref[...]
+        keys_v[half:, :HD] = own_ref[...]
+        keys_v[:, HD:] = key_mark[...]
+        acc[...] = jnp.zeros_like(acc)
+
+    key_at = lax.broadcasted_iota(jnp.int32, (rows, rows), 0)
+    query_at = lax.broadcasted_iota(jnp.int32, (rows, rows), 1)
+    behind = key_at <= query_at
+    stats = []
+    for g in range(2):
+        lanes = slice(g * HD, (g + 1) * HD)
+        query = normalized(q_ref[0, :, lanes].astype(jnp.float32), gain_ref[...], query_scale)
+        query_t = jnp.concatenate([query.T.astype(jnp.bfloat16), query_mark[...]], axis=0)
+        total = jnp.zeros((1, rows), jnp.float32)
+        for c in range(chunks):
+            begin = pl.multiple_of((block + c) * rows, rows)
+            e = jnp.exp(dot(keys_v[pl.ds(begin, rows), :], query_t))
+            if c == 0:
+                e = jnp.where(behind, 0.0, e)
+            if c == chunks - 1:
+                e = jnp.where(behind, e, 0.0)
+            total = total + jnp.sum(e, axis=0, keepdims=True)
+            e_ref[0, g, c * rows : (c + 1) * rows, :] = e.astype(jnp.bfloat16)
+        inverse = 1.0 / total
+        stats.append(inverse)
+        grad = (go_ref[0, :, lanes].astype(jnp.float32).T * inverse).T.astype(jnp.bfloat16)
+        span = pl.ds(pl.multiple_of(block * rows, rows), chunks * rows)
+        acc[span, :] = acc[span, :] + dot(e_ref[0, g], grad)
+    stat_ref[0] = jnp.concatenate(stats + [jnp.zeros((6, rows), jnp.float32)], axis=0)
+
+    @pl.when(block == pl.num_programs(0) - 1)
+    def _():
+        dv_before[...] = acc[:half, :].astype(jnp.bfloat16)
+        dv_own[...] = acc[half:, :]
+
+
+def whole(shape):
+    return pl.BlockSpec(shape, lambda b, code: (0,) * len(shape))
+
+
+def attend_scores(code, q, go, keys, keys_before, key_mark, query_mark, gain):
+    blocks, rows, _ = q.shape
+    half = blocks * rows
+    span = half + rows
+    picked = pl.BlockSpec((1, rows, 2 * HD), lambda b, code: (b ^ code[0], 0, 0))
+    return call(
+        scores_kernel,
+        [
+            shaped((blocks, 2, span, rows)),
+            shaped((blocks, 8, rows), jnp.float32),
+            shaped((half, HD), jnp.float32),
+            shaped((half, HD)),
+        ],
+        40,
+        2 * 2 * half * span * 3 * HD,
+        2 * half * span * 2 + 8 * half * HD * 2,
+        grid_spec=pltpu.PrefetchScalarGridSpec(
+            num_scalar_prefetch=1,
+            grid=(blocks,),
+            in_specs=[
+                picked,
+                picked,
+                whole((half, HD)),
+                whole((half, HD)),
+                whole((2 * half, HD)),
+                pl.BlockSpec((HD, rows), lambda b, code: (0, b)),
+                whole((1, HD)),
+            ],
+            out_specs=[
+                pl.BlockSpec((1, 2, span, rows), lambda b, code: (b, 0, 0, 0)),
+                pl.BlockSpec((1, 8, rows), lambda b, code: (b, 0, 0)),
+                whole((half, HD)),
+                whole((half, HD)),
+            ],
+            scratch_shapes=[
+                pltpu.VMEM((2 * half, 2 * HD), jnp.bfloat16),
+                pltpu.VMEM((2 * half, HD), jnp.float32),
+            ],
+        ),
+        name="attend_scores",
+    )(code, q, go, keys, keys_before, key_mark, query_mark, gain)
+
+
+def values_kernel(
+    code, q_ref, go_ref, own_ref, before_ref, v_own, v_before, gain_ref, e_ref, stat_ref,
+    out_ref, gq_ref, dk_own, dk_before, values_v, values_t, keys_t, acc
+):
+    block = pl.program_id(0)
+    rows = q_ref.shape[1]
+    span_rows = e_ref.shape[2]
+    half = own_ref.shape[0]
+
+    @pl.when(block == 0)
+    def _():
+        values_v[:half, :] = v_before[...]
+        values_v[half:, :] = v_own[...]
+        values_t[...] = values_v[...].astype(jnp.float32).T.astype(jnp.bfloat16)
+        keys_t[:, :half] = before_ref[...].astype(jnp.float32).T.astype(jnp.bfloat16)
+        keys_t[:, half:] = own_ref[...].astype(jnp.float32).T.astype(jnp.bfloat16)
+        acc[...] = jnp.zeros_like(acc)
+
+    span = pl.ds(pl.multiple_of(block * rows, rows), span_rows)
+    for g in range(2):
+        lanes = slice(g * HD, (g + 1) * HD)
+        raw = q_ref[0, :, lanes].astype(jnp.float32)
+        query = normalized(raw, gain_ref[...], query_scale).astype(jnp.bfloat16)
+        inverse = stat_ref[0, g : g + 1, :]
+        e = e_ref[0, g]
+        out_t = dot(values_t[:, span], e) * inverse
+        out_ref[0, :, lanes] = out_t.T.astype(jnp.bfloat16)
+        grad_t = go_ref[0, :, lanes].astype(jnp.float32).T
+        along = jnp.sum(out_t * grad_t, axis=0, keepdims=True) * inverse
+        dprob = dot(values_v[span, :], (grad_t * inverse).astype(jnp.bfloat16))
+        dscore = (e.astype(jnp.float32) * (dprob - along)).astype(jnp.bfloat16)
+        acc[span, :] = acc[span, :] + dot(dscore, query)
+        dquery = dot(keys_t[:, span], dscore).T
+        gq_ref[0, :, lanes] = normalized_pull(raw, gain_ref[...], query_scale, dquery).astype(
+            jnp.bfloat16
+        )
+
+    @pl.when(block == pl.num_programs(0) - 1)
+    def _():
+        dk_before[...] = acc[:half, :].astype(jnp.bfloat16)
+        dk_own[...] = acc[half:, :]
+
+
+def attend_values(code, q, go, keys, keys_before, values, values_before, gain, e, stat):
+    blocks, rows, _ = q.shape
+    half = blocks * rows
+    span = half + rows
+    picked = pl.BlockSpec((1, rows, 2 * HD), lambda b, code: (b ^ code[0], 0, 0))
+    return call(
+        values_kernel,
+        [
+            shaped(q.shape),
+            shaped(q.shape),
+            shaped((half, HD), jnp.float32),
+            shaped((half, HD)),
+        ],
+        40,
+        2 * 2 * half * span * 4 * HD,
+        2 * half * span * 2 + 8 * half * HD * 2,
+        grid_spec=pltpu.PrefetchScalarGridSpec(
+            num_scalar_prefetch=1,
+            grid=(blocks,),
+            in_specs=[picked, picked]
+            + [whole((half, HD))] * 4
+            + [
+                whole((1, HD)),
+                pl.BlockSpec((1, 2, span, rows), lambda b, code: (b, 0, 0, 0)),
+                pl.BlockSpec((1, 8, rows), lambda b, code: (b, 0, 0)),
+            ],
+            out_specs=[picked, picked, whole((half, HD)), whole((half, HD))],
+            scratch_shapes=[
+                pltpu.VMEM((2 * half, HD), jnp.bfloat16),
+                pltpu.VMEM((HD, 2 * half), jnp.bfloat16),
+                pltpu.VMEM((HD, 2 * half), jnp.bfloat16),
+                pltpu.VMEM((2 * half, HD), jnp.float32),
+            ],
+        ),
+        name="attend_values",
+    )(code, q, go, keys, keys_before, values, values_before, gain, e, stat)
+
+
+def weight_grad_kernel(code, mine, theirs, a0, a1, a2, a3, far, mid, acts_v, grad_v, acts_sem):
+    acts = (a0, a1, a2, a3)
+    rows, features = a0.shape
+    width = far.shape[0]
+    copies = [
+        pltpu.make_async_copy(acts[j], acts_v.at[j], acts_sem.at[j]) for j in range(4)
+    ]
+    for copy in copies:
+        copy.start()
+    first = code[3] == 1
+    for j in range(4):
+        span = pl.ds(pl.multiple_of((code[0] ^ j) * rows, rows), rows)
+        own = mine[span, :].astype(jnp.float32).T
+        other = theirs[span, :].astype(jnp.float32).T
+        grad_v[j, :width, :] = jnp.where(first, own, other).astype(jnp.bfloat16)
+        grad_v[j, width:, :] = jnp.where(first, other, own).astype(jnp.bfloat16)
+    for copy in copies:
+        copy.wait()
+    tile = features // 3
+    for n in range(3):
+        lanes = slice(n * tile, (n + 1) * tile)
+        both = dot(grad_v[0], acts_v[0, :, lanes])
+        for j in range(1, 4):
+            both = both + dot(grad_v[j], acts_v[j, :, lanes])
+        far[:, lanes] = both[:width].astype(jnp.bfloat16)
+        mid[:, lanes] = both[width:].astype(jnp.bfloat16)
+
+
+def weight_grad(code, mine, theirs, acts):
+    rows, features = acts[0].shape
+    width = mine.shape[1]
+    return call(
+        weight_grad_kernel,
+        [shaped((width, features)), shaped((width, features))],
+        32,
+        2 * 4 * rows * features * 2 * width,
+        4 * rows * features * 2 + 2 * width * features * 2,
+        in_specs=[SMEM, VMEM, VMEM] + [ANY] * 4,
+        out_specs=[VMEM, VMEM],
+        scratch_shapes=[
+            pltpu.VMEM((4, rows, features), jnp.bfloat16),
+            pltpu.VMEM((4, 2 * width, rows), jnp.bfloat16),
+            pltpu.SemaphoreType.DMA((4,)),
+        ],
+        name="weight_grad",
+    )(code, mine, theirs, *acts)
+
+
+def input_grad_kernel(code, *refs):
+    grads, key_w, value_w = refs[:4], refs[4:11], refs[11:18]
+    kept, sent, w_v, w_sem = refs[18:]
+    rows, features = kept.shape[1:]
+    width = grads[0].shape[1]
+
+    def weight_copies(act):
+        for part, weights in enumerate((key_w, value_w)):
+            for slot in range(2):
+                row = 2 * part + slot
+                slot_copies(
+                    code, code[1 + slot], weights, w_v.at[pl.ds(row * width, width)], w_sem.at[row], act
+                )
+
+    weight_copies(True)
+    weight_copies(False)
+    tile = features // 3
+    for j in (3, 1, 2, 0):
+        span = pl.ds(pl.multiple_of((code[0] ^ j) * rows, rows), rows)
+        grad = jnp.concatenate([ref[span, :] for ref in grads], axis=1)
+        target = sent if j % 2 else kept
+        for n in range(3):
+            lanes = slice(n * tile, (n + 1) * tile)
+            target[j // 2, :, lanes] = dot(grad, w_v[:, lanes]).astype(jnp.bfloat16)
+
+
+def input_grad(code, grads, key_weights, value_weights, rows):
+    width, features = key_weights[0].shape
+    return call(
+        input_grad_kernel,
+        [shaped((2, rows, features)), shaped((2, rows, features))],
+        32,
+        2 * 4 * rows * features * 4 * width,
+        4 * rows * features * 2 + 4 * width * features * 2,
+        in_specs=[SMEM] + [VMEM] * 4 + [ANY] * 14,
+        out_specs=[VMEM, VMEM],
+        scratch_shapes=[
+            pltpu.VMEM((4 * width, features), jnp.bfloat16),
+            pltpu.SemaphoreType.DMA((4,)),
+        ],
+        name="input_grad",
+    )(code, *grads, *key_weights, *value_weights)
+
+
+def body_planes(normed, q_raw, key_weight, value_weight, q_gain, k_gain, segment_ids, grad_out):
+    rows, features = normed.shape
+    half = 4 * rows
+    width = key_weight.shape[1]
+    place = lax.axis_index("seq")
+    uly = lax.axis_index("uly")
+    z, x, c = place // 4, (place // 2) % 2, place % 2
+
+    def slot_code(slot):
+        distance = z - (c + 2 * slot)
+        return jnp.where(distance >= 0, distance, 3 - distance)
+
+    code = jnp.stack(
+        [place % 4, slot_code(uly), slot_code(1 - uly), (c == uly).astype(jnp.int32)]
+    ).astype(jnp.int32)
+    gain_q = q_gain.reshape(1, HD)
+
+    slabs = call(
+        transpose_in_kernel,
+        shaped((2 * width, features)),
+        16,
+        0,
+        8 * width * features,
+        in_specs=[VMEM, VMEM],
+        out_specs=VMEM,
+        name="transpose_in",
+    )(key_weight, value_weight)
+    other = move(
+        slabs, [((z, x, 1 - z % 2), (z, x, z % 2)) for z in range(4) for x in (0, 1)]
+    )
+    first, second = jnp.where(c == 0, slabs, other), jnp.where(c == 0, other, slabs)
+    key_weights = line_gather(jnp.concatenate([first[:width], second[:width]], axis=0))
+    value_weights = line_gather(jnp.concatenate([first[width:], second[width:]], axis=0))
+
+    normed_x = swap_x(normed)
+    acts = (normed, swap_core(normed), normed_x, swap_core(normed_x))
+
+    heads = jnp.stack([q_raw, grad_out]).reshape(2, rows, 2, 2, 2 * HD)
+
+    def pick(array, axis, index):
+        return lax.dynamic_index_in_dim(array, index, axis, keepdims=False)
+
+    near = pick(heads, 3, x)
+    from_x = swap_x(pick(heads, 3, 1 - x))
+    stage = jnp.stack([near, from_x])
+    from_core = swap_core(pick(stage, 3, 1 - c))
+    stage = pick(stage, 3, c)
+    ordered = jnp.stack([stage[0], from_core[0], stage[1], from_core[1]])
+    q, go = ordered[:, 0], ordered[:, 1]
+
+    seg_pad = jnp.concatenate([jnp.full((half,), -1, jnp.int32), segment_ids])
+    key_seg = lax.dynamic_slice_in_dim(seg_pad, z * half, 2 * half, 0)
+    query_seg = lax.dynamic_slice_in_dim(segment_ids, z * half, half, 0)
+    lane = lax.broadcasted_iota(jnp.int32, (2 * half, HD), 1)
+    key_mark = jnp.where((lane < 2) & (lane != key_seg[:, None]), -MASKED, 0.0).astype(jnp.bfloat16)
+    row = lax.broadcasted_iota(jnp.int32, (HD, half), 0)
+    query_mark = jnp.where(row == query_seg[None, :], 1.0, 0.0).astype(jnp.bfloat16)
+
+    forward = [(z, c, z + 1) for z in range(3) for c in (0, 1)]
+    backward = [(z + 1, c, z) for z in range(3) for c in (0, 1)]
+
+    mine, theirs = project(code, acts, key_weights)
+    key_raw = mine.astype(jnp.float32) + swap_uly(theirs).astype(jnp.float32)
+    keys = normalized(key_raw, k_gain, 1.0).astype(jnp.bfloat16)
+    keys_before = along_z(keys, forward)
+    mine, theirs = project(code, acts, value_weights)
+    values = (mine.astype(jnp.float32) + swap_uly(theirs).astype(jnp.float32)).astype(jnp.bfloat16)
+    values_before = along_z(values, forward)
+
+    e, stat, dv_own, dv_before = attend_scores(
+        code, q, go, keys, keys_before, key_mark, query_mark, gain_q
+    )
+    value_grad = (dv_own + along_z(dv_before, backward).astype(jnp.float32)).astype(jnp.bfloat16)
+    value_grad_far = swap_uly(value_grad)
+    value_sums = line_reduce(*weight_grad(code, value_grad, value_grad_far, acts), z)
+
+    out, gq, dk_own, dk_before = attend_values(
+        code, q, go, keys, keys_before, values, values_before, gain_q, e, stat
+    )
+    dkey = dk_own + along_z(dk_before, backward).astype(jnp.float32)
+    key_grad = normalized_pull(key_raw, k_gain, 1.0, dkey).astype(jnp.bfloat16)
+    key_grad_far = swap_uly(key_grad)
+    key_sums = line_reduce(*weight_grad(code, key_grad, key_grad_far, acts), z)
+
+    pair = jnp.stack([out, gq], axis=1).reshape(2, 2, 2, rows, 2 * HD)
+    from_core = swap_core(pair[:, 1])
+    both = jnp.where(
+        c == 0, jnp.stack([pair[:, 0], from_core], axis=2), jnp.stack([from_core, pair[:, 0]], axis=2)
+    )
+    from_x = swap_x(both[1])
+    near = both[0]
+    both = jnp.where(
+        x == 0, jnp.stack([near, from_x], axis=2), jnp.stack([from_x, near], axis=2)
+    )
+    both = both.transpose(0, 3, 1, 2, 4).reshape(2, rows, 8 * HD)
+    attention, grad_q = both[0], both[1]
+
+    kept, sent = input_grad(
+        code, (key_grad, key_grad_far, value_grad, value_grad_far), key_weights, value_weights, rows
+    )
+    away = kept[1].astype(jnp.float32) + swap_core(sent[1]).astype(jnp.float32)
+    from_x = swap_x(away.astype(jnp.bfloat16))
+    grad_normed = (
+        kept[0].astype(jnp.float32)
+        + swap_core(sent[0]).astype(jnp.float32)
+        + from_x.astype(jnp.float32)
+    ).astype(jnp.bfloat16)
+
+    sums = jnp.stack([key_sums, value_sums]).reshape(2, 2, width, features)
+    other = move(
+        pick(sums, 1, 1 - c).astype(jnp.bfloat16),
+        [((z, x, z % 2), (z, x, 1 - z % 2)) for z in range(4) for x in (0, 1)],
+    )
+    halves = jnp.where(c == z % 2, pick(sums, 1, c), other.astype(jnp.float32))
+    grad_key_weight, grad_value_weight = call(
+        transpose_out_kernel,
+        [shaped((features, width), jnp.float32)] * 2,
+        16,
+        0,
+        16 * width * features,
+        in_specs=[VMEM, VMEM],
+        out_specs=[VMEM, VMEM],
+        name="transpose_out",
+    )(halves[0], halves[1])
+    return (attention, grad_normed, grad_q, grad_key_weight, grad_value_weight)
+
+
+def body(normed, q_raw, *rest):
+    planes = (
+        lax.axis_size("seq") == 16
+        and lax.axis_size("uly") == 2
+        and 4 * normed.shape[0] == WINDOW
+        and q_raw.shape[1] == 8 * HD
+    )
+    return (body_planes if planes else body_general)(normed, q_raw, *rest)
+
+
 def solution(mesh):
     return jax.shard_map(
         body,

time: 465 us -> 261 us (0.56)
  waiting for transfers between devices: 313 us -> 67.9 us
  starting transfers between devices: 26.6 us -> 83.9 us
  matrix products: 52 us -> 0 us
  Pallas kernels: 0 us -> 45.5 us
  between operations: 14.5 us -> 1.44 us
  blocking collectives: 12 us -> 0 us
  local copies, waits for them, and re-layouts: 22.9 us -> 31.8 us
  other arithmetic: 19.3 us -> 26.5 us
    reduce_scatter x4 -> x0, waiting for transfers between devices: 160 us -> none  [the longest x1 81.5 us: body(): lax.psum_scatter(value_part.astype(jnp.bfloat16), 'seq', scatter_dimensio...]
    all_gather x2 -> x0, waiting for transfers between devices: 113 us -> none  [the longest x1 60 us: body(): lax.all_gather(key_weight, 'seq', axis=1, tiled=True)]
    ppermute x8 -> x44, starting transfers between devices: 26.4 us -> 83.9 us  [the longest x40 79.1 us: move(): return lax.ppermute(array, 'seq', [(at(*a), at(*b)) for a, b in rule])]
    dot_general x12 -> x0, matrix products: 52 us -> none  [the longest x1 7.35 us: attend_block(): jnp.einsum('hgbl,lhe->bhge', weights, value_block, preferred_element_type...]
    pallas_call x0 -> x9, Pallas kernels: none -> 45.5 us  [the longest x2 11 us: project(): call(project_kernel, [shaped((4 * rows, width)), shaped((4 * rows, width)...]
    ppermute x8 -> x44, waiting for transfers between devices: 38.3 us -> 67.9 us  [the longest x40 64.8 us: move(): return lax.ppermute(array, 'seq', [(at(*a), at(*b)) for a, b in rule])]
    all_gather x2 -> x0, blocking collectives: 12 us -> none  [the longest x1 6.12 us: body(): lax.all_gather(key_grad, 'uly', axis=1, tiled=True)]
    add x2 -> x8, other arithmetic: 2.13 us -> 13.2 us  [the longest x2 3.67 us: line_reduce(): f3 = along_z(far + f2, [(1, 0, 0), (2, 1, 3)])]
  transfers between devices with their start and end apart: 14 -> 44, of which waited for: 11 -> 14; matrix products, arithmetic and copies ran while one was open for 11% -> 16% of each run, Pallas kernels for 0% -> 18%
where the time goes in v1:
time: 261 us; the launch traced here: 257 us
  starting transfers between devices  83.9 us (32%)
  waiting for transfers between devices  67.9 us (26%)
  Pallas kernels  45.5 us (17%)
  local copies, waits for them, and re-layouts  31.8 us (12%)
  other arithmetic  26.5 us (10%)
    ppermute x40, starting transfers between devices, move(): return lax.ppermute(array, 'seq', [(at(*a), at(*b)) for a, b in rule])  79.1 us
    ppermute x40, waiting for transfers between devices, move(): return lax.ppermute(array, 'seq', [(at(*a), at(*b)) for a, b in rule])  64.8 us
    unnamed x81, local copies, waits for them, and re-layouts  18.5 us
    pallas_call x2, Pallas kernels, project(): call(project_kernel, [shaped((4 * rows, width)), shaped((4 * rows, width)...  11 us
    pallas_call x2, Pallas kernels, weight_grad(): call(weight_grad_kernel, [shaped((width, features)), shaped((width, featu...  10.4 us
    pallas_call x1, Pallas kernels, attend_values(): call(values_kernel, [shaped(q.shape), shaped(q.shape), shaped((half, HD),...  8.6 us
    pallas_call x1, Pallas kernels, attend_scores(): call(scores_kernel, [shaped((blocks, 2, span, rows)), shaped((blocks, 8,...  8.56 us
    pallas_call x1, Pallas kernels, input_grad(): call(input_grad_kernel, [shaped((2, rows, features)), shaped((2, rows, fe...  5.68 us
  transfers between devices with their start and end apart: 44, of which 14 were waited for; matrix products, arithmetic and copies ran while one was open for 16% of the time, Pallas kernels for 18%

profile of v1, /device:TPU:17, one launch (start us, length us, event | category | flops | bytes accessed | tf_op | source)
XLA Modules:
  0.0 257.0 jit_solution(15793848434843949772)
XLA Ops:
  3.9 3.6 %collective-permute-start.5 = (bf16[128,2688]{1,0:T(8,128)(2,1)S(1)}, bf16[128,2688]{1,0:T(8,128)(2,1)}, u32[]{:S(2)}, u32[]{:S(2)}) collective-permute-start(bf16[128,2688]{1,0:T(8,128)(2,1)S(1)} %transpose_in.1), channel_id=1, source_target_pairs={{2,0},{6,4},{8,10},{12,14},{18,16},{22,20},{24,26},{28,30},{3,1},{... | collective-permute-start | bytes 2064392 | tf_op jit(solution)/shard_map/ppermute | solution.py:176
  12.8 12.7 %collective-permute-done = bf16[2,256,2,256]{3,1,0,2:T(8,128)(2,1)} collective-permute-done((bf16[2,256,2,256]{3,1,0,2:T(8,128)(2,1)}, bf16[2,256,2,256]{3,1,0,2:T(8,128)(2,1)}, u32[]{:S(2)}, u32[]{:S(2)}) %collective-permute-start) | collective-permute-done | bytes 524320 | tf_op jit(solution)/shard_map/ppermute | solution.py:176
  36.0 5.2 %collective-permute-done.9.refs_8_ = bf16[128,2688]{1,0:T(8,128)(2,1)S(1)} collective-permute-done((bf16[128,2688]{1,0:T(8,128)(2,1)S(1)}, bf16[128,2688]{1,0:T(8,128)(2,1)S(1)}, u32[]{:S(2)}, u32[]{:S(2)}) %collective-permute-start.9) | collective-permute-done | bytes 688160 | tf_op jit(solution)/shard_map/ppermute | solution.py:176
  42.5 6.1 %collective-permute-done.17.refs_8_.refs_15_ = bf16[128,2688]{1,0:T(8,128)(2,1)} collective-permute-done((bf16[128,2688]{1,0:T(8,128)(2,1)S(1)}, bf16[128,2688]{1,0:T(8,128)(2,1)}, u32[]{:S(2)}, u32[]{:S(2)}) %collective-permute-start.17) | collective-permute-done | bytes 688160 | tf_op jit(solution)/shard_map/ppermute | solution.py:176
  53.8 3.8 %collective-permute-start.10 = (bf16[128,2688]{1,0:T(8,128)(2,1)}, bf16[128,2688]{1,0:T(8,128)(2,1)}, u32[]{:S(2)}, u32[]{:S(2)}) collective-permute-start(bf16[128,2688]{1,0:T(8,128)(2,1)} %copy-done.10), channel_id=1, source_target_pairs={{18,10},{22,14},{8,0},{12,4},{19,11},{23,15},{9,1},{13,5}} | collective-permute-start | bytes 2064392 | tf_op jit(solution)/shard_map/ppermute | solution.py:176
  66.1 3.2 %collective-permute-done.7.refs_6_ = bf16[128,2688]{1,0:T(8,128)(2,1)} collective-permute-done((bf16[128,2688]{1,0:T(8,128)(2,1)}, bf16[128,2688]{1,0:T(8,128)(2,1)}, u32[]{:S(2)}, u32[]{:S(2)}) %collective-permute-start.7) | collective-permute-done | bytes 688160 | tf_op jit(solution)/shard_map/ppermute | solution.py:176
  72.3 5.6 %project.3 = (bf16[1024,128]{1,0:T(8,128)(2,1)S(1)}, bf16[1024,128]{1,0:T(8,128)(2,1)S(1)}) custom-call(s32[4]{0:T(128)S(1)} %pad_add_fusion.code, bf16[256,2688]{1,0:T(8,128)(2,1)S(1)} %copy-done, bf16[256,2688]{1,0:T(8,128)(2,1)} %collective-permute-done.2.refs_1_.a1, bf16[256,2688]{1,0:T(8,128)(2,1)S(1)} %collective-permute-done.3.refs_2_.a2, ...), custom_call_target="tpu_custom_call" | custom-call | flops 1409286144 | bytes 6881280 | tf_op jit(solution)/shard_map/project/pallas_call | solution.py:288
  79.3 5.4 %project.2 = (bf16[1024,128]{1,0:T(8,128)(2,1)S(1)}, bf16[1024,128]{1,0:T(8,128)(2,1)S(1)}) custom-call(s32[4]{0:T(128)S(1)} %pad_add_fusion.code, bf16[256,2688]{1,0:T(8,128)(2,1)S(1)} %copy-done, bf16[256,2688]{1,0:T(8,128)(2,1)} %collective-permute-done.2.refs_1_.a1, bf16[256,2688]{1,0:T(8,128)(2,1)S(1)} %collective-permute-done.3.refs_2_.a2, ...), custom_call_target="tpu_custom_call" | custom-call | flops 1409286144 | bytes 6881280 | tf_op jit(solution)/shard_map/project/pallas_call | solution.py:288
  85.5 4.0 %collective-permute-start.21 = (bf16[1024,128]{1,0:T(8,128)(2,1)S(1)}, bf16[1024,128]{1,0:T(8,128)(2,1)S(1)}, u32[]{:S(2)}, u32[]{:S(2)}) collective-permute-start(bf16[1024,128]{1,0:T(8,128)(2,1)S(1)} %add_convert_fusion.1.v_own), channel_id=1, source_target_pairs={{0,8},{4,12},{2,10},{6,14},{8,16},{12,20},{10,18},{14,22},{16,24},... | collective-permute-start | bytes 786440 | tf_op jit(solution)/shard_map/ppermute | solution.py:176
  90.5 4.2 %collective-permute-start.13 = (bf16[1024,128]{1,0:T(8,128)(2,1)S(1)}, bf16[1024,128]{1,0:T(8,128)(2,1)S(1)}, u32[]{:S(2)}, u32[]{:S(2)}) collective-permute-start(bf16[1024,128]{1,0:T(8,128)(2,1)S(1)} %multiply_convert_fusion.1.own_ref), channel_id=1, source_target_pairs={{0,8},{4,12},{2,10},{6,14},{8,16},{12,20},{10,18},{14,22},{16,24},... | collective-permute-start | bytes 786440 | tf_op jit(solution)/shard_map/ppermute | solution.py:176
  94.7 6.4 %collective-permute-done.13.before_ref = bf16[1024,128]{1,0:T(8,128)(2,1)S(1)} collective-permute-done((bf16[1024,128]{1,0:T(8,128)(2,1)S(1)}, bf16[1024,128]{1,0:T(8,128)(2,1)S(1)}, u32[]{:S(2)}, u32[]{:S(2)}) %collective-permute-start.13) | collective-permute-done | bytes 262176 | tf_op jit(solution)/shard_map/ppermute | solution.py:176
  101.1 8.6 %attend_scores.1 = (bf16[4,2,1280,256]{3,2,1,0:T(8,128)(2,1)S(1)}, f32[4,8,256]{2,1,0:T(8,128)S(1)}, f32[1024,128]{1,0:T(8,128)S(1)}, bf16[1024,128]{1,0:T(8,128)(2,1)S(1)}) custom-call(s32[4]{0:T(128)S(1)} %pad_add_fusion.code, bf16[4,256,256]{2,1,0:T(8,128)(2,1)S(1)} %get-tuple-element.63.q_ref, bf16[4,256,256]{2,1,0:T(8,128)(2,1)S(1)} %get-tuple-element.62.go_ref, ...), custom_call_target="tpu_custom_call" | custom-call | flops 2013265920 | bytes 7340032 | tf_op jit(solution)/shard_map/attend_scores/pallas_call | solution.py:378
  109.7 3.0 %collective-permute-start.26 = (bf16[1024,128]{1,0:T(8,128)(2,1)S(1)}, bf16[1024,128]{1,0:T(8,128)(2,1)S(1)}, u32[]{:S(2)}, u32[]{:S(2)}) collective-permute-start(bf16[1024,128]{1,0:T(8,128)(2,1)S(1)} %get-tuple-element.36), channel_id=1, source_target_pairs={{8,0},{12,4},{10,2},{14,6},{16,8},{20,12},{18,10},{22,14},{24,16},... | collective-permute-start | bytes 786440 | tf_op jit(solution)/shard_map/ppermute | solution.py:176
  112.7 8.6 %attend_values.1 = (bf16[4,256,256]{2,1,0:T(8,128)(2,1)S(1)}, bf16[4,256,256]{2,1,0:T(8,128)(2,1)S(1)}, f32[1024,128]{1,0:T(8,128)S(1)}, bf16[1024,128]{1,0:T(8,128)(2,1)S(1)}) custom-call(s32[4]{0:T(128)S(1)} %pad_add_fusion.code, bf16[4,256,256]{2,1,0:T(8,128)(2,1)S(1)} %get-tuple-element.63.q_ref, bf16[4,256,256]{2,1,0:T(8,128)(2,1)S(1)} %get-tuple-element.62.go_ref, ...), custom_call_target="tpu_custom_call" | custom-call | flops 2684354560 | bytes 7340032 | tf_op jit(solution)/shard_map/attend_values/pallas_call | solution.py:464
  125.1 3.7 %collective-permute-start.22 = (bf16[2,2,256,256]{3,2,0,1:T(8,128)(2,1)S(1)}, bf16[2,2,256,256]{3,2,0,1:T(8,128)(2,1)S(1)}, u32[]{:S(2)}, u32[]{:S(2)}) collective-permute-start(bf16[2,2,256,256]{3,2,0,1:T(8,128)(2,1)S(1)} %get-tuple-element.61), channel_id=1, source_target_pairs={{0,2},{2,0},{4,6},{6,4},{8,10},{10,8},{12,14},{14,12},{16,18},{18,... | collective-permute-start | bytes 1572872 | tf_op jit(solution)/shard_map/ppermute | solution.py:176
  129.0 5.2 %weight_grad.3 = (bf16[128,2688]{1,0:T(8,128)(2,1)S(1)}, bf16[128,2688]{1,0:T(8,128)(2,1)}) custom-call(s32[4]{0:T(128)S(1)} %pad_add_fusion.code, bf16[1024,128]{1,0:T(8,128)(2,1)S(1)} %add_convert_fusion.refs_2_.mine, bf16[1024,128]{1,0:T(8,128)(2,1)S(1)} %collective-permute-done.27.refs_3_.theirs, bf16[256,2688]{1,0:T(8,128)(2,1)S(1)} %copy-done, ...), custom_call_target="tpu_custom_call" | custom-call | flops 1409286144 | bytes 6881280 | tf_op jit(solution)/shard_map/weight_grad/pallas_call | solution.py:528
  140.6 5.2 %weight_grad.2 = (bf16[128,2688]{1,0:T(8,128)(2,1)}, bf16[128,2688]{1,0:T(8,128)(2,1)S(1)}) custom-call(s32[4]{0:T(128)S(1)} %pad_add_fusion.code, bf16[1024,128]{1,0:T(8,128)(2,1)S(1)} %multiply_convert_fusion.refs_0_.mine, bf16[1024,128]{1,0:T(8,128)(2,1)S(1)} %collective-permute-done.25.refs_1_.theirs, bf16[256,2688]{1,0:T(8,128)(2,1)S(1)} %copy-done, ...), custom_call_target="tpu_custom_call" | custom-call | flops 1409286144 | bytes 6881280 | tf_op jit(solution)/shard_map/weight_grad/pallas_call | solution.py:528
  160.9 5.7 %input_grad.1 = (bf16[2,256,2688]{2,1,0:T(8,128)(2,1)S(1)}, bf16[2,256,2688]{2,1,0:T(8,128)(2,1)S(1)}) custom-call(s32[4]{0:T(128)S(1)} %pad_add_fusion.code, bf16[1024,128]{1,0:T(8,128)(2,1)S(1)} %copy-done.20, bf16[1024,128]{1,0:T(8,128)(2,1)S(1)} %copy-done.26, bf16[1024,128]{1,0:T(8,128)(2,1)S(1)} %copy-done.18, bf16[1024,128]{1,0:T(8,128)(2,1)S(1)} %copy-done.24, ...), custom_call_target="tpu_custom_call" | custom-call | flops 2818572288 | bytes 8257536 | tf_op jit(solution)/shard_map/input_grad/pallas_call | solution.py:573
  170.3 6.0 %collective-permute-start.41 = (bf16[128,2688]{1,0:T(8,128)(2,1)}, bf16[128,2688]{1,0:T(8,128)(2,1)}, u32[]{:S(2)}, u32[]{:S(2)}) collective-permute-start(bf16[128,2688]{1,0:T(8,128)(2,1)} %add.146), channel_id=1, source_target_pairs={{18,10},{22,14},{8,16},{12,20},{19,11},{23,15},{9,17},{13,21}} | collective-permute-start | bytes 2064392 | tf_op jit(solution)/shard_map/ppermute | solution.py:176
  195.5 8.9 %collective-permute-start.28 = (bf16[256,2688]{1,0:T(8,128)(2,1)}, bf16[256,2688]{1,0:T(8,128)(2,1)}, u32[]{:S(2)}, u32[]{:S(2)}) collective-permute-start(bf16[256,2688]{1,0:T(8,128)(2,1)} %get-tuple-element.50), channel_id=1, source_target_pairs={{0,2},{2,0},{4,6},{6,4},{8,10},{10,8},{12,14},{14,12},{16,18},{18,... | collective-permute-start | bytes 4128776 | tf_op jit(solution)/shard_map/ppermute | solution.py:176
  207.5 3.7 %collective-permute-start.33 = (bf16[128,2688]{1,0:T(8,128)(2,1)S(1)}, bf16[128,2688]{1,0:T(8,128)(2,1)S(1)}, u32[]{:S(2)}, u32[]{:S(2)}) collective-permute-start(bf16[128,2688]{1,0:T(8,128)(2,1)S(1)} %add.138), channel_id=1, source_target_pairs={{8,0},{12,4},{18,26},{22,30},{9,1},{13,5},{19,27},{23,31}} | collective-permute-start | bytes 2064392 | tf_op jit(solution)/shard_map/ppermute | solution.py:176
  215.3 3.7 %collective-permute-done.33 = bf16[128,2688]{1,0:T(8,128)(2,1)S(1)} collective-permute-done((bf16[128,2688]{1,0:T(8,128)(2,1)S(1)}, bf16[128,2688]{1,0:T(8,128)(2,1)S(1)}, u32[]{:S(2)}, u32[]{:S(2)}) %collective-permute-start.33) | collective-permute-done | bytes 688160 | tf_op jit(solution)/shard_map/ppermute | solution.py:176
  232.2 21.5 %collective-permute-done.30 = bf16[256,2688]{1,0:T(8,128)(2,1)} collective-permute-done((bf16[256,2688]{1,0:T(8,128)(2,1)}, bf16[256,2688]{1,0:T(8,128)(2,1)}, u32[]{:S(2)}, u32[]{:S(2)}) %collective-permute-start.30) | collective-permute-done | bytes 1376288 | tf_op jit(solution)/shard_map/ppermute | solution.py:176
  253.7 3.3 %fusion.2 = bf16[256,2688]{1,0:T(8,128)(2,1)} fusion(bf16[256,2688]{1,0:T(8,128)(2,1)} %collective-permute-done.30, bf16[256,2688]{1,0:T(8,128)(2,1)} %collective-permute-done.28, bf16[2,256,2688]{2,1,0:T(8,128)(2,1)S(1)} %copy-done.9), kind=kLoop, calls=%fused_computation.8 | loop fusion | flops 4128768 | bytes 5505024 | tf_op jit(solution)/shard_map/convert_element_type | solution.py:695
  (205 shorter events, 108.3 us)
Async XLA Ops:
  3.9 23.8 %collective-permute-start.5 = (bf16[128,2688]{1,0:T(8,128)(2,1)S(1)}, bf16[128,2688]{1,0:T(8,128)(2,1)}, u32[]{:S(2)}, u32[]{:S(2)}) collective-permute-start(bf16[128,2688]{1,0:T(8,128)(2,1)S(1)} %transpose_in.1), channel_id=1, source_target_pairs={{2,0},{6,4},{8,10},{12,14},{18,16},{22,20},{24,26},{28,30},{3,1},{... | collective-permute-start | bytes 2064392 | tf_op jit(solution)/shard_map/ppermute | solution.py:176
  11.4 14.1 %collective-permute-start = (bf16[2,256,2,256]{3,1,0,2:T(8,128)(2,1)}, bf16[2,256,2,256]{3,1,0,2:T(8,128)(2,1)}, u32[]{:S(2)}, u32[]{:S(2)}) collective-permute-start(bf16[2,256,2,256]{3,1,0,2:T(8,128)(2,1)} %get-tuple-element.66), channel_id=1, source_target_pairs={{0,4},{2,6},{4,0},{6,2},{8,12},{10,14},{12,8},{14,10},{16,20},{18,... | collective-permute-start | bytes 1572872 | tf_op jit(solution)/shard_map/ppermute | solution.py:176
  12.6 41.2 %collective-permute-start.3 = (bf16[256,2688]{1,0:T(8,128)(2,1)S(1)}, bf16[256,2688]{1,0:T(8,128)(2,1)S(1)}, u32[]{:S(2)}, u32[]{:S(2)}) collective-permute-start(bf16[256,2688]{1,0:T(8,128)(2,1)S(1)} %copy-done), channel_id=1, source_target_pairs={{0,4},{2,6},{4,0},{6,2},{8,12},{10,14},{12,8},{14,10},{16,20},{18,... | collective-permute-start | bytes 4128776 | tf_op jit(solution)/shard_map/ppermute | solution.py:176
  30.4 27.2 %collective-permute-start.2 = (bf16[256,2688]{1,0:T(8,128)(2,1)S(1)}, bf16[256,2688]{1,0:T(8,128)(2,1)}, u32[]{:S(2)}, u32[]{:S(2)}) collective-permute-start(bf16[256,2688]{1,0:T(8,128)(2,1)S(1)} %copy-done), channel_id=1, source_target_pairs={{0,2},{2,0},{4,6},{6,4},{8,10},{10,8},{12,14},{14,12},{16,18},{18,... | collective-permute-start | bytes 4128776 | tf_op jit(solution)/shard_map/ppermute | solution.py:176
  32.5 16.0 %collective-permute-start.17 = (bf16[128,2688]{1,0:T(8,128)(2,1)S(1)}, bf16[128,2688]{1,0:T(8,128)(2,1)}, u32[]{:S(2)}, u32[]{:S(2)}) collective-permute-start(bf16[128,2688]{1,0:T(8,128)(2,1)S(1)} %pad_maximum_fusion.2.refs_4_.refs_11_), channel_id=1, source_target_pairs={{10,2},{14,6},{16,8},{20,12},{26,18},{30,22},{11,3},{15,7},{17,9},... | collective-permute-start | bytes 2064392 | tf_op jit(solution)/shard_map/ppermute | solution.py:176
  33.8 16.8 %collective-permute-start.14 = (bf16[128,2688]{1,0:T(8,128)(2,1)S(1)}, bf16[128,2688]{1,0:T(8,128)(2,1)}, u32[]{:S(2)}, u32[]{:S(2)}) collective-permute-start(bf16[128,2688]{1,0:T(8,128)(2,1)S(1)} %pad_maximum_fusion.2.refs_4_.refs_11_), channel_id=1, source_target_pairs={{0,8},{4,12},{10,18},{14,22},{16,24},{20,28},{1,9},{5,13},{11,19},... | collective-permute-start | bytes 2064392 | tf_op jit(solution)/shard_map/ppermute | solution.py:176
  53.8 18.5 %collective-permute-start.4 = (bf16[256,2688]{1,0:T(8,128)(2,1)S(1)}, bf16[256,2688]{1,0:T(8,128)(2,1)}, u32[]{:S(2)}, u32[]{:S(2)}) collective-permute-start(bf16[256,2688]{1,0:T(8,128)(2,1)S(1)} %collective-permute-done.3.refs_2_.a2), channel_id=1, source_target_pairs={{0,2},{2,0},{4,6},{6,4},{8,10},{10,8},{12,14},{14,12},{16,18},{18,... | collective-permute-start | bytes 4128776 | tf_op jit(solution)/shard_map/ppermute | solution.py:176
  65.4 13.8 %collective-permute-start.11 = (bf16[128,2688]{1,0:T(8,128)(2,1)}, bf16[128,2688]{1,0:T(8,128)(2,1)S(1)}, u32[]{:S(2)}, u32[]{:S(2)}) collective-permute-start(bf16[128,2688]{1,0:T(8,128)(2,1)} %collective-permute-done.10.refs_9_), channel_id=1, source_target_pairs={{10,2},{14,6},{11,3},{15,7}} | collective-permute-start | bytes 2064392 | tf_op jit(solution)/shard_map/ppermute | solution.py:176
  85.5 27.2 %collective-permute-start.21 = (bf16[1024,128]{1,0:T(8,128)(2,1)S(1)}, bf16[1024,128]{1,0:T(8,128)(2,1)S(1)}, u32[]{:S(2)}, u32[]{:S(2)}) collective-permute-start(bf16[1024,128]{1,0:T(8,128)(2,1)S(1)} %add_convert_fusion.1.v_own), channel_id=1, source_target_pairs={{0,8},{4,12},{2,10},{6,14},{8,16},{12,20},{10,18},{14,22},{16,24},... | collective-permute-start | bytes 786440 | tf_op jit(solution)/shard_map/ppermute | solution.py:176
  109.7 13.5 %collective-permute-start.26 = (bf16[1024,128]{1,0:T(8,128)(2,1)S(1)}, bf16[1024,128]{1,0:T(8,128)(2,1)S(1)}, u32[]{:S(2)}, u32[]{:S(2)}) collective-permute-start(bf16[1024,128]{1,0:T(8,128)(2,1)S(1)} %get-tuple-element.36), channel_id=1, source_target_pairs={{8,0},{12,4},{10,2},{14,6},{16,8},{20,12},{18,10},{22,14},{24,16},... | collective-permute-start | bytes 786440 | tf_op jit(solution)/shard_map/ppermute | solution.py:176
  134.3 13.1 %collective-permute-start.37 = (bf16[128,2688]{1,0:T(8,128)(2,1)S(1)}, bf16[128,2688]{1,0:T(8,128)(2,1)S(1)}, u32[]{:S(2)}, u32[]{:S(2)}) collective-permute-start(bf16[128,2688]{1,0:T(8,128)(2,1)S(1)} %get-tuple-element.41), channel_id=1, source_target_pairs={{24,16},{28,20},{2,10},{6,14},{25,17},{29,21},{3,11},{7,15}} | collective-permute-start | bytes 2064392 | tf_op jit(solution)/shard_map/ppermute | solution.py:176
  136.8 29.8 %collective-permute-start.40 = (bf16[128,2688]{1,0:T(8,128)(2,1)}, bf16[128,2688]{1,0:T(8,128)(2,1)}, u32[]{:S(2)}, u32[]{:S(2)}) collective-permute-start(bf16[128,2688]{1,0:T(8,128)(2,1)} %get-tuple-element.42), channel_id=1, source_target_pairs={{26,18},{30,22},{0,8},{4,12},{27,19},{31,23},{1,9},{5,13}} | collective-permute-start | bytes 2064392 | tf_op jit(solution)/shard_map/ppermute | solution.py:176
  145.9 24.4 %collective-permute-start.31 = (bf16[128,2688]{1,0:T(8,128)(2,1)}, bf16[128,2688]{1,0:T(8,128)(2,1)}, u32[]{:S(2)}, u32[]{:S(2)}) collective-permute-start(bf16[128,2688]{1,0:T(8,128)(2,1)} %get-tuple-element.39), channel_id=1, source_target_pairs={{24,16},{28,20},{2,10},{6,14},{25,17},{29,21},{3,11},{7,15}} | collective-permute-start | bytes 2064392 | tf_op jit(solution)/shard_map/ppermute | solution.py:176
  148.5 30.1 %collective-permute-start.38 = (bf16[128,2688]{1,0:T(8,128)(2,1)}, bf16[128,2688]{1,0:T(8,128)(2,1)}, u32[]{:S(2)}, u32[]{:S(2)}) collective-permute-start(bf16[128,2688]{1,0:T(8,128)(2,1)} %add.143), channel_id=1, source_target_pairs={{16,8},{20,12},{10,18},{14,22},{17,9},{21,13},{11,19},{15,23}} | collective-permute-start | bytes 2064392 | tf_op jit(solution)/shard_map/ppermute | solution.py:176
  150.9 31.4 %collective-permute-start.23 = (bf16[2,2,256,256]{3,2,0,1:T(8,128)(2,1)}, bf16[2,2,256,256]{3,2,0,1:T(8,128)(2,1)}, u32[]{:S(2)}, u32[]{:S(2)}) collective-permute-start(bf16[2,2,256,256]{3,2,0,1:T(8,128)(2,1)} %get-tuple-element.59), channel_id=1, source_target_pairs={{0,4},{2,6},{4,0},{6,2},{8,12},{10,14},{12,8},{14,10},{16,20},{18,... | collective-permute-start | bytes 1572872 | tf_op jit(solution)/shard_map/ppermute | solution.py:176
  152.2 53.7 %collective-permute-start.42 = (bf16[128,2688]{1,0:T(8,128)(2,1)}, bf16[128,2688]{1,0:T(8,128)(2,1)}, u32[]{:S(2)}, u32[]{:S(2)}) collective-permute-start(bf16[128,2688]{1,0:T(8,128)(2,1)} %get-tuple-element.42), channel_id=1, source_target_pairs={{2,10},{6,14},{24,16},{28,20},{3,11},{7,15},{25,17},{29,21}} | collective-permute-start | bytes 2064392 | tf_op jit(solution)/shard_map/ppermute | solution.py:176
  166.7 25.2 %collective-permute-start.34 = (bf16[128,2688]{1,0:T(8,128)(2,1)S(1)}, bf16[128,2688]{1,0:T(8,128)(2,1)}, u32[]{:S(2)}, u32[]{:S(2)}) collective-permute-start(bf16[128,2688]{1,0:T(8,128)(2,1)S(1)} %copy-done.7), channel_id=1, source_target_pairs={{26,18},{30,22},{0,8},{4,12},{27,19},{31,23},{1,9},{5,13}} | collective-permute-start | bytes 2064392 | tf_op jit(solution)/shard_map/ppermute | solution.py:176
  170.3 35.8 %collective-permute-start.41 = (bf16[128,2688]{1,0:T(8,128)(2,1)}, bf16[128,2688]{1,0:T(8,128)(2,1)}, u32[]{:S(2)}, u32[]{:S(2)}) collective-permute-start(bf16[128,2688]{1,0:T(8,128)(2,1)} %add.146), channel_id=1, source_target_pairs={{18,10},{22,14},{8,16},{12,20},{19,11},{23,15},{9,17},{13,21}} | collective-permute-start | bytes 2064392 | tf_op jit(solution)/shard_map/ppermute | solution.py:176
  178.6 16.9 %collective-permute-start.32 = (bf16[128,2688]{1,0:T(8,128)(2,1)}, bf16[128,2688]{1,0:T(8,128)(2,1)}, u32[]{:S(2)}, u32[]{:S(2)}) collective-permute-start(bf16[128,2688]{1,0:T(8,128)(2,1)} %add.137), channel_id=1, source_target_pairs={{16,8},{20,12},{10,18},{14,22},{17,9},{21,13},{11,19},{15,23}} | collective-permute-start | bytes 2064392 | tf_op jit(solution)/shard_map/ppermute | solution.py:176
  182.3 25.1 %collective-permute-start.39 = (bf16[128,2688]{1,0:T(8,128)(2,1)}, bf16[128,2688]{1,0:T(8,128)(2,1)}, u32[]{:S(2)}, u32[]{:S(2)}) collective-permute-start(bf16[128,2688]{1,0:T(8,128)(2,1)} %add.144), channel_id=1, source_target_pairs={{8,0},{12,4},{18,26},{22,30},{9,1},{13,5},{19,27},{23,31}} | collective-permute-start | bytes 2064392 | tf_op jit(solution)/shard_map/ppermute | solution.py:176
  191.8 21.6 %collective-permute-start.36 = (bf16[128,2688]{1,0:T(8,128)(2,1)S(1)}, bf16[128,2688]{1,0:T(8,128)(2,1)S(1)}, u32[]{:S(2)}, u32[]{:S(2)}) collective-permute-start(bf16[128,2688]{1,0:T(8,128)(2,1)S(1)} %copy-done.7), channel_id=1, source_target_pairs={{2,10},{6,14},{24,16},{28,20},{3,11},{7,15},{25,17},{29,21}} | collective-permute-start | bytes 2064392 | tf_op jit(solution)/shard_map/ppermute | solution.py:176
  195.5 36.6 %collective-permute-start.28 = (bf16[256,2688]{1,0:T(8,128)(2,1)}, bf16[256,2688]{1,0:T(8,128)(2,1)}, u32[]{:S(2)}, u32[]{:S(2)}) collective-permute-start(bf16[256,2688]{1,0:T(8,128)(2,1)} %get-tuple-element.50), channel_id=1, source_target_pairs={{0,2},{2,0},{4,6},{6,4},{8,10},{10,8},{12,14},{14,12},{16,18},{18,... | collective-permute-start | bytes 4128776 | tf_op jit(solution)/shard_map/ppermute | solution.py:176
  205.9 15.0 %collective-permute-start.29 = (bf16[256,2688]{1,0:T(8,128)(2,1)S(1)}, bf16[256,2688]{1,0:T(8,128)(2,1)S(1)}, u32[]{:S(2)}, u32[]{:S(2)}) collective-permute-start(bf16[256,2688]{1,0:T(8,128)(2,1)S(1)} %copy-done.32), channel_id=1, source_target_pairs={{0,2},{2,0},{4,6},{6,4},{8,10},{10,8},{12,14},{14,12},{16,18},{18,... | collective-permute-start | bytes 4128776 | tf_op jit(solution)/shard_map/ppermute | solution.py:176
  222.7 31.0 %collective-permute-start.30 = (bf16[256,2688]{1,0:T(8,128)(2,1)}, bf16[256,2688]{1,0:T(8,128)(2,1)}, u32[]{:S(2)}, u32[]{:S(2)}) collective-permute-start(bf16[256,2688]{1,0:T(8,128)(2,1)} %fusion), channel_id=1, source_target_pairs={{0,4},{2,6},{4,0},{6,2},{8,12},{10,14},{12,8},{14,10},{16,20},{18,... | collective-permute-start | bytes 4128776 | tf_op jit(solution)/shard_map/ppermute | solution.py:176
  (58 other events, 460.4 us)

commit v2 on v1

--- a/solution.py
+++ b/solution.py
@@ -163,7 +163,7 @@
 MIB = 1 << 20
 MASKED = 16384.0
 NT = (((1,), (1,)), ((), ()))
-ANY = pl.BlockSpec(memory_space=pl.ANY)
+HBM = pl.BlockSpec(memory_space=pltpu.HBM)
 SMEM = pl.BlockSpec(memory_space=pltpu.SMEM)
 VMEM = pl.BlockSpec(memory_space=pltpu.VMEM)
 
@@ -212,37 +212,29 @@
     return jax.ShapeDtypeStruct(shape, dtype)
 
 
-def transpose_in_kernel(key_ref, value_ref, out_ref):
-    both = jnp.concatenate([key_ref[...], value_ref[...]], axis=1).astype(jnp.float32)
-    out_ref[...] = both.T.astype(jnp.bfloat16)
-
-
-def transpose_out_kernel(key_ref, value_ref, key_out, value_out):
-    width = key_ref.shape[0]
-    both = jnp.concatenate([key_ref[...], value_ref[...]], axis=0).T
-    key_out[...] = both[:, :width]
-    value_out[...] = both[:, width:]
-
-
-def line_gather(own):
-    r1 = along_z(own, [(0, 0, 1), (1, 1, 2), (2, 0, 3)])
-    l1 = along_z(own, [(1, 1, 0), (2, 0, 1), (3, 1, 2)])
-    r2 = along_z(r1, [(1, 0, 2), (2, 1, 3)])
-    l2 = along_z(l1, [(2, 1, 1), (1, 0, 0)])
-    r3 = along_z(r2, [(2, 0, 3)])
-    l3 = along_z(l2, [(1, 1, 0)])
-    return (own, r1, r2, r3, l1, l2, l3)
-
-
-def line_reduce(far, mid, z):
-    f1 = along_z(far, [(3, 0, 2), (0, 1, 1)])
-    m1 = along_z(mid, [(3, 1, 2), (0, 0, 1)])
-    f2 = along_z(far + f1, [(2, 0, 1), (1, 1, 2)])
-    near = along_z(mid, [(0, 1, 1), (3, 0, 2)])
-    m2 = along_z(mid + m1, [(2, 1, 1), (1, 0, 2)])
-    f3 = along_z(far + f2, [(1, 0, 0), (2, 1, 3)])
-    own = jnp.where((z == 0) | (z == 3), far, mid).astype(jnp.float32)
-    return own + f3.astype(jnp.float32) + m2.astype(jnp.float32) + near.astype(jnp.float32)
+def after_all(arrays, *earlier):
+    return lax.optimization_barrier(tuple(arrays) + earlier)[: len(arrays)]
+
+
+def after(array, *earlier):
+    return after_all((array,), *earlier)[0]
+
+
+HOP_ONE = [(0, 0, 1), (3, 1, 2), (1, 1, 0), (2, 0, 3)]
+HOP_INNER = [(1, 1, 2), (2, 0, 1)]
+HOP_SECOND = [(1, 0, 2), (2, 1, 1)]
+HOP_OUTER = [(1, 0, 0), (2, 1, 3)]
+HOP_THIRD = [(2, 0, 3), (1, 1, 0)]
+BACK_THIRD, BACK_OUTER, BACK_MID, BACK_INNER, BACK_ONE = (
+    [(to, c, z) for z, c, to in hops]
+    for hops in (HOP_THIRD, HOP_OUTER, HOP_SECOND, HOP_INNER, HOP_ONE)
+)
+
+CHAIN = ((0, 1, 1, 0, 3, 2, 5, 4), (4, 5, 2, 3, 0, 1, 1, 0))
+
+
+def summed(parts):
+    return functools.reduce(jnp.add, [part.astype(jnp.float32) for part in parts])
 
 
 def slot_copies(code, slot_at, refs, buffer, sems, act):
@@ -255,31 +247,48 @@
 
 
 def project_kernel(code, *refs):
-    acts, weights = refs[:4], refs[4:11]
-    mine, theirs, acts_v, w_v, acts_sem, w_sem = refs[11:]
+    acts, weights = refs[:4], refs[4:-6]
+    mine, theirs, acts_v, w_v, acts_sem, w_sem = refs[-6:]
     width = mine.shape[1]
-    rows = acts[0].shape[0]
+    rows, features = acts[0].shape
     place = code[0]
 
     def weight_copies(act):
         for slot in range(2):
             slot_copies(
-                code, code[1 + slot], weights, w_v.at[pl.ds(slot * width, width)], w_sem.at[slot], act
+                code,
+                code[1 + slot],
+                weights,
+                w_v.at[pl.ds(slot * width, width)],
+                w_sem.at[slot],
+                act,
             )
 
     weight_copies(True)
-    copies = [
-        pltpu.make_async_copy(acts[j], acts_v.at[j], acts_sem.at[j]) for j in range(4)
-    ]
+    tile = features // 3
+    copies = []
+    for n in range(3):
+        lanes = pl.ds(n * tile, tile)
+        for j in range(4):
+            to = pl.ds(pl.multiple_of((place ^ j) * rows, rows), rows)
+            copies.append(
+                pltpu.make_async_copy(
+                    acts[j].at[:, lanes], acts_v.at[to, lanes], acts_sem.at[4 * n + j]
+                )
+            )
     for copy in copies:
         copy.start()
     weight_copies(False)
-    for j in range(4):
-        copies[j].wait()
-        both = lax.dot_general(acts_v[j], w_v[...], NT, preferred_element_type=jnp.float32)
-        begin = pl.multiple_of((place ^ j) * rows, rows)
-        mine[pl.ds(begin, rows), :] = both[:, :width].astype(jnp.bfloat16)
-        theirs[pl.ds(begin, rows), :] = both[:, width:].astype(jnp.bfloat16)
+    both = 0.0
+    for n in range(3):
+        lanes = slice(n * tile, (n + 1) * tile)
+        for copy in copies[4 * n : 4 * n + 4]:
+            copy.wait()
+        both = both + lax.dot_general(
+            acts_v[:, lanes], w_v[:, lanes], NT, preferred_element_type=jnp.float32
+        )
+    mine[...] = both[:, :width].astype(jnp.bfloat16)
+    theirs[...] = both[:, width:].astype(jnp.bfloat16)
 
 
 def project(code, acts, weights):
@@ -288,15 +297,15 @@
     return call(
         project_kernel,
         [shaped((4 * rows, width)), shaped((4 * rows, width))],
-        24,
+        12,
         2 * 4 * rows * features * 2 * width,
         4 * rows * features * 2 + 2 * width * features * 2,
-        in_specs=[SMEM] + [ANY] * 11,
+        in_specs=[SMEM] + [HBM] * (4 + len(weights)),
         out_specs=[VMEM, VMEM],
         scratch_shapes=[
-            pltpu.VMEM((4, rows, features), jnp.bfloat16),
+            pltpu.VMEM((4 * rows, features), jnp.bfloat16),
             pltpu.VMEM((2 * width, features), jnp.bfloat16),
-            pltpu.SemaphoreType.DMA((4,)),
+            pltpu.SemaphoreType.DMA((12,)),
             pltpu.SemaphoreType.DMA((2,)),
         ],
         name="project",
@@ -383,7 +392,7 @@
             shaped((half, HD), jnp.float32),
             shaped((half, HD)),
         ],
-        40,
+        14,
         2 * 2 * half * span * 3 * HD,
         2 * half * span * 2 + 8 * half * HD * 2,
         grid_spec=pltpu.PrefetchScalarGridSpec(
@@ -469,7 +478,7 @@
             shaped((half, HD), jnp.float32),
             shaped((half, HD)),
         ],
-        40,
+        16,
         2 * 2 * half * span * 4 * HD,
         2 * half * span * 2 + 8 * half * HD * 2,
         grid_spec=pltpu.PrefetchScalarGridSpec(
@@ -528,10 +537,10 @@
     return call(
         weight_grad_kernel,
         [shaped((width, features)), shaped((width, features))],
-        32,
-        2 * 4 * rows * features * 2 * width,
-        4 * rows * features * 2 + 2 * width * features * 2,
-        in_specs=[SMEM, VMEM, VMEM] + [ANY] * 4,
+        12,
+        0,
+        0,
+        in_specs=[SMEM, VMEM, VMEM] + [HBM] * 4,
         out_specs=[VMEM, VMEM],
         scratch_shapes=[
             pltpu.VMEM((4, rows, features), jnp.bfloat16),
@@ -543,8 +552,8 @@
 
 
 def input_grad_kernel(code, *refs):
-    grads, key_w, value_w = refs[:4], refs[4:11], refs[11:18]
-    kept, sent, w_v, w_sem = refs[18:]
+    grads, key_w, value_w = refs[:4], refs[4:10], refs[10:16]
+    kept, sent, w_v, w_sem = refs[16:]
     rows, features = kept.shape[1:]
     width = grads[0].shape[1]
 
@@ -573,10 +582,10 @@
     return call(
         input_grad_kernel,
         [shaped((2, rows, features)), shaped((2, rows, features))],
-        32,
+        16,
         2 * 4 * rows * features * 4 * width,
         4 * rows * features * 2 + 4 * width * features * 2,
-        in_specs=[SMEM] + [VMEM] * 4 + [ANY] * 14,
+        in_specs=[SMEM] + [VMEM] * 4 + [HBM] * 12,
         out_specs=[VMEM, VMEM],
         scratch_shapes=[
             pltpu.VMEM((4 * width, features), jnp.bfloat16),
@@ -594,51 +603,56 @@
     uly = lax.axis_index("uly")
     z, x, c = place // 4, (place // 2) % 2, place % 2
 
-    def slot_code(slot):
-        distance = z - (c + 2 * slot)
-        return jnp.where(distance >= 0, distance, 3 - distance)
-
-    code = jnp.stack(
-        [place % 4, slot_code(uly), slot_code(1 - uly), (c == uly).astype(jnp.int32)]
-    ).astype(jnp.int32)
+    on_line = z * 2 + c
+    chosen = [
+        jnp.asarray(CHAIN, jnp.int32)[slot, on_line] for slot in (uly, 1 - uly)
+    ]
+    inner = (z == 1) | (z == 2)
+    first_is_own = jnp.where(inner, c, 1 - c) == uly
+    code = jnp.stack([place % 4, *chosen, first_is_own]).astype(jnp.int32)
     gain_q = q_gain.reshape(1, HD)
 
-    slabs = call(
-        transpose_in_kernel,
-        shaped((2 * width, features)),
-        16,
-        0,
-        8 * width * features,
-        in_specs=[VMEM, VMEM],
-        out_specs=VMEM,
-        name="transpose_in",
-    )(key_weight, value_weight)
-    other = move(
-        slabs, [((z, x, 1 - z % 2), (z, x, z % 2)) for z in range(4) for x in (0, 1)]
-    )
-    first, second = jnp.where(c == 0, slabs, other), jnp.where(c == 0, other, slabs)
-    key_weights = line_gather(jnp.concatenate([first[:width], second[:width]], axis=0))
-    value_weights = line_gather(jnp.concatenate([first[width:], second[width:]], axis=0))
+    def picked(first_is_low, low, high):
+        return jnp.where(first_is_low, low, high)
 
     normed_x = swap_x(normed)
-    acts = (normed, swap_core(normed), normed_x, swap_core(normed_x))
-
-    heads = jnp.stack([q_raw, grad_out]).reshape(2, rows, 2, 2, 2 * HD)
-
-    def pick(array, axis, index):
-        return lax.dynamic_index_in_dim(array, index, axis, keepdims=False)
-
-    near = pick(heads, 3, x)
-    from_x = swap_x(pick(heads, 3, 1 - x))
-    stage = jnp.stack([near, from_x])
-    from_core = swap_core(pick(stage, 3, 1 - c))
-    stage = pick(stage, 3, c)
-    ordered = jnp.stack([stage[0], from_core[0], stage[1], from_core[1]])
-    q, go = ordered[:, 0], ordered[:, 1]
-
-    seg_pad = jnp.concatenate([jnp.full((half,), -1, jnp.int32), segment_ids])
+
+    def slab(weight):
+        other = move(
+            weight.T, [((z, x, 1 - z % 2), (z, x, z % 2)) for z in range(4) for x in (0, 1)]
+        )
+        both = (picked(c == 0, weight.T, other), picked(c == 0, other, weight.T))
+        return jnp.concatenate(both, axis=0)
+
+    key_slab = slab(key_weight)
+    value_slab = slab(value_weight)
+
+    k_one, k_inner = along_z(key_slab, HOP_ONE), along_z(key_slab, HOP_INNER)
+    v_one, v_inner = along_z(value_slab, HOP_ONE), along_z(value_slab, HOP_INNER)
+    normed_c = swap_core(after(normed, key_slab))
+    k_second, k_outer = along_z(k_one, HOP_SECOND), along_z(k_inner, HOP_OUTER)
+    v_one, v_inner = after_all((v_one, v_inner), k_one, k_inner)
+    v_second, v_outer = along_z(v_one, HOP_SECOND), along_z(v_inner, HOP_OUTER)
+    k_second, k_outer = after_all((k_second, k_outer), v_one, v_inner)
+    k_third = along_z(k_second, HOP_THIRD)
+    normed_x = after(normed_x, k_second, k_outer)
+    normed_xc = swap_core(normed_x)
+
+    def head(array, index):
+        return array[:, index * 2 * HD : (index + 1) * 2 * HD]
+
+    sources = after_all((q_raw, grad_out), normed_x)
+    from_x = swap_x(
+        jnp.stack([picked(x == 1, head(a, 2 * k), head(a, 2 * k + 1)) for a in sources for k in (0, 1)])
+    )
+    near = [picked(x == 0, head(a, 2 * k), head(a, 2 * k + 1)) for a in sources for k in (0, 1)]
+    v_second, v_outer = after_all((v_second, v_outer), normed_x, k_second)
+    v_third = along_z(v_second, HOP_THIRD)
+
+    segments = after(segment_ids, v_second, v_outer)
+    seg_pad = jnp.concatenate([jnp.full((half,), -1, jnp.int32), segments])
     key_seg = lax.dynamic_slice_in_dim(seg_pad, z * half, 2 * half, 0)
-    query_seg = lax.dynamic_slice_in_dim(segment_ids, z * half, half, 0)
+    query_seg = lax.dynamic_slice_in_dim(segments, z * half, half, 0)
     lane = lax.broadcasted_iota(jnp.int32, (2 * half, HD), 1)
     key_mark = jnp.where((lane < 2) & (lane != key_seg[:, None]), -MASKED, 0.0).astype(jnp.bfloat16)
     row = lax.broadcasted_iota(jnp.int32, (HD, half), 0)
@@ -647,69 +661,113 @@
     forward = [(z, c, z + 1) for z in range(3) for c in (0, 1)]
     backward = [(z + 1, c, z) for z in range(3) for c in (0, 1)]
 
+    acts = (normed, normed_c, normed_x, normed_xc)
+    k_third = after(k_third, v_second, v_outer)
+    key_weights = (key_slab, k_one, k_inner, k_second, k_outer, k_third)
     mine, theirs = project(code, acts, key_weights)
-    key_raw = mine.astype(jnp.float32) + swap_uly(theirs).astype(jnp.float32)
+    key_far = swap_uly(theirs)
+    from_x = after(from_x, theirs)
+    arrays = [near[0], near[1], near[2], near[3], from_x[0], from_x[1], from_x[2], from_x[3]]
+    from_core = swap_core(
+        jnp.stack([picked(c == 1, arrays[2 * k], arrays[2 * k + 1]) for k in range(4)])
+    )
+    kept = [picked(c == 0, arrays[2 * k], arrays[2 * k + 1]) for k in range(4)]
+
+    value_weights = (value_slab, v_one, v_inner, v_second, v_outer, after(v_third, theirs))
+    value_mine, value_theirs = project(code, acts, value_weights)
+    value_far = swap_uly(value_theirs)
+    key_far = after(key_far, value_theirs)
+    key_raw = mine.astype(jnp.float32) + key_far.astype(jnp.float32)
     keys = normalized(key_raw, k_gain, 1.0).astype(jnp.bfloat16)
     keys_before = along_z(keys, forward)
-    mine, theirs = project(code, acts, value_weights)
-    values = (mine.astype(jnp.float32) + swap_uly(theirs).astype(jnp.float32)).astype(jnp.bfloat16)
+    value_far, from_core = after_all((value_far, from_core), keys)
+    values = (value_mine.astype(jnp.float32) + value_far.astype(jnp.float32)).astype(jnp.bfloat16)
     values_before = along_z(values, forward)
-
+    q = jnp.stack([kept[0], from_core[0], kept[2], from_core[2]])
+    go = jnp.stack([kept[1], from_core[1], kept[3], from_core[3]])
+
+    keys_before = after(keys_before, values)
     e, stat, dv_own, dv_before = attend_scores(
         code, q, go, keys, keys_before, key_mark, query_mark, gain_q
     )
-    value_grad = (dv_own + along_z(dv_before, backward).astype(jnp.float32)).astype(jnp.bfloat16)
-    value_grad_far = swap_uly(value_grad)
-    value_sums = line_reduce(*weight_grad(code, value_grad, value_grad_far, acts), z)
-
+    dv_back = along_z(dv_before, backward)
+    values_before = after(values_before, e)
     out, gq, dk_own, dk_before = attend_values(
         code, q, go, keys, keys_before, values, values_before, gain_q, e, stat
     )
-    dkey = dk_own + along_z(dk_before, backward).astype(jnp.float32)
+    dk_back = along_z(dk_before, backward)
+    value_grad = (dv_own + after(dv_back, dk_own).astype(jnp.float32)).astype(jnp.bfloat16)
+    value_grad_far = swap_uly(value_grad)
+
+    out, gq = after_all((out, gq), value_grad)
+    from_core = swap_core(jnp.stack([out[1], out[3], gq[1], gq[3]]))
+    own_pairs = ((out[0], from_core[0]), (gq[0], from_core[2]))
+    far_pairs = ((out[2], from_core[1]), (gq[2], from_core[3]))
+
+    def by_core(pairs):
+        return [picked((c == 0) == (k == 0), a, b) for a, b in pairs for k in (0, 1)]
+
+    back_payload = jnp.stack(by_core(far_pairs))
+    back_x = swap_x(back_payload)
+    own_heads = by_core(own_pairs)
+
+    dkey = dk_own + after(dk_back, back_payload).astype(jnp.float32)
     key_grad = normalized_pull(key_raw, k_gain, 1.0, dkey).astype(jnp.bfloat16)
     key_grad_far = swap_uly(key_grad)
-    key_sums = line_reduce(*weight_grad(code, key_grad, key_grad_far, acts), z)
-
-    pair = jnp.stack([out, gq], axis=1).reshape(2, 2, 2, rows, 2 * HD)
-    from_core = swap_core(pair[:, 1])
-    both = jnp.where(
-        c == 0, jnp.stack([pair[:, 0], from_core], axis=2), jnp.stack([from_core, pair[:, 0]], axis=2)
-    )
-    from_x = swap_x(both[1])
-    near = both[0]
-    both = jnp.where(
-        x == 0, jnp.stack([near, from_x], axis=2), jnp.stack([from_x, near], axis=2)
-    )
-    both = both.transpose(0, 3, 1, 2, 4).reshape(2, rows, 8 * HD)
-    attention, grad_q = both[0], both[1]
-
-    kept, sent = input_grad(
-        code, (key_grad, key_grad_far, value_grad, value_grad_far), key_weights, value_weights, rows
-    )
-    away = kept[1].astype(jnp.float32) + swap_core(sent[1]).astype(jnp.float32)
-    from_x = swap_x(away.astype(jnp.bfloat16))
-    grad_normed = (
-        kept[0].astype(jnp.float32)
-        + swap_core(sent[0]).astype(jnp.float32)
-        + from_x.astype(jnp.float32)
-    ).astype(jnp.bfloat16)
-
-    sums = jnp.stack([key_sums, value_sums]).reshape(2, 2, width, features)
-    other = move(
-        pick(sums, 1, 1 - c).astype(jnp.bfloat16),
-        [((z, x, z % 2), (z, x, 1 - z % 2)) for z in range(4) for x in (0, 1)],
-    )
-    halves = jnp.where(c == z % 2, pick(sums, 1, c), other.astype(jnp.float32))
-    grad_key_weight, grad_value_weight = call(
-        transpose_out_kernel,
-        [shaped((features, width), jnp.float32)] * 2,
-        16,
-        0,
-        16 * width * features,
-        in_specs=[VMEM, VMEM],
-        out_specs=[VMEM, VMEM],
-        name="transpose_out",
-    )(halves[0], halves[1])
+    value_grad_far = after(value_grad_far, key_grad)
+
+    v_first, v_second = weight_grad(code, value_grad, value_grad_far, acts)
+    v_third, v_outer = along_z(v_second, BACK_THIRD), along_z(v_first, BACK_OUTER)
+    key_grad_far = after(key_grad_far, v_first, back_x)
+    grads = (key_grad, key_grad_far, value_grad, value_grad_far)
+    kept, sent = input_grad(code, grads, key_weights, value_weights, rows)
+    sent = swap_core(sent)
+    key_grad_far = after(key_grad_far, kept)
+    k_first, k_second = weight_grad(code, key_grad, key_grad_far, acts)
+    k_third, k_outer = along_z(k_second, BACK_THIRD), along_z(k_first, BACK_OUTER)
+    v_third, v_outer = after_all((v_third, v_outer), k_first)
+    v_mid_payload, v_inner_payload = v_first + v_third, v_second + v_outer
+    v_mid, v_inner = along_z(v_mid_payload, BACK_MID), along_z(v_inner_payload, BACK_INNER)
+    sent = after(sent, v_mid_payload, v_inner_payload)
+    away = (kept[1].astype(jnp.float32) + sent[1].astype(jnp.float32)).astype(jnp.bfloat16)
+    from_x = swap_x(away)
+    own_sum = kept[0].astype(jnp.float32) + sent[0].astype(jnp.float32)
+    k_third, k_outer = after_all((k_third, k_outer), away)
+    k_mid_payload, k_inner_payload = k_first + k_third, k_second + k_outer
+    k_mid, k_inner = along_z(k_mid_payload, BACK_MID), along_z(k_inner_payload, BACK_INNER)
+    v_mid, v_inner, own_sum, back_x = after_all(
+        (v_mid, v_inner, own_sum, back_x), k_mid_payload, k_inner_payload
+    )
+    v_one_payload = v_first + v_mid
+    v_one = along_z(v_one_payload, BACK_ONE)
+    k_mid, k_inner = after_all((k_mid, k_inner), v_one_payload)
+    k_one_payload = k_first + k_mid
+    k_one = along_z(k_one_payload, BACK_ONE)
+
+    def by_x(own, far, k):
+        return [picked(x == 0, own[k], far[k]), picked(x == 0, far[k], own[k])]
+
+    attention, grad_q = (
+        jnp.concatenate(by_x(own_heads, back_x, k) + by_x(own_heads, back_x, k + 1), axis=1)
+        for k in (0, 2)
+    )
+    def halves(total):
+        own, away = (picked(c == k, total[:width], total[width:]) for k in (0, 1))
+        other = move(
+            away.astype(jnp.bfloat16),
+            [((z, x, z % 2), (z, x, 1 - z % 2)) for z in range(4) for x in (0, 1)],
+        )
+        return own, other
+
+    def owned(own, other):
+        return jnp.where(c == z % 2, own, other.astype(jnp.float32)).T
+
+    v_one, from_x = after_all((v_one, from_x), k_one_payload)
+    value_sum, value_other = halves(summed((v_second, v_inner, v_one)))
+    grad_normed = (own_sum + from_x.astype(jnp.float32)).astype(jnp.bfloat16)
+    grad_value_weight = owned(value_sum, after(value_other, grad_normed))
+    k_one = after(k_one, grad_value_weight, grad_normed, attention, grad_q)
+    grad_key_weight = owned(*halves(summed((k_second, k_inner, k_one))))
     return (attention, grad_normed, grad_q, grad_key_weight, grad_value_weight)
 
 

time: 261 us -> 206 us (0.79)
  local copies, waits for them, and re-layouts: 31.8 us -> 5.18 us
  starting transfers between devices: 83.9 us -> 66.3 us
  Pallas kernels: 45.5 us -> 40.1 us
  waiting for transfers between devices: 67.9 us -> 62.7 us
    ppermute x40 -> x37, starting transfers between devices: 79.1 us -> 62.4 us  [move(): return lax.ppermute(array, 'seq', [(at(*a), at(*b)) for a, b in rule])]
    unnamed x81 -> x72, local copies, waits for them, and re-layouts: 18.5 us -> 4.5 us
    squeeze x6 -> x0, local copies, waits for them, and re-layouts: 5.24 us -> none  [the longest x2 2.32 us: body_planes(): attention, grad_q = (both[0], both[1])]
    add x8, other arithmetic: 13.2 us -> 9.02 us  [the longest x2 2.79 us: body_planes(): k_mid_payload, k_inner_payload = (k_first + k_third, k_second + k_outer)]
    slice x6 -> x3, local copies, waits for them, and re-layouts: 4.18 us -> 0.07 us  [the longest x2 0.04 us: body_planes(): from_core = swap_core(jnp.stack([out[1], out[3], gq[1], gq[3]]))]
    ppermute x40 -> x37, waiting for transfers between devices: 64.8 us -> 60.8 us  [move(): return lax.ppermute(array, 'seq', [(at(*a), at(*b)) for a, b in rule])]
    another operation x4 -> x0, local copies, waits for them, and re-layouts: 3.79 us -> none  [the longest x3 2.76 us: body_planes(): heads = jnp.stack([q_raw, grad_out]).reshape(2, rows, 2, 2, 2 * HD)]
    select_n x3 -> x5, other arithmetic: 1.52 us -> 4.4 us  [picked(): return jnp.where(first_is_low, low, high)]
  transfers between devices with their start and end apart: 44 -> 41, of which waited for: 14 -> 15; matrix products, arithmetic and copies ran while one was open for 16% -> 12% of each run, Pallas kernels for 18% -> 17%
where the time goes in v2:
time: 206 us; the launch traced here: 204 us
  starting transfers between devices  66.3 us (32%)
  waiting for transfers between devices  62.7 us (30%)
  Pallas kernels  40.1 us (19%)
  other arithmetic  28.1 us (14%)
  local copies, waits for them, and re-layouts  5.18 us (3%)
    ppermute x37, starting transfers between devices, move(): return lax.ppermute(array, 'seq', [(at(*a), at(*b)) for a, b in rule])  62.4 us
    ppermute x37, waiting for transfers between devices, move(): return lax.ppermute(array, 'seq', [(at(*a), at(*b)) for a, b in rule])  60.8 us
    pallas_call x2, Pallas kernels, project(): call(project_kernel, [shaped((4 * rows, width)), shaped((4 * rows, width)...  9.49 us
    pallas_call x1, Pallas kernels, attend_values(): call(values_kernel, [shaped(q.shape), shaped(q.shape), shaped((half, HD),...  8.57 us
    pallas_call x1, Pallas kernels, attend_scores(): call(scores_kernel, [shaped((blocks, 2, span, rows)), shaped((blocks, 8,...  8.55 us
    pallas_call x2, Pallas kernels, weight_grad(): call(weight_grad_kernel, [shaped((width, features)), shaped((width, featu...  7.65 us
    pallas_call x1, Pallas kernels, input_grad(): call(input_grad_kernel, [shaped((2, rows, features)), shaped((2, rows, fe...  5.83 us
    unnamed x72, local copies, waits for them, and re-layouts  4.5 us
  transfers between devices with their start and end apart: 41, of which 15 were waited for; matrix products, arithmetic and copies ran while one was open for 12% of the time, Pallas kernels for 17%

profile of v2, /device:TPU:17, one launch (start us, length us, event | category | flops | bytes accessed | tf_op | source)
XLA Modules:
  0.0 204.0 jit_solution(9955829449739332055)
XLA Ops:
  0.6 2.6 %collective-permute-start.6 = (bf16[64,2688]{1,0:T(8,128)(2,1)}, bf16[64,2688]{1,0:T(8,128)(2,1)S(1)}, u32[]{:S(2)}, u32[]{:S(2)}) collective-permute-start(bf16[64,2688]{1,0:T(8,128)(2,1)} %bitcast.53), channel_id=1, source_target_pairs={{2,0},{6,4},{8,10},{12,14},{18,16},{22,20},{24,26},{28,30},{3,1},{... | collective-permute-start | bytes 1032200 | tf_op jit(solution)/shard_map/ppermute | solution.py:176
  14.4 5.0 %collective-permute-done.4.refs_6_ = bf16[128,2688]{1,0:T(8,128)(2,1)S(1)} collective-permute-done((bf16[128,2688]{1,0:T(8,128)(2,1)S(1)}, bf16[128,2688]{1,0:T(8,128)(2,1)S(1)}, u32[]{:S(2)}, u32[]{:S(2)}) %collective-permute-start.4) | collective-permute-done | bytes 688160 | tf_op jit(solution)/shard_map/ppermute | solution.py:176
  23.7 4.4 %collective-permute-done.8.refs_6_.refs_12_ = bf16[128,2688]{1,0:T(8,128)(2,1)} collective-permute-done((bf16[128,2688]{1,0:T(8,128)(2,1)S(1)}, bf16[128,2688]{1,0:T(8,128)(2,1)}, u32[]{:S(2)}, u32[]{:S(2)}) %collective-permute-start.8) | collective-permute-done | bytes 688160 | tf_op jit(solution)/shard_map/ppermute | solution.py:176
  28.2 7.0 %collective-permute-start.11 = (bf16[128,2688]{1,0:T(8,128)(2,1)}, bf16[128,2688]{1,0:T(8,128)(2,1)}, u32[]{:S(2)}, u32[]{:S(2)}) collective-permute-start(bf16[128,2688]{1,0:T(8,128)(2,1)} %collective-permute-done.7.refs_5_.refs_11_), channel_id=1, source_target_pairs={{8,16},{12,20},{18,10},{22,14},{9,17},{13,21},{19,11},{23,15}} | collective-permute-start | bytes 2064392 | tf_op jit(solution)/shard_map/ppermute | solution.py:176
  40.1 2.8 %collective-permute-start.10 = (bf16[256,2688]{1,0:T(8,128)(2,1)S(1)}, bf16[256,2688]{1,0:T(8,128)(2,1)S(1)}, u32[]{:S(2)}, u32[]{:S(2)}) collective-permute-start(bf16[256,2688]{1,0:T(8,128)(2,1)S(1)} %collective-permute-done.refs_2_.a2), channel_id=1, source_target_pairs={{0,2},{2,0},{4,6},{6,4},{8,10},{10,8},{12,14},{14,12},{16,18},{18,... | collective-permute-start | bytes 4128776 | tf_op jit(solution)/shard_map/ppermute | solution.py:176
  42.9 2.6 %collective-permute-done.12.refs_8_.refs_14_ = bf16[128,2688]{1,0:T(8,128)(2,1)} collective-permute-done((bf16[128,2688]{1,0:T(8,128)(2,1)}, bf16[128,2688]{1,0:T(8,128)(2,1)}, u32[]{:S(2)}, u32[]{:S(2)}) %collective-permute-start.12) | collective-permute-done | bytes 688160 | tf_op jit(solution)/shard_map/ppermute | solution.py:176
  51.6 4.8 %project.2 = (bf16[1024,128]{1,0:T(8,128)(2,1)S(1)}, bf16[1024,128]{1,0:T(8,128)(2,1)S(1)}) custom-call(s32[4]{0:T(128)S(1)} %pad_add_fusion.code, bf16[256,2688]{1,0:T(8,128)(2,1)S(1)} %copy-done, bf16[256,2688]{1,0:T(8,128)(2,1)S(1)} %collective-permute-done.9.refs_1_.a1, bf16[256,2688]{1,0:T(8,128)(2,1)S(1)} %collective-permute-done.refs_2_.a2, ...), custom_call_target="tpu_custom_call" | custom-call | flops 1409286144 | bytes 6881280 | tf_op jit(solution)/shard_map/project/pallas_call | solution.py:297
  57.4 2.6 %collective-permute-done.16 = bf16[4,256,256]{2,1,0:T(8,128)(2,1)S(1)} collective-permute-done((bf16[4,256,256]{2,1,0:T(8,128)(2,1)S(1)}, bf16[4,256,256]{2,1,0:T(8,128)(2,1)S(1)}, u32[]{:S(2)}, u32[]{:S(2)}) %collective-permute-start.16) | collective-permute-done | bytes 524320 | tf_op jit(solution)/shard_map/ppermute | solution.py:176
  60.0 4.7 %project.3 = (bf16[1024,128]{1,0:T(8,128)(2,1)S(1)}, bf16[1024,128]{1,0:T(8,128)(2,1)S(1)}) custom-call(s32[4]{0:T(128)S(1)} %pad_add_fusion.code, bf16[256,2688]{1,0:T(8,128)(2,1)S(1)} %copy-done, bf16[256,2688]{1,0:T(8,128)(2,1)S(1)} %collective-permute-done.9.refs_1_.a1, bf16[256,2688]{1,0:T(8,128)(2,1)S(1)} %collective-permute-done.refs_2_.a2, ...), custom_call_target="tpu_custom_call" | custom-call | flops 1409286144 | bytes 6881280 | tf_op jit(solution)/shard_map/project/pallas_call | solution.py:297
  66.2 2.6 %collective-permute-start.17 = (bf16[4,256,256]{2,1,0:T(8,128)(2,1)S(1)}, bf16[4,256,256]{2,1,0:T(8,128)(2,1)S(1)}, u32[]{:S(2)}, u32[]{:S(2)}) collective-permute-start(bf16[4,256,256]{2,1,0:T(8,128)(2,1)S(1)} %pad_maximum_fusion.3), channel_id=1, source_target_pairs={{0,2},{2,0},{4,6},{6,4},{8,10},{10,8},{12,14},{14,12},{16,18},{18,... | collective-permute-start | bytes 1572872 | tf_op jit(solution)/shard_map/ppermute | solution.py:176
  73.2 5.8 %collective-permute-done.19.before_ref = bf16[1024,128]{1,0:T(8,128)(2,1)S(1)} collective-permute-done((bf16[1024,128]{1,0:T(8,128)(2,1)S(1)}, bf16[1024,128]{1,0:T(8,128)(2,1)S(1)}, u32[]{:S(2)}, u32[]{:S(2)}) %collective-permute-start.19) | collective-permute-done | bytes 262176 | tf_op jit(solution)/shard_map/ppermute | solution.py:176
  79.2 8.5 %attend_scores.1 = (bf16[4,2,1280,256]{3,2,1,0:T(8,128)(2,1)S(1)}, f32[4,8,256]{2,1,0:T(8,128)S(1)}, f32[1024,128]{1,0:T(8,128)S(1)}, bf16[1024,128]{1,0:T(8,128)(2,1)S(1)}) custom-call(s32[4]{0:T(128)S(1)} %pad_add_fusion.code, bf16[4,256,256]{2,1,0:T(8,128)(2,1)S(1)} %pad_maximum_fusion.4.q_ref, bf16[4,256,256]{2,1,0:T(8,128)(2,1)S(1)} %pad_maximum_fusion.5.go_ref, ...), custom_call_target="tpu_custom_call" | custom-call | flops 2013265920 | bytes 7340032 | tf_op jit(solution)/shard_map/attend_scores/pallas_call | solution.py:387
  89.9 8.6 %attend_values.1 = (bf16[4,256,256]{2,1,0:T(8,128)(2,1)S(1)}, bf16[4,256,256]{2,1,0:T(8,128)(2,1)S(1)}, f32[1024,128]{1,0:T(8,128)S(1)}, bf16[1024,128]{1,0:T(8,128)(2,1)S(1)}) custom-call(s32[4]{0:T(128)S(1)} %pad_add_fusion.code, bf16[4,256,256]{2,1,0:T(8,128)(2,1)S(1)} %pad_maximum_fusion.4.q_ref, bf16[4,256,256]{2,1,0:T(8,128)(2,1)S(1)} %pad_maximum_fusion.5.go_ref, ...), custom_call_target="tpu_custom_call" | custom-call | flops 2684354560 | bytes 7340032 | tf_op jit(solution)/shard_map/attend_values/pallas_call | solution.py:473
  100.3 2.2 %collective-permute-start.22 = (bf16[4,256,256]{2,1,0:T(8,128)(2,1)}, bf16[4,256,256]{2,1,0:T(8,128)(2,1)}, u32[]{:S(2)}, u32[]{:S(2)}) collective-permute-start(bf16[4,256,256]{2,1,0:T(8,128)(2,1)} %pad_maximum_fusion.6), channel_id=1, source_target_pairs={{0,2},{2,0},{4,6},{6,4},{8,10},{10,8},{12,14},{14,12},{16,18},{18,... | collective-permute-start | bytes 1572872 | tf_op jit(solution)/shard_map/ppermute | solution.py:176
  107.2 5.0 %collective-permute-done.24 = bf16[1024,128]{1,0:T(8,128)(2,1)S(1)} collective-permute-done((bf16[1024,128]{1,0:T(8,128)(2,1)}, bf16[1024,128]{1,0:T(8,128)(2,1)S(1)}, u32[]{:S(2)}, u32[]{:S(2)}) %collective-permute-start.24) | collective-permute-done | bytes 262176 | tf_op jit(solution)/shard_map/ppermute | solution.py:176
  114.3 3.3 %weight_grad.2 = (bf16[128,2688]{1,0:T(8,128)(2,1)S(1)}, bf16[128,2688]{1,0:T(8,128)(2,1)S(1)}) custom-call(s32[4]{0:T(128)S(1)} %pad_add_fusion.code, bf16[1024,128]{1,0:T(8,128)(2,1)S(1)} %copy-done.13, bf16[1024,128]{1,0:T(8,128)(2,1)S(1)} %collective-permute-done.23.theirs.refs_3_, bf16[256,2688]{1,0:T(8,128)(2,1)S(1)} %copy-done, ...), custom_call_target="tpu_custom_call" | custom-call | tf_op jit(solution)/shard_map/weight_grad/pallas_call | solution.py:537
  120.4 5.8 %input_grad.1 = (bf16[2,256,2688]{2,1,0:T(8,128)(2,1)S(1)}, bf16[2,256,2688]{2,1,0:T(8,128)(2,1)S(1)}) custom-call(s32[4]{0:T(128)S(1)} %pad_add_fusion.code, bf16[1024,128]{1,0:T(8,128)(2,1)S(1)} %multiply_convert_fusion.refs_0_.mine, bf16[1024,128]{1,0:T(8,128)(2,1)S(1)} %collective-permute-done.27.refs_1_.theirs, bf16[1024,128]{1,0:T(8,128)(2,1)S(1)} %copy-done.13, ...), custom_call_target="tpu_custom_call" | custom-call | flops 2818572288 | bytes 8257536 | tf_op jit(solution)/shard_map/input_grad/pallas_call | solution.py:582
  130.0 4.3 %weight_grad.3 = (bf16[128,2688]{1,0:T(8,128)(2,1)}, bf16[128,2688]{1,0:T(8,128)(2,1)}) custom-call(s32[4]{0:T(128)S(1)} %pad_add_fusion.code, bf16[1024,128]{1,0:T(8,128)(2,1)S(1)} %multiply_convert_fusion.refs_0_.mine, bf16[1024,128]{1,0:T(8,128)(2,1)S(1)} %collective-permute-done.27.refs_1_.theirs, bf16[256,2688]{1,0:T(8,128)(2,1)S(1)} %copy-done, ...), custom_call_target="tpu_custom_call" | custom-call | tf_op jit(solution)/shard_map/weight_grad/pallas_call | solution.py:537
  136.4 11.7 %collective-permute-done.26 = bf16[128,2688]{1,0:T(8,128)(2,1)S(1)} collective-permute-done((bf16[128,2688]{1,0:T(8,128)(2,1)S(1)}, bf16[128,2688]{1,0:T(8,128)(2,1)S(1)}, u32[]{:S(2)}, u32[]{:S(2)}) %collective-permute-start.26) | collective-permute-done | bytes 688160 | tf_op jit(solution)/shard_map/ppermute | solution.py:176
  156.8 5.9 %collective-permute-done.33 = bf16[128,2688]{1,0:T(8,128)(2,1)} collective-permute-done((bf16[128,2688]{1,0:T(8,128)(2,1)}, bf16[128,2688]{1,0:T(8,128)(2,1)}, u32[]{:S(2)}, u32[]{:S(2)}) %collective-permute-start.33) | collective-permute-done | bytes 688160 | tf_op jit(solution)/shard_map/ppermute | solution.py:176
  177.3 8.3 %collective-permute-done.36 = bf16[128,2688]{1,0:T(8,128)(2,1)S(1)} collective-permute-done((bf16[128,2688]{1,0:T(8,128)(2,1)S(1)}, bf16[128,2688]{1,0:T(8,128)(2,1)S(1)}, u32[]{:S(2)}, u32[]{:S(2)}) %collective-permute-start.36) | collective-permute-done | bytes 688160 | tf_op jit(solution)/shard_map/ppermute | solution.py:176
  190.1 2.6 %add_convert_fusion = bf16[256,2688]{1,0:T(8,128)(2,1)} fusion(f32[256,2688]{1,0:T(8,128)S(1)} %copy-done.25, bf16[256,2688]{1,0:T(8,128)(2,1)} %collective-permute-done.35), kind=kLoop, calls=%fused_computation | loop fusion | flops 2064384 | bytes 5505024 | tf_op jit(solution)/shard_map/convert_element_type | solution.py:767
  193.7 2.4 %collective-permute-done.38 = bf16[128,2688]{1,0:T(8,128)(2,1)S(1)} collective-permute-done((bf16[128,2688]{1,0:T(8,128)(2,1)S(1)}, bf16[128,2688]{1,0:T(8,128)(2,1)S(1)}, u32[]{:S(2)}, u32[]{:S(2)}) %collective-permute-start.38) | collective-permute-done | bytes 688160 | tf_op jit(solution)/shard_map/ppermute | solution.py:176
  198.8 4.3 %collective-permute-done.40 = bf16[64,2688]{1,0:T(8,128)(2,1)S(1)} collective-permute-done((bf16[64,2688]{1,0:T(8,128)(2,1)S(1)}, bf16[64,2688]{1,0:T(8,128)(2,1)S(1)}, u32[]{:S(2)}, u32[]{:S(2)}) %collective-permute-start.40) | collective-permute-done | bytes 344096 | tf_op jit(solution)/shard_map/ppermute | solution.py:176
  (186 shorter events, 84.6 us)
Async XLA Ops:
  4.6 35.5 %collective-permute-start = (bf16[256,2688]{1,0:T(8,128)(2,1)}, bf16[256,2688]{1,0:T(8,128)(2,1)S(1)}, u32[]{:S(2)}, u32[]{:S(2)}) collective-permute-start(bf16[256,2688]{1,0:T(8,128)(2,1)} %a0.3), channel_id=1, source_target_pairs={{0,4},{2,6},{4,0},{6,2},{8,12},{10,14},{12,8},{14,10},{16,20},{18,... | collective-permute-start | bytes 4128776 | tf_op jit(solution)/shard_map/ppermute | solution.py:176
  7.3 12.1 %collective-permute-start.4 = (bf16[128,2688]{1,0:T(8,128)(2,1)S(1)}, bf16[128,2688]{1,0:T(8,128)(2,1)S(1)}, u32[]{:S(2)}, u32[]{:S(2)}) collective-permute-start(bf16[128,2688]{1,0:T(8,128)(2,1)S(1)} %pad_maximum_fusion.refs_4_), channel_id=1, source_target_pairs={{10,18},{14,22},{16,8},{20,12},{11,19},{15,23},{17,9},{21,13}} | collective-permute-start | bytes 2064392 | tf_op jit(solution)/shard_map/ppermute | solution.py:176
  8.7 12.8 %collective-permute-start.2 = (bf16[128,2688]{1,0:T(8,128)(2,1)S(1)}, bf16[128,2688]{1,0:T(8,128)(2,1)}, u32[]{:S(2)}, u32[]{:S(2)}) collective-permute-start(bf16[128,2688]{1,0:T(8,128)(2,1)S(1)} %pad_maximum_fusion.refs_4_), channel_id=1, source_target_pairs={{0,8},{4,12},{26,18},{30,22},{10,2},{14,6},{16,24},{20,28},{1,9},{... | collective-permute-start | bytes 2064392 | tf_op jit(solution)/shard_map/ppermute | solution.py:176
  10.9 17.2 %collective-permute-start.8 = (bf16[128,2688]{1,0:T(8,128)(2,1)S(1)}, bf16[128,2688]{1,0:T(8,128)(2,1)}, u32[]{:S(2)}, u32[]{:S(2)}) collective-permute-start(bf16[128,2688]{1,0:T(8,128)(2,1)S(1)} %pad_maximum_fusion.1.refs_4_.refs_10_), channel_id=1, source_target_pairs={{10,18},{14,22},{16,8},{20,12},{11,19},{15,23},{17,9},{21,13}} | collective-permute-start | bytes 2064392 | tf_op jit(solution)/shard_map/ppermute | solution.py:176
  12.2 16.0 %collective-permute-start.7 = (bf16[128,2688]{1,0:T(8,128)(2,1)S(1)}, bf16[128,2688]{1,0:T(8,128)(2,1)}, u32[]{:S(2)}, u32[]{:S(2)}) collective-permute-start(bf16[128,2688]{1,0:T(8,128)(2,1)S(1)} %pad_maximum_fusion.1.refs_4_.refs_10_), channel_id=1, source_target_pairs={{0,8},{4,12},{26,18},{30,22},{10,2},{14,6},{16,24},{20,28},{1,9},{... | collective-permute-start | bytes 2064392 | tf_op jit(solution)/shard_map/ppermute | solution.py:176
  19.4 19.8 %collective-permute-start.5 = (bf16[128,2688]{1,0:T(8,128)(2,1)S(1)}, bf16[128,2688]{1,0:T(8,128)(2,1)}, u32[]{:S(2)}, u32[]{:S(2)}) collective-permute-start(bf16[128,2688]{1,0:T(8,128)(2,1)S(1)} %collective-permute-done.4.refs_6_), channel_id=1, source_target_pairs={{8,0},{12,4},{18,26},{22,30},{9,1},{13,5},{19,27},{23,31}} | collective-permute-start | bytes 2064392 | tf_op jit(solution)/shard_map/ppermute | solution.py:176
  21.6 17.7 %collective-permute-start.3 = (bf16[128,2688]{1,0:T(8,128)(2,1)}, bf16[128,2688]{1,0:T(8,128)(2,1)}, u32[]{:S(2)}, u32[]{:S(2)}) collective-permute-start(bf16[128,2688]{1,0:T(8,128)(2,1)} %collective-permute-done.2.refs_5_), channel_id=1, source_target_pairs={{8,16},{12,20},{18,10},{22,14},{9,17},{13,21},{19,11},{23,15}} | collective-permute-start | bytes 2064392 | tf_op jit(solution)/shard_map/ppermute | solution.py:176
  28.2 14.7 %collective-permute-start.11 = (bf16[128,2688]{1,0:T(8,128)(2,1)}, bf16[128,2688]{1,0:T(8,128)(2,1)}, u32[]{:S(2)}, u32[]{:S(2)}) collective-permute-start(bf16[128,2688]{1,0:T(8,128)(2,1)} %collective-permute-done.7.refs_5_.refs_11_), channel_id=1, source_target_pairs={{8,16},{12,20},{18,10},{22,14},{9,17},{13,21},{19,11},{23,15}} | collective-permute-start | bytes 2064392 | tf_op jit(solution)/shard_map/ppermute | solution.py:176
  45.5 14.5 %collective-permute-start.13 = (bf16[128,2688]{1,0:T(8,128)(2,1)}, bf16[128,2688]{1,0:T(8,128)(2,1)S(1)}, u32[]{:S(2)}, u32[]{:S(2)}) collective-permute-start(bf16[128,2688]{1,0:T(8,128)(2,1)} %collective-permute-done.11.refs_7_.refs_13_), channel_id=1, source_target_pairs={{16,24},{20,28},{10,2},{14,6},{17,25},{21,29},{11,3},{15,7}} | collective-permute-start | bytes 2064392 | tf_op jit(solution)/shard_map/ppermute | solution.py:176
  47.5 12.4 %collective-permute-start.16 = (bf16[4,256,256]{2,1,0:T(8,128)(2,1)S(1)}, bf16[4,256,256]{2,1,0:T(8,128)(2,1)S(1)}, u32[]{:S(2)}, u32[]{:S(2)}) collective-permute-start(bf16[4,256,256]{2,1,0:T(8,128)(2,1)S(1)} %pad_maximum_fusion.2), channel_id=1, source_target_pairs={{0,4},{2,6},{4,0},{6,2},{8,12},{10,14},{12,8},{14,10},{16,20},{18,... | collective-permute-start | bytes 1572872 | tf_op jit(solution)/shard_map/ppermute | solution.py:176
  56.3 12.4 %collective-permute-start.18 = (bf16[1024,128]{1,0:T(8,128)(2,1)S(1)}, bf16[1024,128]{1,0:T(8,128)(2,1)S(1)}, u32[]{:S(2)}, u32[]{:S(2)}) collective-permute-start(bf16[1024,128]{1,0:T(8,128)(2,1)S(1)} %get-tuple-element.74), channel_id=1, source_target_pairs={{0,1},{1,0},{2,3},{3,2},{4,5},{5,4},{6,7},{7,6},{8,9},{9,8},{10,11... | collective-permute-start | bytes 786440 | tf_op jit(solution)/shard_map/ppermute | solution.py:196
  71.3 18.6 %collective-permute-start.20 = (bf16[1024,128]{1,0:T(8,128)(2,1)S(1)}, bf16[1024,128]{1,0:T(8,128)(2,1)S(1)}, u32[]{:S(2)}, u32[]{:S(2)}) collective-permute-start(bf16[1024,128]{1,0:T(8,128)(2,1)S(1)} %add_convert_fusion.3.v_own), channel_id=1, source_target_pairs={{0,8},{4,12},{2,10},{6,14},{8,16},{12,20},{10,18},{14,22},{16,24},... | collective-permute-start | bytes 786440 | tf_op jit(solution)/shard_map/ppermute | solution.py:176
  102.5 11.8 %collective-permute-start.23 = (bf16[1024,128]{1,0:T(8,128)(2,1)}, bf16[1024,128]{1,0:T(8,128)(2,1)S(1)}, u32[]{:S(2)}, u32[]{:S(2)}) collective-permute-start(bf16[1024,128]{1,0:T(8,128)(2,1)} %add_convert_fusion.2.mine.refs_2_), channel_id=1, source_target_pairs={{0,1},{1,0},{2,3},{3,2},{4,5},{5,4},{6,7},{7,6},{8,9},{9,8},{10,11... | collective-permute-start | bytes 786440 | tf_op jit(solution)/shard_map/ppermute | solution.py:196
  105.8 13.8 %collective-permute-start.28 = (bf16[4,256,256]{2,1,0:T(8,128)(2,1)S(1)}, bf16[4,256,256]{2,1,0:T(8,128)(2,1)S(1)}, u32[]{:S(2)}, u32[]{:S(2)}) collective-permute-start(bf16[4,256,256]{2,1,0:T(8,128)(2,1)S(1)} %pad_maximum_fusion.7), channel_id=1, source_target_pairs={{0,4},{2,6},{4,0},{6,2},{8,12},{10,14},{12,8},{14,10},{16,20},{18,... | collective-permute-start | bytes 1572872 | tf_op jit(solution)/shard_map/ppermute | solution.py:176
  126.2 26.8 %collective-permute-start.31 = (bf16[2,256,2688]{2,1,0:T(8,128)(2,1)S(1)}, bf16[2,256,2688]{2,1,0:T(8,128)(2,1)S(1)}, u32[]{:S(2)}, u32[]{:S(2)}) collective-permute-start(bf16[2,256,2688]{2,1,0:T(8,128)(2,1)S(1)} %get-tuple-element.108), channel_id=1, source_target_pairs={{0,2},{2,0},{4,6},{6,4},{8,10},{10,8},{12,14},{14,12},{16,18},{18,... | collective-permute-start | bytes 8257544 | tf_op jit(solution)/shard_map/ppermute | solution.py:176
  128.7 19.3 %collective-permute-start.26 = (bf16[128,2688]{1,0:T(8,128)(2,1)S(1)}, bf16[128,2688]{1,0:T(8,128)(2,1)S(1)}, u32[]{:S(2)}, u32[]{:S(2)}) collective-permute-start(bf16[128,2688]{1,0:T(8,128)(2,1)S(1)} %get-tuple-element.100), channel_id=1, source_target_pairs={{0,8},{4,12},{26,18},{30,22},{1,9},{5,13},{27,19},{31,23}} | collective-permute-start | bytes 2064392 | tf_op jit(solution)/shard_map/ppermute | solution.py:176
  134.4 22.5 %collective-permute-start.32 = (bf16[128,2688]{1,0:T(8,128)(2,1)}, bf16[128,2688]{1,0:T(8,128)(2,1)S(1)}, u32[]{:S(2)}, u32[]{:S(2)}) collective-permute-start(bf16[128,2688]{1,0:T(8,128)(2,1)} %get-tuple-element.110), channel_id=1, source_target_pairs={{24,16},{28,20},{2,10},{6,14},{25,17},{29,21},{3,11},{7,15}} | collective-permute-start | bytes 2064392 | tf_op jit(solution)/shard_map/ppermute | solution.py:176
  135.1 27.6 %collective-permute-start.33 = (bf16[128,2688]{1,0:T(8,128)(2,1)}, bf16[128,2688]{1,0:T(8,128)(2,1)}, u32[]{:S(2)}, u32[]{:S(2)}) collective-permute-start(bf16[128,2688]{1,0:T(8,128)(2,1)} %get-tuple-element.105), channel_id=1, source_target_pairs={{0,8},{4,12},{26,18},{30,22},{1,9},{5,13},{27,19},{31,23}} | collective-permute-start | bytes 2064392 | tf_op jit(solution)/shard_map/ppermute | solution.py:176
  150.2 18.1 %collective-permute-start.30 = (bf16[128,2688]{1,0:T(8,128)(2,1)}, bf16[128,2688]{1,0:T(8,128)(2,1)S(1)}, u32[]{:S(2)}, u32[]{:S(2)}) collective-permute-start(bf16[128,2688]{1,0:T(8,128)(2,1)} %add.120), channel_id=1, source_target_pairs={{18,10},{22,14},{8,16},{12,20},{19,11},{23,15},{9,17},{13,21}} | collective-permute-start | bytes 2064392 | tf_op jit(solution)/shard_map/ppermute | solution.py:176
  151.5 18.7 %collective-permute-start.29 = (bf16[128,2688]{1,0:T(8,128)(2,1)}, bf16[128,2688]{1,0:T(8,128)(2,1)}, u32[]{:S(2)}, u32[]{:S(2)}) collective-permute-start(bf16[128,2688]{1,0:T(8,128)(2,1)} %add.119), channel_id=1, source_target_pairs={{16,8},{20,12},{10,18},{14,22},{17,9},{21,13},{11,19},{15,23}} | collective-permute-start | bytes 2064392 | tf_op jit(solution)/shard_map/ppermute | solution.py:176
  155.1 33.1 %collective-permute-start.35 = (bf16[256,2688]{1,0:T(8,128)(2,1)S(1)}, bf16[256,2688]{1,0:T(8,128)(2,1)}, u32[]{:S(2)}, u32[]{:S(2)}) collective-permute-start(bf16[256,2688]{1,0:T(8,128)(2,1)S(1)} %get-tuple-element.123), channel_id=1, source_target_pairs={{0,4},{2,6},{4,0},{6,2},{8,12},{10,14},{12,8},{14,10},{16,20},{18,... | collective-permute-start | bytes 4128776 | tf_op jit(solution)/shard_map/ppermute | solution.py:176
  165.5 11.8 %collective-permute-start.37 = (bf16[128,2688]{1,0:T(8,128)(2,1)S(1)}, bf16[128,2688]{1,0:T(8,128)(2,1)S(1)}, u32[]{:S(2)}, u32[]{:S(2)}) collective-permute-start(bf16[128,2688]{1,0:T(8,128)(2,1)S(1)} %add.125), channel_id=1, source_target_pairs={{18,10},{22,14},{8,16},{12,20},{19,11},{23,15},{9,17},{13,21}} | collective-permute-start | bytes 2064392 | tf_op jit(solution)/shard_map/ppermute | solution.py:176
  167.0 18.6 %collective-permute-start.36 = (bf16[128,2688]{1,0:T(8,128)(2,1)S(1)}, bf16[128,2688]{1,0:T(8,128)(2,1)S(1)}, u32[]{:S(2)}, u32[]{:S(2)}) collective-permute-start(bf16[128,2688]{1,0:T(8,128)(2,1)S(1)} %add.124), channel_id=1, source_target_pairs={{16,8},{20,12},{10,18},{14,22},{17,9},{21,13},{11,19},{15,23}} | collective-permute-start | bytes 2064392 | tf_op jit(solution)/shard_map/ppermute | solution.py:176
  171.5 16.7 %collective-permute-start.34 = (bf16[128,2688]{1,0:T(8,128)(2,1)S(1)}, bf16[128,2688]{1,0:T(8,128)(2,1)S(1)}, u32[]{:S(2)}, u32[]{:S(2)}) collective-permute-start(bf16[128,2688]{1,0:T(8,128)(2,1)S(1)} %add.126), channel_id=1, source_target_pairs={{8,0},{12,4},{18,26},{22,30},{2,10},{6,14},{24,16},{28,20},{9,1},{... | collective-permute-start | bytes 2064392 | tf_op jit(solution)/shard_map/ppermute | solution.py:176
  (53 other events, 473.8 us)

commit v3 on v2

--- a/solution.py
+++ b/solution.py
@@ -196,14 +196,12 @@
     return lax.ppermute(array, "uly", [(0, 1), (1, 0)])
 
 
-def call(kernel, out_shape, vmem, flops, bytes_accessed, **rest):
+def call(kernel, out_shape, vmem, flops=0, accessed=0, **rest):
     return pl.pallas_call(
         kernel,
         out_shape=out_shape,
         compiler_params=pltpu.CompilerParams(vmem_limit_bytes=vmem * MIB),
-        cost_estimate=pl.CostEstimate(
-            flops=flops, bytes_accessed=bytes_accessed, transcendentals=0
-        ),
+        cost_estimate=pl.CostEstimate(flops=flops, bytes_accessed=accessed, transcendentals=0),
         **rest,
     )
 
@@ -233,8 +231,97 @@
 CHAIN = ((0, 1, 1, 0, 3, 2, 5, 4), (4, 5, 2, 3, 0, 1, 1, 0))
 
 
-def summed(parts):
-    return functools.reduce(jnp.add, [part.astype(jnp.float32) for part in parts])
+def sums_kernel(counts, *refs):
+    terms, outs = refs[: sum(counts)], refs[sum(counts) :]
+    for out, count in zip(outs, counts):
+        total = terms[0][...].astype(jnp.float32)
+        for term in terms[1:count]:
+            total = total + term[...].astype(jnp.float32)
+        out[...] = total.astype(out.dtype)
+        terms = terms[count:]
+
+
+def sums(*groups):
+    terms = [term for group in groups for term in group]
+    return call(
+        functools.partial(sums_kernel, [len(group) for group in groups]),
+        [shaped(group[0].shape) for group in groups],
+        12,
+        in_specs=[VMEM] * len(terms),
+        out_specs=[VMEM] * len(groups),
+        name="sums",
+    )(*terms)
+
+
+def halves_kernel(code, a, b, c, own, away):
+    width = own.shape[0]
+    total = a[...].astype(jnp.float32) + b[...].astype(jnp.float32) + c[...].astype(jnp.float32)
+    low = code[4] == 0
+    own[...] = jnp.where(low, total[:width], total[width:])
+    away[...] = jnp.where(low, total[width:], total[:width]).astype(jnp.bfloat16)
+
+
+def halves(code, parts):
+    width, features = parts[0].shape
+    return call(
+        halves_kernel,
+        [shaped((width // 2, features), jnp.float32), shaped((width // 2, features))],
+        12,
+        in_specs=[SMEM] + [VMEM] * 3,
+        out_specs=[VMEM] * 2,
+        name="halves",
+    )(code, *parts)
+
+
+def owned_kernel(code, own, other, out):
+    out[...] = jnp.where(code[6] == 1, own[...], other[...].astype(jnp.float32))
+
+
+def owned(code, own, other):
+    return call(
+        owned_kernel,
+        shaped(own.shape, jnp.float32),
+        12,
+        in_specs=[SMEM] + [VMEM] * 2,
+        out_specs=VMEM,
+        name="owned",
+    )(code, own, other).T
+
+
+def pack_kernel(first, second, out):
+    out[0] = first[1]
+    out[1] = second[1]
+
+
+def pack(first, second):
+    return call(
+        pack_kernel, shaped(second.shape), 12, in_specs=[VMEM] * 2, out_specs=VMEM, name="pack"
+    )(first, second)
+
+
+def by_head_kernel(code, near, near_other, far, attention, grad_q):
+    lanes = near.shape[3]
+    core, x = code[4], code[5]
+    for which, out in enumerate((attention, grad_q)):
+        for k, side, source in (
+            (core, x, near.at[0, which]),
+            (1 - core, x, near_other.at[0, which]),
+            (core, 1 - x, far.at[0, which]),
+            (1 - core, 1 - x, far.at[1, which]),
+        ):
+            out[:, pl.ds(pl.multiple_of((2 * k + side) * lanes, lanes), lanes)] = source[...]
+
+
+def by_head(code, near, near_other, far):
+    _, _, rows, lanes = near.shape
+    return call(
+        by_head_kernel,
+        [shaped((rows, 4 * lanes))] * 2,
+        12,
+        in_specs=[SMEM] + [VMEM] * 3,
+        out_specs=[VMEM] * 2,
+        name="by_head",
+    )(code, near, near_other, far)
 
 
 def slot_copies(code, slot_at, refs, buffer, sems, act):
@@ -248,7 +335,7 @@
 
 def project_kernel(code, *refs):
     acts, weights = refs[:4], refs[4:-6]
-    mine, theirs, acts_v, w_v, acts_sem, w_sem = refs[-6:]
+    mine, theirs, w_v, acts_v, acts_sem, w_sem = refs[-6:]
     width = mine.shape[1]
     rows, features = acts[0].shape
     place = code[0]
@@ -296,15 +383,12 @@
     width = weights[0].shape[0]
     return call(
         project_kernel,
-        [shaped((4 * rows, width)), shaped((4 * rows, width))],
+        [shaped((4 * rows, width)), shaped((4 * rows, width)), shaped((2 * width, features))],
         12,
-        2 * 4 * rows * features * 2 * width,
-        4 * rows * features * 2 + 2 * width * features * 2,
         in_specs=[SMEM] + [HBM] * (4 + len(weights)),
-        out_specs=[VMEM, VMEM],
+        out_specs=[VMEM, VMEM, VMEM],
         scratch_shapes=[
             pltpu.VMEM((4 * rows, features), jnp.bfloat16),
-            pltpu.VMEM((2 * width, features), jnp.bfloat16),
             pltpu.SemaphoreType.DMA((12,)),
             pltpu.SemaphoreType.DMA((2,)),
         ],
@@ -393,8 +477,6 @@
             shaped((half, HD)),
         ],
         14,
-        2 * 2 * half * span * 3 * HD,
-        2 * half * span * 2 + 8 * half * HD * 2,
         grid_spec=pltpu.PrefetchScalarGridSpec(
             num_scalar_prefetch=1,
             grid=(blocks,),
@@ -424,7 +506,7 @@
 
 def values_kernel(
     code, q_ref, go_ref, own_ref, before_ref, v_own, v_before, gain_ref, e_ref, stat_ref,
-    out_ref, gq_ref, dk_own, dk_before, values_v, values_t, keys_t, acc
+    kept, sent, dk_own, dk_before, values_v, values_t, keys_t, acc
 ):
     block = pl.program_id(0)
     rows = q_ref.shape[1]
@@ -440,6 +522,14 @@
         keys_t[:, half:] = own_ref[...].astype(jnp.float32).T.astype(jnp.bfloat16)
         acc[...] = jnp.zeros_like(acc)
 
+    piece = block ^ code[0]
+    odd = (piece % 2 == 1) & jnp.ones((rows, HD), jnp.bool_)
+
+    def put(which, lanes, result):
+        for target, here in ((kept, ~odd), (sent, odd)):
+            at_piece = target.at[piece // 2, which, :, lanes]
+            at_piece[...] = jnp.where(here, result, at_piece[...])
+
     span = pl.ds(pl.multiple_of(block * rows, rows), span_rows)
     for g in range(2):
         lanes = slice(g * HD, (g + 1) * HD)
@@ -448,16 +538,15 @@
         inverse = stat_ref[0, g : g + 1, :]
         e = e_ref[0, g]
         out_t = dot(values_t[:, span], e) * inverse
-        out_ref[0, :, lanes] = out_t.T.astype(jnp.bfloat16)
+        put(0, lanes, out_t.T.astype(jnp.bfloat16))
         grad_t = go_ref[0, :, lanes].astype(jnp.float32).T
         along = jnp.sum(out_t * grad_t, axis=0, keepdims=True) * inverse
         dprob = dot(values_v[span, :], (grad_t * inverse).astype(jnp.bfloat16))
         dscore = (e.astype(jnp.float32) * (dprob - along)).astype(jnp.bfloat16)
         acc[span, :] = acc[span, :] + dot(dscore, query)
         dquery = dot(keys_t[:, span], dscore).T
-        gq_ref[0, :, lanes] = normalized_pull(raw, gain_ref[...], query_scale, dquery).astype(
-            jnp.bfloat16
-        )
+        pulled = normalized_pull(raw, gain_ref[...], query_scale, dquery)
+        put(1, lanes, pulled.astype(jnp.bfloat16))
 
     @pl.when(block == pl.num_programs(0) - 1)
     def _():
@@ -473,14 +562,12 @@
     return call(
         values_kernel,
         [
-            shaped(q.shape),
-            shaped(q.shape),
+            shaped((2, 2, rows, 2 * HD)),
+            shaped((2, 2, rows, 2 * HD)),
             shaped((half, HD), jnp.float32),
             shaped((half, HD)),
         ],
         16,
-        2 * 2 * half * span * 4 * HD,
-        2 * half * span * 2 + 8 * half * HD * 2,
         grid_spec=pltpu.PrefetchScalarGridSpec(
             num_scalar_prefetch=1,
             grid=(blocks,),
@@ -491,7 +578,12 @@
                 pl.BlockSpec((1, 2, span, rows), lambda b, code: (b, 0, 0, 0)),
                 pl.BlockSpec((1, 8, rows), lambda b, code: (b, 0, 0)),
             ],
-            out_specs=[picked, picked, whole((half, HD)), whole((half, HD))],
+            out_specs=[
+                whole((2, 2, rows, 2 * HD)),
+                whole((2, 2, rows, 2 * HD)),
+                whole((half, HD)),
+                whole((half, HD)),
+            ],
             scratch_shapes=[
                 pltpu.VMEM((2 * half, HD), jnp.bfloat16),
                 pltpu.VMEM((HD, 2 * half), jnp.bfloat16),
@@ -538,8 +630,8 @@
         weight_grad_kernel,
         [shaped((width, features)), shaped((width, features))],
         12,
-        0,
-        0,
+        2 * 4 * rows * features * 2 * width,
+        4 * rows * features * 2 + 2 * width * features * 2,
         in_specs=[SMEM, VMEM, VMEM] + [HBM] * 4,
         out_specs=[VMEM, VMEM],
         scratch_shapes=[
@@ -551,48 +643,31 @@
     )(code, mine, theirs, *acts)
 
 
-def input_grad_kernel(code, *refs):
-    grads, key_w, value_w = refs[:4], refs[4:10], refs[10:16]
-    kept, sent, w_v, w_sem = refs[16:]
-    rows, features = kept.shape[1:]
-    width = grads[0].shape[1]
-
-    def weight_copies(act):
-        for part, weights in enumerate((key_w, value_w)):
-            for slot in range(2):
-                row = 2 * part + slot
-                slot_copies(
-                    code, code[1 + slot], weights, w_v.at[pl.ds(row * width, width)], w_sem.at[row], act
-                )
-
-    weight_copies(True)
-    weight_copies(False)
+def input_grad_kernel(piece, code, *refs):
+    grads, weights, out = refs[:8], refs[8:12], refs[12]
+    rows = out.shape[0]
+    span = pl.ds(pl.multiple_of((code[0] ^ piece) * rows, rows), rows)
+    total = 0.0
+    for k, weight in enumerate(weights):
+        grad = jnp.concatenate([ref[span, :] for ref in grads[2 * k : 2 * k + 2]], axis=1)
+        total = total + dot(grad, weight[...])
+    out[...] = total.astype(jnp.bfloat16)
+
+
+def input_grad(code, piece, grads, weights, rows):
+    width, features = weights[0].shape
     tile = features // 3
-    for j in (3, 1, 2, 0):
-        span = pl.ds(pl.multiple_of((code[0] ^ j) * rows, rows), rows)
-        grad = jnp.concatenate([ref[span, :] for ref in grads], axis=1)
-        target = sent if j % 2 else kept
-        for n in range(3):
-            lanes = slice(n * tile, (n + 1) * tile)
-            target[j // 2, :, lanes] = dot(grad, w_v[:, lanes]).astype(jnp.bfloat16)
-
-
-def input_grad(code, grads, key_weights, value_weights, rows):
-    width, features = key_weights[0].shape
-    return call(
-        input_grad_kernel,
-        [shaped((2, rows, features)), shaped((2, rows, features))],
+    return call(
+        functools.partial(input_grad_kernel, piece),
+        shaped((rows, features)),
         16,
-        2 * 4 * rows * features * 4 * width,
-        4 * rows * features * 2 + 4 * width * features * 2,
-        in_specs=[SMEM] + [VMEM] * 4 + [HBM] * 12,
-        out_specs=[VMEM, VMEM],
-        scratch_shapes=[
-            pltpu.VMEM((4 * width, features), jnp.bfloat16),
-            pltpu.SemaphoreType.DMA((4,)),
-        ],
+        grid=(3,),
+        in_specs=[SMEM]
+        + [pl.BlockSpec(grad.shape, lambda n: (0, 0)) for grad in grads]
+        + [pl.BlockSpec((width, tile), lambda n: (0, n))] * 4,
+        out_specs=pl.BlockSpec((rows, tile), lambda n: (0, n)),
         name="input_grad",
-    )(code, *grads, *key_weights, *value_weights)
+    )(code, *grads, *weights)
 
 
 def body_planes(normed, q_raw, key_weight, value_weight, q_gain, k_gain, segment_ids, grad_out):
@@ -609,7 +684,7 @@
     ]
     inner = (z == 1) | (z == 2)
     first_is_own = jnp.where(inner, c, 1 - c) == uly
-    code = jnp.stack([place % 4, *chosen, first_is_own]).astype(jnp.int32)
+    code = jnp.stack([place % 4, *chosen, first_is_own, c, x, c == z % 2]).astype(jnp.int32)
     gain_q = q_gain.reshape(1, HD)
 
     def picked(first_is_low, low, high):
@@ -664,7 +739,7 @@
     acts = (normed, normed_c, normed_x, normed_xc)
     k_third = after(k_third, v_second, v_outer)
     key_weights = (key_slab, k_one, k_inner, k_second, k_outer, k_third)
-    mine, theirs = project(code, acts, key_weights)
+    mine, theirs, key_w = project(code, acts, key_weights)
     key_far = swap_uly(theirs)
     from_x = after(from_x, theirs)
     arrays = [near[0], near[1], near[2], near[3], from_x[0], from_x[1], from_x[2], from_x[3]]
@@ -674,7 +749,7 @@
     kept = [picked(c == 0, arrays[2 * k], arrays[2 * k + 1]) for k in range(4)]
 
     value_weights = (value_slab, v_one, v_inner, v_second, v_outer, after(v_third, theirs))
-    value_mine, value_theirs = project(code, acts, value_weights)
+    value_mine, value_theirs, value_w = project(code, acts, value_weights)
     value_far = swap_uly(value_theirs)
     key_far = after(key_far, value_theirs)
     key_raw = mine.astype(jnp.float32) + key_far.astype(jnp.float32)
@@ -687,87 +762,68 @@
     go = jnp.stack([kept[1], from_core[1], kept[3], from_core[3]])
 
     keys_before = after(keys_before, values)
+    key_w_core, value_w_core = swap_core(key_w), swap_core(value_w)
     e, stat, dv_own, dv_before = attend_scores(
         code, q, go, keys, keys_before, key_mark, query_mark, gain_q
     )
     dv_back = along_z(dv_before, backward)
-    values_before = after(values_before, e)
-    out, gq, dk_own, dk_before = attend_values(
+    values_before = after(values_before, e, key_w_core, value_w_core)
+    near, sent_back, dk_own, dk_before = attend_values(
         code, q, go, keys, keys_before, values, values_before, gain_q, e, stat
     )
     dk_back = along_z(dk_before, backward)
     value_grad = (dv_own + after(dv_back, dk_own).astype(jnp.float32)).astype(jnp.bfloat16)
     value_grad_far = swap_uly(value_grad)
 
-    out, gq = after_all((out, gq), value_grad)
-    from_core = swap_core(jnp.stack([out[1], out[3], gq[1], gq[3]]))
-    own_pairs = ((out[0], from_core[0]), (gq[0], from_core[2]))
-    far_pairs = ((out[2], from_core[1]), (gq[2], from_core[3]))
-
-    def by_core(pairs):
-        return [picked((c == 0) == (k == 0), a, b) for a, b in pairs for k in (0, 1)]
-
-    back_payload = jnp.stack(by_core(far_pairs))
-    back_x = swap_x(back_payload)
-    own_heads = by_core(own_pairs)
-
-    dkey = dk_own + after(dk_back, back_payload).astype(jnp.float32)
+    near_other = swap_core(sent_back)
+    far = pack(near, near_other)
+    back_x = swap_x(far)
+
+    v_first, v_second = weight_grad(code, value_grad, after(value_grad_far, far), acts)
+    v_third, v_outer = along_z(v_second, BACK_THIRD), along_z(v_first, BACK_OUTER)
+    dkey = dk_own + after(dk_back, v_first).astype(jnp.float32)
     key_grad = normalized_pull(key_raw, k_gain, 1.0, dkey).astype(jnp.bfloat16)
     key_grad_far = swap_uly(key_grad)
-    value_grad_far = after(value_grad_far, key_grad)
-
-    v_first, v_second = weight_grad(code, value_grad, value_grad_far, acts)
-    v_third, v_outer = along_z(v_second, BACK_THIRD), along_z(v_first, BACK_OUTER)
-    key_grad_far = after(key_grad_far, v_first, back_x)
     grads = (key_grad, key_grad_far, value_grad, value_grad_far)
-    kept, sent = input_grad(code, grads, key_weights, value_weights, rows)
-    sent = swap_core(sent)
-    key_grad_far = after(key_grad_far, kept)
+    grads_core = tuple(swap_core(grad) for grad in grads)
     k_first, k_second = weight_grad(code, key_grad, key_grad_far, acts)
-    k_third, k_outer = along_z(k_second, BACK_THIRD), along_z(k_first, BACK_OUTER)
-    v_third, v_outer = after_all((v_third, v_outer), k_first)
-    v_mid_payload, v_inner_payload = v_first + v_third, v_second + v_outer
+    k_third = along_z(k_second, BACK_THIRD)
+    back_x = after(back_x, k_first)
+    grads = grads[:2] + after_all(grads_core[:2], back_x) + grads[2:] + grads_core[2:]
+    weights = (key_w, key_w_core, value_w, value_w_core)
+    away = input_grad(code, 2, grads, weights, rows)
+    from_x = swap_x(away)
+    v_third, v_outer = after_all((v_third, v_outer), away)
+    v_mid_payload, v_inner_payload = sums((v_first, v_third), (v_second, v_outer))
     v_mid, v_inner = along_z(v_mid_payload, BACK_MID), along_z(v_inner_payload, BACK_INNER)
-    sent = after(sent, v_mid_payload, v_inner_payload)
-    away = (kept[1].astype(jnp.float32) + sent[1].astype(jnp.float32)).astype(jnp.bfloat16)
-    from_x = swap_x(away)
-    own_sum = kept[0].astype(jnp.float32) + sent[0].astype(jnp.float32)
-    k_third, k_outer = after_all((k_third, k_outer), away)
-    k_mid_payload, k_inner_payload = k_first + k_third, k_second + k_outer
-    k_mid, k_inner = along_z(k_mid_payload, BACK_MID), along_z(k_inner_payload, BACK_INNER)
-    v_mid, v_inner, own_sum, back_x = after_all(
-        (v_mid, v_inner, own_sum, back_x), k_mid_payload, k_inner_payload
-    )
-    v_one_payload = v_first + v_mid
+    key_grad_far = after(key_grad_far, v_mid_payload)
+    kept = input_grad(code, 0, (key_grad, key_grad_far) + grads[2:], weights, rows)
+    k_third = after(k_third, kept)
+    (k_mid_payload,) = sums((k_first, k_third))
+    k_mid, k_outer = along_z(k_mid_payload, BACK_MID), along_z(after(k_first, k_third), BACK_OUTER)
+    v_mid, v_inner = after_all((v_mid, v_inner), k_mid_payload)
+    (v_one_payload,) = sums((v_first, v_mid))
     v_one = along_z(v_one_payload, BACK_ONE)
-    k_mid, k_inner = after_all((k_mid, k_inner), v_one_payload)
-    k_one_payload = k_first + k_mid
-    k_one = along_z(k_one_payload, BACK_ONE)
-
-    def by_x(own, far, k):
-        return [picked(x == 0, own[k], far[k]), picked(x == 0, far[k], own[k])]
-
-    attention, grad_q = (
-        jnp.concatenate(by_x(own_heads, back_x, k) + by_x(own_heads, back_x, k + 1), axis=1)
-        for k in (0, 2)
-    )
-    def halves(total):
-        own, away = (picked(c == k, total[:width], total[width:]) for k in (0, 1))
-        other = move(
-            away.astype(jnp.bfloat16),
-            [((z, x, z % 2), (z, x, 1 - z % 2)) for z in range(4) for x in (0, 1)],
+    attention, grad_q = by_head(code, near, near_other, after(back_x, v_one_payload, v_inner))
+    k_mid, k_outer = after_all((k_mid, k_outer), attention)
+    k_one_payload, k_inner_payload = sums((k_first, k_mid), (k_second, k_outer))
+    k_one, k_inner = along_z(k_one_payload, BACK_ONE), along_z(k_inner_payload, BACK_INNER)
+
+    def to_core(away):
+        return move(
+            away, [((z, x, z % 2), (z, x, 1 - z % 2)) for z in range(4) for x in (0, 1)]
         )
-        return own, other
-
-    def owned(own, other):
-        return jnp.where(c == z % 2, own, other.astype(jnp.float32)).T
-
-    v_one, from_x = after_all((v_one, from_x), k_one_payload)
-    value_sum, value_other = halves(summed((v_second, v_inner, v_one)))
-    grad_normed = (own_sum + from_x.astype(jnp.float32)).astype(jnp.bfloat16)
-    grad_value_weight = owned(value_sum, after(value_other, grad_normed))
-    k_one = after(k_one, grad_value_weight, grad_normed, attention, grad_q)
-    grad_key_weight = owned(*halves(summed((k_second, k_inner, k_one))))
+
+    from_x = after(from_x, k_inner_payload)
+    (grad_normed,) = sums((kept, from_x))
+    v_one = after(v_one, grad_normed)
+    value_own, value_away = halves(code, (v_second, v_inner, v_one))
+    value_other = to_core(value_away)
+    k_one, k_inner = after_all((k_one, k_inner), value_own)
+    key_own, key_away = halves(code, (k_second, k_inner, k_one))
+    key_other = to_core(key_away)
+    grad_value_weight = owned(code, value_own, after(value_other, key_own))
+    grad_key_weight = owned(code, key_own, after(key_other, grad_value_weight))
     return (attention, grad_normed, grad_q, grad_key_weight, grad_value_weight)
 
 

time: 206 us -> 182 us (0.88)
  other arithmetic: 28.1 us -> 4.34 us
  waiting for transfers between devices: 62.7 us -> 53.1 us
  Pallas kernels: 40.1 us -> 48.3 us
  starting transfers between devices: 66.3 us -> 71.3 us
  local copies, waits for them, and re-layouts: 5.18 us -> 2.06 us
    ppermute x37 -> x42, waiting for transfers between devices: 60.8 us -> 44.6 us  [move(): return lax.ppermute(array, 'seq', [(at(*a), at(*b)) for a, b in rule])]
    pallas_call x2 -> x14, Pallas kernels: 14.4 us -> 23.7 us  [the longest x1 8.78 us: attend_values(): call(values_kernel, [shaped((2, 2, rows, 2 * HD)), shaped((2, 2, rows, 2...]
    add x8 -> x0, other arithmetic: 9.02 us -> none  [the longest x2 2.79 us: body_planes(): k_mid_payload, k_inner_payload = (k_first + k_third, k_second + k_outer)]
    ppermute x4, waiting for transfers between devices: 1.91 us -> 8.57 us  [swap_uly(): return lax.ppermute(array, 'uly', [(0, 1), (1, 0)])]
    ppermute x37 -> x42, starting transfers between devices: 62.4 us -> 68.5 us  [move(): return lax.ppermute(array, 'seq', [(at(*a), at(*b)) for a, b in rule])]
    convert_element_type x4 -> x0, other arithmetic: 4.87 us -> none  [the longest x1 2.64 us: body_planes(): grad_normed = (own_sum + from_x.astype(jnp.float32)).astype(jnp.bfloat16)]
    unnamed x72 -> x16, local copies, waits for them, and re-layouts: 4.5 us -> 0.05 us
    select_n x5 -> x2, other arithmetic: 4.4 us -> 1.25 us  [picked(): return jnp.where(first_is_low, low, high)]
  transfers between devices with their start and end apart: 41 -> 46, of which waited for: 15 -> 19; matrix products, arithmetic and copies ran while one was open for 12% -> 3% of each run, Pallas kernels for 17% -> 26%
where the time goes in v3:
time: 182 us; the launch traced here: 180 us
  starting transfers between devices  71.3 us (39%)
  waiting for transfers between devices  53.1 us (29%)
  Pallas kernels  48.3 us (27%)
  other arithmetic  4.34 us (2%)
  local copies, waits for them, and re-layouts  2.06 us (1%)
    ppermute x42, starting transfers between devices, move(): return lax.ppermute(array, 'seq', [(at(*a), at(*b)) for a, b in rule])  68.5 us
    ppermute x42, waiting for transfers between devices, move(): return lax.ppermute(array, 'seq', [(at(*a), at(*b)) for a, b in rule])  44.6 us
    pallas_call x2, Pallas kernels, project(): call(project_kernel, [shaped((4 * rows, width)), shaped((4 * rows, width)...  9.44 us
    pallas_call x1, Pallas kernels, attend_values(): call(values_kernel, [shaped((2, 2, rows, 2 * HD)), shaped((2, 2, rows, 2...  8.78 us
    ppermute x4, waiting for transfers between devices, swap_uly(): return lax.ppermute(array, 'uly', [(0, 1), (1, 0)])  8.57 us
    pallas_call x1, Pallas kernels, attend_scores(): call(scores_kernel, [shaped((blocks, 2, span, rows)), shaped((blocks, 8,...  8.56 us
    pallas_call x2, Pallas kernels, weight_grad(): call(weight_grad_kernel, [shaped((width, features)), shaped((width, featu...  6.6 us
    pallas_call x2, Pallas kernels, input_grad(): call(functools.partial(input_grad_kernel, piece), shaped((rows, features)...  6.3 us
  transfers between devices with their start and end apart: 46, of which 19 were waited for; matrix products, arithmetic and copies ran while one was open for 3% of the time, Pallas kernels for 26%

profile of v3, /device:TPU:17, one launch (start us, length us, event | category | flops | bytes accessed | tf_op | source)
XLA Modules:
  0.0 180.5 jit_solution(15706950694127611306)
XLA Ops:
  0.6 2.6 %collective-permute-start.6 = (bf16[64,2688]{1,0:T(8,128)(2,1)}, bf16[64,2688]{1,0:T(8,128)(2,1)S(1)}, u32[]{:S(2)}, u32[]{:S(2)}) collective-permute-start(bf16[64,2688]{1,0:T(8,128)(2,1)} %bitcast.36), channel_id=1, source_target_pairs={{2,0},{6,4},{8,10},{12,14},{18,16},{22,20},{24,26},{28,30},{3,1},{... | collective-permute-start | bytes 1032200 | tf_op jit(solution)/shard_map/ppermute | solution.py:176
  12.7 6.7 %collective-permute-done.4.refs_6_ = bf16[128,2688]{1,0:T(8,128)(2,1)} collective-permute-done((bf16[128,2688]{1,0:T(8,128)(2,1)S(1)}, bf16[128,2688]{1,0:T(8,128)(2,1)}, u32[]{:S(2)}, u32[]{:S(2)}) %collective-permute-start.4) | collective-permute-done | bytes 688160 | tf_op jit(solution)/shard_map/ppermute | solution.py:176
  23.7 3.8 %collective-permute-done.8.refs_6_ = bf16[128,2688]{1,0:T(8,128)(2,1)} collective-permute-done((bf16[128,2688]{1,0:T(8,128)(2,1)S(1)}, bf16[128,2688]{1,0:T(8,128)(2,1)}, u32[]{:S(2)}, u32[]{:S(2)}) %collective-permute-start.8) | collective-permute-done | bytes 688160 | tf_op jit(solution)/shard_map/ppermute | solution.py:176
  28.2 8.2 %collective-permute-start.11 = (bf16[128,2688]{1,0:T(8,128)(2,1)}, bf16[128,2688]{1,0:T(8,128)(2,1)}, u32[]{:S(2)}, u32[]{:S(2)}) collective-permute-start(bf16[128,2688]{1,0:T(8,128)(2,1)} %collective-permute-done.7.refs_5_), channel_id=1, source_target_pairs={{8,16},{12,20},{18,10},{22,14},{9,17},{13,21},{19,11},{23,15}} | collective-permute-start | bytes 2064392 | tf_op jit(solution)/shard_map/ppermute | solution.py:176
  41.5 2.9 %collective-permute-start.10 = (bf16[256,2688]{1,0:T(8,128)(2,1)S(1)}, bf16[256,2688]{1,0:T(8,128)(2,1)S(1)}, u32[]{:S(2)}, u32[]{:S(2)}) collective-permute-start(bf16[256,2688]{1,0:T(8,128)(2,1)S(1)} %collective-permute-done.refs_2_.a2), channel_id=1, source_target_pairs={{0,2},{2,0},{4,6},{6,4},{8,10},{10,8},{12,14},{14,12},{16,18},{18,... | collective-permute-start | bytes 4128776 | tf_op jit(solution)/shard_map/ppermute | solution.py:176
  50.6 4.7 %project.2 = (bf16[1024,128]{1,0:T(8,128)(2,1)S(1)}, bf16[1024,128]{1,0:T(8,128)(2,1)S(1)}, bf16[256,2688]{1,0:T(8,128)(2,1)S(1)}) custom-call(s32[7]{0:T(128)S(1)} %stack.71.code, bf16[256,2688]{1,0:T(8,128)(2,1)S(1)} %copy-done, bf16[256,2688]{1,0:T(8,128)(2,1)S(1)} %collective-permute-done.9.refs_1_.a1, ...), custom_call_target="tpu_custom_call" | custom-call | tf_op jit(solution)/shard_map/project/pallas_call | solution.py:384
  56.7 3.9 %collective-permute-done.16 = bf16[4,256,256]{2,1,0:T(8,128)(2,1)S(1)} collective-permute-done((bf16[4,256,256]{2,1,0:T(8,128)(2,1)S(1)}, bf16[4,256,256]{2,1,0:T(8,128)(2,1)S(1)}, u32[]{:S(2)}, u32[]{:S(2)}) %collective-permute-start.16) | collective-permute-done | bytes 524320 | tf_op jit(solution)/shard_map/ppermute | solution.py:176
  60.5 4.7 %project.3 = (bf16[1024,128]{1,0:T(8,128)(2,1)S(1)}, bf16[1024,128]{1,0:T(8,128)(2,1)S(1)}, bf16[256,2688]{1,0:T(8,128)(2,1)S(1)}) custom-call(s32[7]{0:T(128)S(1)} %stack.71.code, bf16[256,2688]{1,0:T(8,128)(2,1)S(1)} %copy-done, bf16[256,2688]{1,0:T(8,128)(2,1)S(1)} %collective-permute-done.9.refs_1_.a1, ...), custom_call_target="tpu_custom_call" | custom-call | tf_op jit(solution)/shard_map/project/pallas_call | solution.py:384
  66.7 3.0 %collective-permute-start.17 = (bf16[4,256,256]{2,1,0:T(8,128)(2,1)S(1)}, bf16[4,256,256]{2,1,0:T(8,128)(2,1)S(1)}, u32[]{:S(2)}, u32[]{:S(2)}) collective-permute-start(bf16[4,256,256]{2,1,0:T(8,128)(2,1)S(1)} %pad_maximum_fusion.3), channel_id=1, source_target_pairs={{0,2},{2,0},{4,6},{6,4},{8,10},{10,8},{12,14},{14,12},{16,18},{18,... | collective-permute-start | bytes 1572872 | tf_op jit(solution)/shard_map/ppermute | solution.py:176
  74.8 5.6 %collective-permute-done.19.before_ref = bf16[1024,128]{1,0:T(8,128)(2,1)S(1)} collective-permute-done((bf16[1024,128]{1,0:T(8,128)(2,1)S(1)}, bf16[1024,128]{1,0:T(8,128)(2,1)S(1)}, u32[]{:S(2)}, u32[]{:S(2)}) %collective-permute-start.19) | collective-permute-done | bytes 262176 | tf_op jit(solution)/shard_map/ppermute | solution.py:176
  80.4 8.6 %attend_scores.1 = (bf16[4,2,1280,256]{3,2,1,0:T(8,128)(2,1)S(1)}, f32[4,8,256]{2,1,0:T(8,128)S(1)}, f32[1024,128]{1,0:T(8,128)S(1)}, bf16[1024,128]{1,0:T(8,128)(2,1)S(1)}) custom-call(s32[7]{0:T(128)S(1)} %stack.71.code, bf16[4,256,256]{2,1,0:T(8,128)(2,1)S(1)} %pad_maximum_fusion.4.q_ref, bf16[4,256,256]{2,1,0:T(8,128)(2,1)S(1)} %pad_maximum_fusion.5.go_ref, ...), custom_call_target="tpu_custom_call" | custom-call | tf_op jit(solution)/shard_map/attend_scores/pallas_call | solution.py:471
  89.0 2.6 %collective-permute-start.26 = (bf16[1024,128]{1,0:T(8,128)(2,1)S(1)}, bf16[1024,128]{1,0:T(8,128)(2,1)S(1)}, u32[]{:S(2)}, u32[]{:S(2)}) collective-permute-start(bf16[1024,128]{1,0:T(8,128)(2,1)S(1)} %get-tuple-element.106), channel_id=1, source_target_pairs={{8,0},{12,4},{10,2},{14,6},{16,8},{20,12},{18,10},{22,14},{24,16},... | collective-permute-start | bytes 786440 | tf_op jit(solution)/shard_map/ppermute | solution.py:176
  91.6 8.8 %attend_values.1 = (bf16[2,2,256,256]{3,2,1,0:T(8,128)(2,1)S(1)}, bf16[2,2,256,256]{3,2,1,0:T(8,128)(2,1)S(1)}, f32[1024,128]{1,0:T(8,128)S(1)}, bf16[1024,128]{1,0:T(8,128)(2,1)S(1)}) custom-call(s32[7]{0:T(128)S(1)} %stack.71.code, bf16[4,256,256]{2,1,0:T(8,128)(2,1)S(1)} %pad_maximum_fusion.4.q_ref, bf16[4,256,256]{2,1,0:T(8,128)(2,1)S(1)} %pad_maximum_fusion.5.go_ref, ...), custom_call_target="tpu_custom_call" | custom-call | tf_op jit(solution)/shard_map/attend_values/pallas_call | solution.py:562
  104.2 5.9 %collective-permute-done.27.theirs.refs_5_ = bf16[1024,128]{1,0:T(8,128)(2,1)S(1)} collective-permute-done((bf16[1024,128]{1,0:T(8,128)(2,1)S(1)}, bf16[1024,128]{1,0:T(8,128)(2,1)S(1)}, u32[]{:S(2)}, u32[]{:S(2)}) %collective-permute-start.27) | collective-permute-done | bytes 262176 | tf_op jit(solution)/shard_map/ppermute | solution.py:196
  110.1 3.3 %weight_grad.2 = (bf16[128,2688]{1,0:T(8,128)(2,1)S(1)}, bf16[128,2688]{1,0:T(8,128)(2,1)S(1)}) custom-call(s32[7]{0:T(128)S(1)} %stack.71.code, bf16[1024,128]{1,0:T(8,128)(2,1)S(1)} %add_convert_fusion.mine.refs_4_, bf16[1024,128]{1,0:T(8,128)(2,1)S(1)} %collective-permute-done.27.theirs.refs_5_, bf16[256,2688]{1,0:T(8,128)(2,1)S(1)} %copy-done, ...), custom_call_target="tpu_custom_call" | custom-call | flops 1409286144 | bytes 6881280 | tf_op jit(solution)/shard_map/weight_grad/pallas_call | solution.py:629
  118.5 2.6 %collective-permute-done.28.theirs.refs_1_ = bf16[1024,128]{1,0:T(8,128)(2,1)S(1)} collective-permute-done((bf16[1024,128]{1,0:T(8,128)(2,1)S(1)}, bf16[1024,128]{1,0:T(8,128)(2,1)S(1)}, u32[]{:S(2)}, u32[]{:S(2)}) %collective-permute-start.28) | collective-permute-done | bytes 262176 | tf_op jit(solution)/shard_map/ppermute | solution.py:196
  121.1 3.3 %weight_grad.3 = (bf16[128,2688]{1,0:T(8,128)(2,1)S(1)}, bf16[128,2688]{1,0:T(8,128)(2,1)S(1)}) custom-call(s32[7]{0:T(128)S(1)} %stack.71.code, bf16[1024,128]{1,0:T(8,128)(2,1)S(1)} %multiply_convert_fusion.mine.refs_0_, bf16[1024,128]{1,0:T(8,128)(2,1)S(1)} %collective-permute-done.28.theirs.refs_1_, bf16[256,2688]{1,0:T(8,128)(2,1)S(1)} %copy-done, ...), custom_call_target="tpu_custom_call" | custom-call | flops 1409286144 | bytes 6881280 | tf_op jit(solution)/shard_map/weight_grad/pallas_call | solution.py:629
  130.2 3.1 %input_grad.2 = bf16[256,2688]{1,0:T(8,128)(2,1)S(1)} custom-call(s32[7]{0:T(128)S(1)} %stack.71.code, bf16[1024,128]{1,0:T(8,128)(2,1)S(1)} %multiply_convert_fusion.mine.refs_0_, bf16[1024,128]{1,0:T(8,128)(2,1)S(1)} %collective-permute-done.28.theirs.refs_1_, bf16[1024,128]{1,0:T(8,128)(2,1)S(1)} %collective-permute-done.31.refs_2_, ...), custom_call_target="tpu_custom_call" | custom-call | tf_op jit(solution)/shard_map/input_grad/pallas_call | solution.py:660
  134.9 3.4 %collective-permute-start.36 = (bf16[128,2688]{1,0:T(8,128)(2,1)S(1)}, bf16[128,2688]{1,0:T(8,128)(2,1)S(1)}, u32[]{:S(2)}, u32[]{:S(2)}) collective-permute-start(bf16[128,2688]{1,0:T(8,128)(2,1)S(1)} %get-tuple-element.119), channel_id=1, source_target_pairs={{18,10},{22,14},{8,16},{12,20},{19,11},{23,15},{9,17},{13,21}} | collective-permute-start | bytes 2064392 | tf_op jit(solution)/shard_map/ppermute | solution.py:176
  139.6 3.2 %input_grad.3.refs_0_ = bf16[256,2688]{1,0:T(8,128)(2,1)S(1)} custom-call(s32[7]{0:T(128)S(1)} %stack.71.code, bf16[1024,128]{1,0:T(8,128)(2,1)S(1)} %multiply_convert_fusion.mine.refs_0_, bf16[1024,128]{1,0:T(8,128)(2,1)S(1)} %collective-permute-done.28.theirs.refs_1_, bf16[1024,128]{1,0:T(8,128)(2,1)S(1)} %collective-permute-done.31.refs_2_, ...), custom_call_target="tpu_custom_call" | custom-call | tf_op jit(solution)/shard_map/input_grad/pallas_call | solution.py:660
  145.6 3.5 %collective-permute-done.36.b = bf16[128,2688]{1,0:T(8,128)(2,1)S(1)} collective-permute-done((bf16[128,2688]{1,0:T(8,128)(2,1)S(1)}, bf16[128,2688]{1,0:T(8,128)(2,1)S(1)}, u32[]{:S(2)}, u32[]{:S(2)}) %collective-permute-start.36) | collective-permute-done | bytes 688160 | tf_op jit(solution)/shard_map/ppermute | solution.py:176
  149.1 7.2 %collective-permute-done.35.refs_1_ = bf16[128,2688]{1,0:T(8,128)(2,1)S(1)} collective-permute-done((bf16[128,2688]{1,0:T(8,128)(2,1)S(1)}, bf16[128,2688]{1,0:T(8,128)(2,1)S(1)}, u32[]{:S(2)}, u32[]{:S(2)}) %collective-permute-start.35) | collective-permute-done | bytes 688160 | tf_op jit(solution)/shard_map/ppermute | solution.py:176
  159.5 4.2 %collective-permute-done.39.refs_1_ = bf16[128,2688]{1,0:T(8,128)(2,1)S(1)} collective-permute-done((bf16[128,2688]{1,0:T(8,128)(2,1)S(1)}, bf16[128,2688]{1,0:T(8,128)(2,1)S(1)}, u32[]{:S(2)}, u32[]{:S(2)}) %collective-permute-start.39) | collective-permute-done | bytes 688160 | tf_op jit(solution)/shard_map/ppermute | solution.py:176
  170.3 2.9 %collective-permute-done.41.c = bf16[128,2688]{1,0:T(8,128)(2,1)S(1)} collective-permute-done((bf16[128,2688]{1,0:T(8,128)(2,1)S(1)}, bf16[128,2688]{1,0:T(8,128)(2,1)S(1)}, u32[]{:S(2)}, u32[]{:S(2)}) %collective-permute-start.41) | collective-permute-done | bytes 688160 | tf_op jit(solution)/shard_map/ppermute | solution.py:176
  (129 shorter events, 70.4 us)
Async XLA Ops:
  4.6 36.9 %collective-permute-start = (bf16[256,2688]{1,0:T(8,128)(2,1)}, bf16[256,2688]{1,0:T(8,128)(2,1)S(1)}, u32[]{:S(2)}, u32[]{:S(2)}) collective-permute-start(bf16[256,2688]{1,0:T(8,128)(2,1)} %a0.3), channel_id=1, source_target_pairs={{0,4},{2,6},{4,0},{6,2},{8,12},{10,14},{12,8},{14,10},{16,20},{18,... | collective-permute-start | bytes 4128776 | tf_op jit(solution)/shard_map/ppermute | solution.py:176
  7.3 12.1 %collective-permute-start.4 = (bf16[128,2688]{1,0:T(8,128)(2,1)S(1)}, bf16[128,2688]{1,0:T(8,128)(2,1)}, u32[]{:S(2)}, u32[]{:S(2)}) collective-permute-start(bf16[128,2688]{1,0:T(8,128)(2,1)S(1)} %pad_maximum_fusion.refs_4_), channel_id=1, source_target_pairs={{10,18},{14,22},{16,8},{20,12},{11,19},{15,23},{17,9},{21,13}} | collective-permute-start | bytes 2064392 | tf_op jit(solution)/shard_map/ppermute | solution.py:176
  8.8 12.8 %collective-permute-start.2 = (bf16[128,2688]{1,0:T(8,128)(2,1)S(1)}, bf16[128,2688]{1,0:T(8,128)(2,1)}, u32[]{:S(2)}, u32[]{:S(2)}) collective-permute-start(bf16[128,2688]{1,0:T(8,128)(2,1)S(1)} %pad_maximum_fusion.refs_4_), channel_id=1, source_target_pairs={{0,8},{4,12},{26,18},{30,22},{10,2},{14,6},{16,24},{20,28},{1,9},{... | collective-permute-start | bytes 2064392 | tf_op jit(solution)/shard_map/ppermute | solution.py:176
  10.1 17.4 %collective-permute-start.8 = (bf16[128,2688]{1,0:T(8,128)(2,1)S(1)}, bf16[128,2688]{1,0:T(8,128)(2,1)}, u32[]{:S(2)}, u32[]{:S(2)}) collective-permute-start(bf16[128,2688]{1,0:T(8,128)(2,1)S(1)} %pad_maximum_fusion.1.refs_4_), channel_id=1, source_target_pairs={{10,18},{14,22},{16,8},{20,12},{11,19},{15,23},{17,9},{21,13}} | collective-permute-start | bytes 2064392 | tf_op jit(solution)/shard_map/ppermute | solution.py:176
  11.4 16.8 %collective-permute-start.7 = (bf16[128,2688]{1,0:T(8,128)(2,1)S(1)}, bf16[128,2688]{1,0:T(8,128)(2,1)}, u32[]{:S(2)}, u32[]{:S(2)}) collective-permute-start(bf16[128,2688]{1,0:T(8,128)(2,1)S(1)} %pad_maximum_fusion.1.refs_4_), channel_id=1, source_target_pairs={{0,8},{4,12},{26,18},{30,22},{10,2},{14,6},{16,24},{20,28},{1,9},{... | collective-permute-start | bytes 2064392 | tf_op jit(solution)/shard_map/ppermute | solution.py:176
  19.4 21.1 %collective-permute-start.5 = (bf16[128,2688]{1,0:T(8,128)(2,1)}, bf16[128,2688]{1,0:T(8,128)(2,1)}, u32[]{:S(2)}, u32[]{:S(2)}) collective-permute-start(bf16[128,2688]{1,0:T(8,128)(2,1)} %collective-permute-done.4.refs_6_), channel_id=1, source_target_pairs={{8,0},{12,4},{18,26},{22,30},{9,1},{13,5},{19,27},{23,31}} | collective-permute-start | bytes 2064392 | tf_op jit(solution)/shard_map/ppermute | solution.py:176
  21.6 19.0 %collective-permute-start.3 = (bf16[128,2688]{1,0:T(8,128)(2,1)}, bf16[128,2688]{1,0:T(8,128)(2,1)}, u32[]{:S(2)}, u32[]{:S(2)}) collective-permute-start(bf16[128,2688]{1,0:T(8,128)(2,1)} %collective-permute-done.2.refs_5_), channel_id=1, source_target_pairs={{8,16},{12,20},{18,10},{22,14},{9,17},{13,21},{19,11},{23,15}} | collective-permute-start | bytes 2064392 | tf_op jit(solution)/shard_map/ppermute | solution.py:176
  28.2 16.2 %collective-permute-start.11 = (bf16[128,2688]{1,0:T(8,128)(2,1)}, bf16[128,2688]{1,0:T(8,128)(2,1)}, u32[]{:S(2)}, u32[]{:S(2)}) collective-permute-start(bf16[128,2688]{1,0:T(8,128)(2,1)} %collective-permute-done.7.refs_5_), channel_id=1, source_target_pairs={{8,16},{12,20},{18,10},{22,14},{9,17},{13,21},{19,11},{23,15}} | collective-permute-start | bytes 2064392 | tf_op jit(solution)/shard_map/ppermute | solution.py:176
  46.4 14.1 %collective-permute-start.13 = (bf16[128,2688]{1,0:T(8,128)(2,1)}, bf16[128,2688]{1,0:T(8,128)(2,1)S(1)}, u32[]{:S(2)}, u32[]{:S(2)}) collective-permute-start(bf16[128,2688]{1,0:T(8,128)(2,1)} %collective-permute-done.11.refs_7_), channel_id=1, source_target_pairs={{16,24},{20,28},{10,2},{14,6},{17,25},{21,29},{11,3},{15,7}} | collective-permute-start | bytes 2064392 | tf_op jit(solution)/shard_map/ppermute | solution.py:176
  48.5 12.0 %collective-permute-start.16 = (bf16[4,256,256]{2,1,0:T(8,128)(2,1)S(1)}, bf16[4,256,256]{2,1,0:T(8,128)(2,1)S(1)}, u32[]{:S(2)}, u32[]{:S(2)}) collective-permute-start(bf16[4,256,256]{2,1,0:T(8,128)(2,1)S(1)} %pad_maximum_fusion.2), channel_id=1, source_target_pairs={{0,4},{2,6},{4,0},{6,2},{8,12},{10,14},{12,8},{14,10},{16,20},{18,... | collective-permute-start | bytes 1572872 | tf_op jit(solution)/shard_map/ppermute | solution.py:176
  55.4 14.8 %collective-permute-start.18 = (bf16[1024,128]{1,0:T(8,128)(2,1)S(1)}, bf16[1024,128]{1,0:T(8,128)(2,1)S(1)}, u32[]{:S(2)}, u32[]{:S(2)}) collective-permute-start(bf16[1024,128]{1,0:T(8,128)(2,1)S(1)} %get-tuple-element.84), channel_id=1, source_target_pairs={{0,1},{1,0},{2,3},{3,2},{4,5},{5,4},{6,7},{7,6},{8,9},{9,8},{10,11... | collective-permute-start | bytes 786440 | tf_op jit(solution)/shard_map/ppermute | solution.py:196
  69.7 21.9 %collective-permute-start.22 = (bf16[256,2688]{1,0:T(8,128)(2,1)S(1)}, bf16[256,2688]{1,0:T(8,128)(2,1)S(1)}, u32[]{:S(2)}, u32[]{:S(2)}) collective-permute-start(bf16[256,2688]{1,0:T(8,128)(2,1)S(1)} %get-tuple-element.98.refs_10_), channel_id=1, source_target_pairs={{0,2},{2,0},{4,6},{6,4},{8,10},{10,8},{12,14},{14,12},{16,18},{18,... | collective-permute-start | bytes 4128776 | tf_op jit(solution)/shard_map/ppermute | solution.py:176
  69.8 21.9 %collective-permute-start.21 = (bf16[256,2688]{1,0:T(8,128)(2,1)S(1)}, bf16[256,2688]{1,0:T(8,128)(2,1)S(1)}, u32[]{:S(2)}, u32[]{:S(2)}) collective-permute-start(bf16[256,2688]{1,0:T(8,128)(2,1)S(1)} %get-tuple-element.97.refs_8_), channel_id=1, source_target_pairs={{0,2},{2,0},{4,6},{6,4},{8,10},{10,8},{12,14},{14,12},{16,18},{18,... | collective-permute-start | bytes 4128776 | tf_op jit(solution)/shard_map/ppermute | solution.py:176
  72.7 18.9 %collective-permute-start.20 = (bf16[1024,128]{1,0:T(8,128)(2,1)S(1)}, bf16[1024,128]{1,0:T(8,128)(2,1)S(1)}, u32[]{:S(2)}, u32[]{:S(2)}) collective-permute-start(bf16[1024,128]{1,0:T(8,128)(2,1)S(1)} %add_convert_fusion.1.v_own), channel_id=1, source_target_pairs={{0,8},{4,12},{2,10},{6,14},{8,16},{12,20},{10,18},{14,22},{16,24},... | collective-permute-start | bytes 786440 | tf_op jit(solution)/shard_map/ppermute | solution.py:176
  89.0 13.1 %collective-permute-start.26 = (bf16[1024,128]{1,0:T(8,128)(2,1)S(1)}, bf16[1024,128]{1,0:T(8,128)(2,1)S(1)}, u32[]{:S(2)}, u32[]{:S(2)}) collective-permute-start(bf16[1024,128]{1,0:T(8,128)(2,1)S(1)} %get-tuple-element.106), channel_id=1, source_target_pairs={{8,0},{12,4},{10,2},{14,6},{16,8},{20,12},{18,10},{22,14},{24,16},... | collective-permute-start | bytes 786440 | tf_op jit(solution)/shard_map/ppermute | solution.py:176
  114.2 13.3 %collective-permute-start.24 = (bf16[2,2,256,256]{3,2,1,0:T(8,128)(2,1)S(1)}, bf16[2,2,256,256]{3,2,1,0:T(8,128)(2,1)S(1)}, u32[]{:S(2)}, u32[]{:S(2)}) collective-permute-start(bf16[2,2,256,256]{3,2,1,0:T(8,128)(2,1)S(1)} %pack.1), channel_id=1, source_target_pairs={{0,4},{2,6},{4,0},{6,2},{8,12},{10,14},{12,8},{14,10},{16,20},{18,... | collective-permute-start | bytes 1572872 | tf_op jit(solution)/shard_map/ppermute | solution.py:176
  116.5 18.1 %collective-permute-start.30 = (bf16[128,2688]{1,0:T(8,128)(2,1)S(1)}, bf16[128,2688]{1,0:T(8,128)(2,1)S(1)}, u32[]{:S(2)}, u32[]{:S(2)}) collective-permute-start(bf16[128,2688]{1,0:T(8,128)(2,1)S(1)} %get-tuple-element.109.refs_0_), channel_id=1, source_target_pairs={{0,8},{4,12},{26,18},{30,22},{1,9},{5,13},{27,19},{31,23}} | collective-permute-start | bytes 2064392 | tf_op jit(solution)/shard_map/ppermute | solution.py:176
  117.8 16.6 %collective-permute-start.29 = (bf16[128,2688]{1,0:T(8,128)(2,1)S(1)}, bf16[128,2688]{1,0:T(8,128)(2,1)S(1)}, u32[]{:S(2)}, u32[]{:S(2)}) collective-permute-start(bf16[128,2688]{1,0:T(8,128)(2,1)S(1)} %get-tuple-element.113.refs_2_.a), channel_id=1, source_target_pairs={{24,16},{28,20},{2,10},{6,14},{25,17},{29,21},{3,11},{7,15}} | collective-permute-start | bytes 2064392 | tf_op jit(solution)/shard_map/ppermute | solution.py:176
  124.4 18.3 %collective-permute-start.37 = (bf16[128,2688]{1,0:T(8,128)(2,1)S(1)}, bf16[128,2688]{1,0:T(8,128)(2,1)S(1)}, u32[]{:S(2)}, u32[]{:S(2)}) collective-permute-start(bf16[128,2688]{1,0:T(8,128)(2,1)S(1)} %get-tuple-element.120.refs_2_.a), channel_id=1, source_target_pairs={{24,16},{28,20},{2,10},{6,14},{25,17},{29,21},{3,11},{7,15}} | collective-permute-start | bytes 2064392 | tf_op jit(solution)/shard_map/ppermute | solution.py:176
  133.4 33.4 %collective-permute-start.38 = (bf16[256,2688]{1,0:T(8,128)(2,1)S(1)}, bf16[256,2688]{1,0:T(8,128)(2,1)S(1)}, u32[]{:S(2)}, u32[]{:S(2)}) collective-permute-start(bf16[256,2688]{1,0:T(8,128)(2,1)S(1)} %input_grad.2), channel_id=1, source_target_pairs={{0,4},{2,6},{4,0},{6,2},{8,12},{10,14},{12,8},{14,10},{16,20},{18,... | collective-permute-start | bytes 4128776 | tf_op jit(solution)/shard_map/ppermute | solution.py:176
  134.9 14.2 %collective-permute-start.36 = (bf16[128,2688]{1,0:T(8,128)(2,1)S(1)}, bf16[128,2688]{1,0:T(8,128)(2,1)S(1)}, u32[]{:S(2)}, u32[]{:S(2)}) collective-permute-start(bf16[128,2688]{1,0:T(8,128)(2,1)S(1)} %get-tuple-element.119), channel_id=1, source_target_pairs={{18,10},{22,14},{8,16},{12,20},{19,11},{23,15},{9,17},{13,21}} | collective-permute-start | bytes 2064392 | tf_op jit(solution)/shard_map/ppermute | solution.py:176
  138.3 18.0 %collective-permute-start.35 = (bf16[128,2688]{1,0:T(8,128)(2,1)S(1)}, bf16[128,2688]{1,0:T(8,128)(2,1)S(1)}, u32[]{:S(2)}, u32[]{:S(2)}) collective-permute-start(bf16[128,2688]{1,0:T(8,128)(2,1)S(1)} %get-tuple-element.118), channel_id=1, source_target_pairs={{16,8},{20,12},{10,18},{14,22},{17,9},{21,13},{11,19},{15,23}} | collective-permute-start | bytes 2064392 | tf_op jit(solution)/shard_map/ppermute | solution.py:176
  143.0 20.8 %collective-permute-start.39 = (bf16[128,2688]{1,0:T(8,128)(2,1)S(1)}, bf16[128,2688]{1,0:T(8,128)(2,1)S(1)}, u32[]{:S(2)}, u32[]{:S(2)}) collective-permute-start(bf16[128,2688]{1,0:T(8,128)(2,1)S(1)} %sums.6), channel_id=1, source_target_pairs={{16,8},{20,12},{10,18},{14,22},{17,9},{21,13},{11,19},{15,23}} | collective-permute-start | bytes 2064392 | tf_op jit(solution)/shard_map/ppermute | solution.py:176
  144.3 19.5 %collective-permute-start.40 = (bf16[128,2688]{1,0:T(8,128)(2,1)S(1)}, bf16[128,2688]{1,0:T(8,128)(2,1)S(1)}, u32[]{:S(2)}, u32[]{:S(2)}) collective-permute-start(bf16[128,2688]{1,0:T(8,128)(2,1)S(1)} %get-tuple-element.127.refs_0_), channel_id=1, source_target_pairs={{0,8},{4,12},{26,18},{30,22},{1,9},{5,13},{27,19},{31,23}} | collective-permute-start | bytes 2064392 | tf_op jit(solution)/shard_map/ppermute | solution.py:176
  (30 other events, 307.1 us)

commit v4 on v3

--- a/solution.py
+++ b/solution.py
@@ -334,48 +334,24 @@
 
 
 def project_kernel(code, *refs):
-    acts, weights = refs[:4], refs[4:-6]
-    mine, theirs, w_v, acts_v, acts_sem, w_sem = refs[-6:]
+    acts, weights = refs[:4], refs[4:-4]
+    mine, theirs, w_v, w_sem = refs[-4:]
     width = mine.shape[1]
-    rows, features = acts[0].shape
-    place = code[0]
+    rows = acts[0].shape[0]
 
     def weight_copies(act):
         for slot in range(2):
             slot_copies(
-                code,
-                code[1 + slot],
-                weights,
-                w_v.at[pl.ds(slot * width, width)],
-                w_sem.at[slot],
-                act,
+                code, code[1 + slot], weights, w_v.at[pl.ds(slot * width, width)], w_sem.at[slot], act
             )
 
     weight_copies(True)
-    tile = features // 3
-    copies = []
-    for n in range(3):
-        lanes = pl.ds(n * tile, tile)
-        for j in range(4):
-            to = pl.ds(pl.multiple_of((place ^ j) * rows, rows), rows)
-            copies.append(
-                pltpu.make_async_copy(
-                    acts[j].at[:, lanes], acts_v.at[to, lanes], acts_sem.at[4 * n + j]
-                )
-            )
-    for copy in copies:
-        copy.start()
     weight_copies(False)
-    both = 0.0
-    for n in range(3):
-        lanes = slice(n * tile, (n + 1) * tile)
-        for copy in copies[4 * n : 4 * n + 4]:
-            copy.wait()
-        both = both + lax.dot_general(
-            acts_v[:, lanes], w_v[:, lanes], NT, preferred_element_type=jnp.float32
-        )
-    mine[...] = both[:, :width].astype(jnp.bfloat16)
-    theirs[...] = both[:, width:].astype(jnp.bfloat16)
+    for j in range(4):
+        here = pl.ds(pl.multiple_of((code[0] ^ j) * rows, rows), rows)
+        both = lax.dot_general(acts[j][...], w_v[...], NT, preferred_element_type=jnp.float32)
+        mine[here, :] = both[:, :width].astype(jnp.bfloat16)
+        theirs[here, :] = both[:, width:].astype(jnp.bfloat16)
 
 
 def project(code, acts, weights):
@@ -385,11 +361,9 @@
         project_kernel,
         [shaped((4 * rows, width)), shaped((4 * rows, width)), shaped((2 * width, features))],
         12,
-        in_specs=[SMEM] + [HBM] * (4 + len(weights)),
+        in_specs=[SMEM] + [VMEM] * 4 + [HBM] * len(weights),
         out_specs=[VMEM, VMEM, VMEM],
         scratch_shapes=[
-            pltpu.VMEM((4 * rows, features), jnp.bfloat16),
-            pltpu.SemaphoreType.DMA((12,)),
             pltpu.SemaphoreType.DMA((2,)),
         ],
         name="project",
@@ -418,7 +392,7 @@
 ):
     block = pl.program_id(0)
     rows = q_ref.shape[1]
-    chunks = e_ref.shape[2] // rows
+    chunks = e_ref.shape[1] // rows
     half = own_ref.shape[0]
 
     @pl.when(block == 0)
@@ -428,30 +402,34 @@
         keys_v[:, HD:] = key_mark[...]
         acc[...] = jnp.zeros_like(acc)
 
-    key_at = lax.broadcasted_iota(jnp.int32, (rows, rows), 0)
-    query_at = lax.broadcasted_iota(jnp.int32, (rows, rows), 1)
-    behind = key_at <= query_at
-    stats = []
+    key_at = lax.broadcasted_iota(jnp.int32, (rows, 2 * rows), 0)
+    query_at = lax.broadcasted_iota(jnp.int32, (rows, 2 * rows), 1)
+    behind = key_at <= jnp.where(query_at >= rows, query_at - rows, query_at)
+    heads, grads = [], []
     for g in range(2):
         lanes = slice(g * HD, (g + 1) * HD)
         query = normalized(q_ref[0, :, lanes].astype(jnp.float32), gain_ref[...], query_scale)
-        query_t = jnp.concatenate([query.T.astype(jnp.bfloat16), query_mark[...]], axis=0)
-        total = jnp.zeros((1, rows), jnp.float32)
-        for c in range(chunks):
-            begin = pl.multiple_of((block + c) * rows, rows)
-            e = jnp.exp(dot(keys_v[pl.ds(begin, rows), :], query_t))
-            if c == 0:
-                e = jnp.where(behind, 0.0, e)
-            if c == chunks - 1:
-                e = jnp.where(behind, e, 0.0)
-            total = total + jnp.sum(e, axis=0, keepdims=True)
-            e_ref[0, g, c * rows : (c + 1) * rows, :] = e.astype(jnp.bfloat16)
-        inverse = 1.0 / total
-        stats.append(inverse)
-        grad = (go_ref[0, :, lanes].astype(jnp.float32).T * inverse).T.astype(jnp.bfloat16)
-        span = pl.ds(pl.multiple_of(block * rows, rows), chunks * rows)
-        acc[span, :] = acc[span, :] + dot(e_ref[0, g], grad)
-    stat_ref[0] = jnp.concatenate(stats + [jnp.zeros((6, rows), jnp.float32)], axis=0)
+        heads.append(jnp.concatenate([query.T.astype(jnp.bfloat16), query_mark[...]], axis=0))
+        grads.append(go_ref[0, :, lanes].astype(jnp.float32).T)
+    query_t = jnp.concatenate(heads, axis=1)
+    total = jnp.zeros((1, 2 * rows), jnp.float32)
+    es = []
+    for c in range(chunks):
+        begin = pl.multiple_of((block + c) * rows, rows)
+        e = jnp.exp(dot(keys_v[pl.ds(begin, rows), :], query_t))
+        if c == 0:
+            e = jnp.where(behind, 0.0, e)
+        if c == chunks - 1:
+            e = jnp.where(behind, e, 0.0)
+        total = total + jnp.sum(e, axis=0, keepdims=True)
+        es.append(e.astype(jnp.bfloat16))
+        e_ref[0, c * rows : (c + 1) * rows, :] = es[-1]
+    inverse = 1.0 / total
+    stat_ref[0] = jnp.broadcast_to(inverse, stat_ref.shape[1:])
+    grad = (jnp.concatenate(grads, axis=1) * inverse).T.astype(jnp.bfloat16)
+    for c in range(chunks):
+        span = pl.ds(pl.multiple_of((block + c) * rows, rows), rows)
+        acc[span, :] = acc[span, :] + dot(es[c], grad)
 
     @pl.when(block == pl.num_programs(0) - 1)
     def _():
@@ -471,8 +449,8 @@
     return call(
         scores_kernel,
         [
-            shaped((blocks, 2, span, rows)),
-            shaped((blocks, 8, rows), jnp.float32),
+            shaped((blocks, span, 2 * rows)),
+            shaped((blocks, 8, 2 * rows), jnp.float32),
             shaped((half, HD), jnp.float32),
             shaped((half, HD)),
         ],
@@ -490,8 +468,8 @@
                 whole((1, HD)),
             ],
             out_specs=[
-                pl.BlockSpec((1, 2, span, rows), lambda b, code: (b, 0, 0, 0)),
-                pl.BlockSpec((1, 8, rows), lambda b, code: (b, 0, 0)),
+                pl.BlockSpec((1, span, 2 * rows), lambda b, code: (b, 0, 0)),
+                pl.BlockSpec((1, 8, 2 * rows), lambda b, code: (b, 0, 0)),
                 whole((half, HD)),
                 whole((half, HD)),
             ],
@@ -510,7 +488,7 @@
 ):
     block = pl.program_id(0)
     rows = q_ref.shape[1]
-    span_rows = e_ref.shape[2]
+    span_rows = e_ref.shape[1]
     half = own_ref.shape[0]
 
     @pl.when(block == 0)
@@ -531,21 +509,31 @@
             at_piece[...] = jnp.where(here, result, at_piece[...])
 
     span = pl.ds(pl.multiple_of(block * rows, rows), span_rows)
+    raws = [q_ref[0, :, g * HD : (g + 1) * HD].astype(jnp.float32) for g in range(2)]
+    queries = jnp.concatenate(
+        [normalized(raw, gain_ref[...], query_scale).astype(jnp.bfloat16) for raw in raws], axis=0
+    )
+    grad_t = jnp.concatenate(
+        [go_ref[0, :, g * HD : (g + 1) * HD].astype(jnp.float32).T for g in range(2)], axis=1
+    )
+    inverse = stat_ref[0, :1, :]
+    e = e_ref[0]
+    out_t = dot(values_t[:, span], e) * inverse
+    along = jnp.sum(out_t * grad_t, axis=0, keepdims=True) * inverse
+    scaled = (grad_t * inverse).astype(jnp.bfloat16)
+    parts = []
+    for c in range(span_rows // rows):
+        here = pl.ds(pl.multiple_of((block + c) * rows, rows), rows)
+        dprob = dot(values_v[here, :], scaled)
+        dscore = e[c * rows : (c + 1) * rows] * (dprob - along).astype(jnp.bfloat16)
+        acc[here, :] = acc[here, :] + dot(dscore, queries)
+        parts.append(dscore)
+    dquery_t = dot(keys_t[:, span], jnp.concatenate(parts, axis=0))
     for g in range(2):
         lanes = slice(g * HD, (g + 1) * HD)
-        raw = q_ref[0, :, lanes].astype(jnp.float32)
-        query = normalized(raw, gain_ref[...], query_scale).astype(jnp.bfloat16)
-        inverse = stat_ref[0, g : g + 1, :]
-        e = e_ref[0, g]
-        out_t = dot(values_t[:, span], e) * inverse
-        put(0, lanes, out_t.T.astype(jnp.bfloat16))
-        grad_t = go_ref[0, :, lanes].astype(jnp.float32).T
-        along = jnp.sum(out_t * grad_t, axis=0, keepdims=True) * inverse
-        dprob = dot(values_v[span, :], (grad_t * inverse).astype(jnp.bfloat16))
-        dscore = (e.astype(jnp.float32) * (dprob - along)).astype(jnp.bfloat16)
-        acc[span, :] = acc[span, :] + dot(dscore, query)
-        dquery = dot(keys_t[:, span], dscore).T
-        pulled = normalized_pull(raw, gain_ref[...], query_scale, dquery)
+        across = slice(g * rows, (g + 1) * rows)
+        put(0, lanes, out_t[:, across].T.astype(jnp.bfloat16))
+        pulled = normalized_pull(raws[g], gain_ref[...], query_scale, dquery_t[:, across].T)
         put(1, lanes, pulled.astype(jnp.bfloat16))
 
     @pl.when(block == pl.num_programs(0) - 1)
@@ -575,8 +563,8 @@
             + [whole((half, HD))] * 4
             + [
                 whole((1, HD)),
-                pl.BlockSpec((1, 2, span, rows), lambda b, code: (b, 0, 0, 0)),
-                pl.BlockSpec((1, 8, rows), lambda b, code: (b, 0, 0)),
+                pl.BlockSpec((1, span, 2 * rows), lambda b, code: (b, 0, 0)),
+                pl.BlockSpec((1, 8, 2 * rows), lambda b, code: (b, 0, 0)),
             ],
             out_specs=[
                 whole((2, 2, rows, 2 * HD)),
@@ -595,30 +583,24 @@
     )(code, q, go, keys, keys_before, values, values_before, gain, e, stat)
 
 
-def weight_grad_kernel(code, mine, theirs, a0, a1, a2, a3, far, mid, acts_v, grad_v, acts_sem):
+def weight_grad_kernel(code, mine, theirs, a0, a1, a2, a3, far, mid):
     acts = (a0, a1, a2, a3)
     rows, features = a0.shape
     width = far.shape[0]
-    copies = [
-        pltpu.make_async_copy(acts[j], acts_v.at[j], acts_sem.at[j]) for j in range(4)
-    ]
-    for copy in copies:
-        copy.start()
     first = code[3] == 1
+    grads = []
     for j in range(4):
         span = pl.ds(pl.multiple_of((code[0] ^ j) * rows, rows), rows)
         own = mine[span, :].astype(jnp.float32).T
         other = theirs[span, :].astype(jnp.float32).T
-        grad_v[j, :width, :] = jnp.where(first, own, other).astype(jnp.bfloat16)
-        grad_v[j, width:, :] = jnp.where(first, other, own).astype(jnp.bfloat16)
-    for copy in copies:
-        copy.wait()
+        both = (jnp.where(first, own, other), jnp.where(first, other, own))
+        grads.append(jnp.concatenate(both, axis=0).astype(jnp.bfloat16))
     tile = features // 3
     for n in range(3):
         lanes = slice(n * tile, (n + 1) * tile)
-        both = dot(grad_v[0], acts_v[0, :, lanes])
+        both = dot(grads[0], acts[0][:, lanes])
         for j in range(1, 4):
-            both = both + dot(grad_v[j], acts_v[j, :, lanes])
+            both = both + dot(grads[j], acts[j][:, lanes])
         far[:, lanes] = both[:width].astype(jnp.bfloat16)
         mid[:, lanes] = both[width:].astype(jnp.bfloat16)
 
@@ -632,40 +614,36 @@
         12,
         2 * 4 * rows * features * 2 * width,
         4 * rows * features * 2 + 2 * width * features * 2,
-        in_specs=[SMEM, VMEM, VMEM] + [HBM] * 4,
+        in_specs=[SMEM] + [VMEM] * 6,
         out_specs=[VMEM, VMEM],
-        scratch_shapes=[
-            pltpu.VMEM((4, rows, features), jnp.bfloat16),
-            pltpu.VMEM((4, 2 * width, rows), jnp.bfloat16),
-            pltpu.SemaphoreType.DMA((4,)),
-        ],
         name="weight_grad",
     )(code, mine, theirs, *acts)
 
 
 def input_grad_kernel(piece, code, *refs):
     grads, weights, out = refs[:8], refs[8:12], refs[12]
-    rows = out.shape[0]
+    rows, features = out.shape
     span = pl.ds(pl.multiple_of((code[0] ^ piece) * rows, rows), rows)
-    total = 0.0
-    for k, weight in enumerate(weights):
-        grad = jnp.concatenate([ref[span, :] for ref in grads[2 * k : 2 * k + 2]], axis=1)
-        total = total + dot(grad, weight[...])
-    out[...] = total.astype(jnp.bfloat16)
+    parts = [
+        jnp.concatenate([ref[span, :] for ref in grads[2 * k : 2 * k + 2]], axis=1) for k in range(4)
+    ]
+    tile = features // 3
+    for n in range(3):
+        lanes = slice(n * tile, (n + 1) * tile)
+        total = dot(parts[0], weights[0][:, lanes])
+        for k in range(1, 4):
+            total = total + dot(parts[k], weights[k][:, lanes])
+        out[:, lanes] = total.astype(jnp.bfloat16)
 
 
 def input_grad(code, piece, grads, weights, rows):
-    width, features = weights[0].shape
-    tile = features // 3
+    features = weights[0].shape[1]
     return call(
         functools.partial(input_grad_kernel, piece),
         shaped((rows, features)),
         16,
-        grid=(3,),
-        in_specs=[SMEM]
-        + [pl.BlockSpec(grad.shape, lambda n: (0, 0)) for grad in grads]
-        + [pl.BlockSpec((width, tile), lambda n: (0, n))] * 4,
-        out_specs=pl.BlockSpec((rows, tile), lambda n: (0, n)),
+        in_specs=[SMEM] + [VMEM] * 12,
+        out_specs=VMEM,
         name="input_grad",
     )(code, *grads, *weights)
 
@@ -705,6 +683,7 @@
     k_one, k_inner = along_z(key_slab, HOP_ONE), along_z(key_slab, HOP_INNER)
     v_one, v_inner = along_z(value_slab, HOP_ONE), along_z(value_slab, HOP_INNER)
     normed_c = swap_core(after(normed, key_slab))
+    k_one, k_inner = after_all((k_one, k_inner), code)
     k_second, k_outer = along_z(k_one, HOP_SECOND), along_z(k_inner, HOP_OUTER)
     v_one, v_inner = after_all((v_one, v_inner), k_one, k_inner)
     v_second, v_outer = along_z(v_one, HOP_SECOND), along_z(v_inner, HOP_OUTER)
@@ -796,12 +775,12 @@
     v_third, v_outer = after_all((v_third, v_outer), away)
     v_mid_payload, v_inner_payload = sums((v_first, v_third), (v_second, v_outer))
     v_mid, v_inner = along_z(v_mid_payload, BACK_MID), along_z(v_inner_payload, BACK_INNER)
-    key_grad_far = after(key_grad_far, v_mid_payload)
+    k_third = after(k_third, v_mid_payload)
+    (k_mid_payload,) = sums((k_first, k_third))
+    key_grad_far = after(key_grad_far, k_mid_payload)
     kept = input_grad(code, 0, (key_grad, key_grad_far) + grads[2:], weights, rows)
-    k_third = after(k_third, kept)
-    (k_mid_payload,) = sums((k_first, k_third))
     k_mid, k_outer = along_z(k_mid_payload, BACK_MID), along_z(after(k_first, k_third), BACK_OUTER)
-    v_mid, v_inner = after_all((v_mid, v_inner), k_mid_payload)
+    v_mid, v_inner = after_all((v_mid, v_inner), kept)
     (v_one_payload,) = sums((v_first, v_mid))
     v_one = along_z(v_one_payload, BACK_ONE)
     attention, grad_q = by_head(code, near, near_other, after(back_x, v_one_payload, v_inner))
@@ -818,12 +797,10 @@
     (grad_normed,) = sums((kept, from_x))
     v_one = after(v_one, grad_normed)
     value_own, value_away = halves(code, (v_second, v_inner, v_one))
-    value_other = to_core(value_away)
-    k_one, k_inner = after_all((k_one, k_inner), value_own)
+    grad_value_weight = owned(code, value_own, to_core(value_away))
+    k_one, k_inner = after_all((k_one, k_inner), grad_value_weight)
     key_own, key_away = halves(code, (k_second, k_inner, k_one))
-    key_other = to_core(key_away)
-    grad_value_weight = owned(code, value_own, after(value_other, key_own))
-    grad_key_weight = owned(code, key_own, after(key_other, grad_value_weight))
+    grad_key_weight = owned(code, key_own, to_core(key_away))
     return (attention, grad_normed, grad_q, grad_key_weight, grad_value_weight)
 
 

time: 182 us -> 176 us (0.967)
  waiting for transfers between devices: 53.1 us -> 63.6 us
  starting transfers between devices: 71.3 us -> 62.3 us
  Pallas kernels: 48.3 us -> 40.4 us
    ppermute x42, starting transfers between devices: 68.5 us -> 58.7 us  [move(): return lax.ppermute(array, 'seq', [(at(*a), at(*b)) for a, b in rule])]
    ppermute x42, waiting for transfers between devices: 44.6 us -> 53.7 us  [move(): return lax.ppermute(array, 'seq', [(at(*a), at(*b)) for a, b in rule])]
    pallas_call x2, Pallas kernels: 9.44 us -> 7.17 us  [project(): call(project_kernel, [shaped((4 * rows, width)), shaped((4 * rows, width)...]
    pallas_call x1, Pallas kernels: 8.56 us -> 6.45 us  [attend_scores(): call(scores_kernel, [shaped((blocks, span, 2 * rows)), shaped((blocks, 8,...]
  transfers between devices with their start and end apart: 46 -> 46, of which waited for: 19 -> 22; matrix products, arithmetic and copies ran while one was open for 3% -> 4% of each run, Pallas kernels for 26% -> 22%
where the time goes in v4:
time: 176 us; the launch traced here: 175 us
  waiting for transfers between devices  63.6 us (36%)
  starting transfers between devices  62.3 us (35%)
  Pallas kernels  40.4 us (23%)
  other arithmetic  5.18 us (3%)
  local copies, waits for them, and re-layouts  2.05 us (1%)
    ppermute x42, starting transfers between devices, move(): return lax.ppermute(array, 'seq', [(at(*a), at(*b)) for a, b in rule])  58.7 us
    ppermute x42, waiting for transfers between devices, move(): return lax.ppermute(array, 'seq', [(at(*a), at(*b)) for a, b in rule])  53.7 us
    ppermute x4, waiting for transfers between devices, swap_uly(): return lax.ppermute(array, 'uly', [(0, 1), (1, 0)])  9.93 us
    pallas_call x1, Pallas kernels, attend_values(): call(values_kernel, [shaped((2, 2, rows, 2 * HD)), shaped((2, 2, rows, 2...  8.66 us
    pallas_call x2, Pallas kernels, project(): call(project_kernel, [shaped((4 * rows, width)), shaped((4 * rows, width)...  7.17 us
    pallas_call x1, Pallas kernels, attend_scores(): call(scores_kernel, [shaped((blocks, span, 2 * rows)), shaped((blocks, 8,...  6.45 us
    pallas_call x2, Pallas kernels, weight_grad(): call(weight_grad_kernel, [shaped((width, features)), shaped((width, featu...  4.8 us
    pallas_call x2, Pallas kernels, input_grad(): call(functools.partial(input_grad_kernel, piece), shaped((rows, features)...  4.69 us
  transfers between devices with their start and end apart: 46, of which 22 were waited for; matrix products, arithmetic and copies ran while one was open for 4% of the time, Pallas kernels for 22%

profile of v4, /device:TPU:17, one launch (start us, length us, event | category | flops | bytes accessed | tf_op | source)
XLA Modules:
  0.0 174.9 jit_solution(18245648980474278735)
XLA Ops:
  0.6 2.6 %collective-permute-start.6 = (bf16[64,2688]{1,0:T(8,128)(2,1)}, bf16[64,2688]{1,0:T(8,128)(2,1)S(1)}, u32[]{:S(2)}, u32[]{:S(2)}) collective-permute-start(bf16[64,2688]{1,0:T(8,128)(2,1)} %bitcast.36), channel_id=1, source_target_pairs={{2,0},{6,4},{8,10},{12,14},{18,16},{22,20},{24,26},{28,30},{3,1},{... | collective-permute-start | bytes 1032200 | tf_op jit(solution)/shard_map/ppermute | solution.py:176
  15.5 4.9 %collective-permute-done.3.refs_6_ = bf16[128,2688]{1,0:T(8,128)(2,1)} collective-permute-done((bf16[128,2688]{1,0:T(8,128)(2,1)}, bf16[128,2688]{1,0:T(8,128)(2,1)}, u32[]{:S(2)}, u32[]{:S(2)}) %collective-permute-start.3) | collective-permute-done | bytes 688160 | tf_op jit(solution)/shard_map/ppermute | solution.py:176
  21.6 3.0 %collective-permute-start.4 = (bf16[128,2688]{1,0:T(8,128)(2,1)}, bf16[128,2688]{1,0:T(8,128)(2,1)}, u32[]{:S(2)}, u32[]{:S(2)}) collective-permute-start(bf16[128,2688]{1,0:T(8,128)(2,1)} %collective-permute-done.2.refs_5_), channel_id=1, source_target_pairs={{8,16},{12,20},{18,10},{22,14},{9,17},{13,21},{19,11},{23,15}} | collective-permute-start | bytes 2064392 | tf_op jit(solution)/shard_map/ppermute | solution.py:176
  29.1 3.3 %collective-permute-start.11 = (bf16[128,2688]{1,0:T(8,128)(2,1)}, bf16[128,2688]{1,0:T(8,128)(2,1)}, u32[]{:S(2)}, u32[]{:S(2)}) collective-permute-start(bf16[128,2688]{1,0:T(8,128)(2,1)} %collective-permute-done.7.refs_5_), channel_id=1, source_target_pairs={{8,16},{12,20},{18,10},{22,14},{9,17},{13,21},{19,11},{23,15}} | collective-permute-start | bytes 2064392 | tf_op jit(solution)/shard_map/ppermute | solution.py:176
  40.9 6.2 %collective-permute-done.12.refs_8_ = bf16[128,2688]{1,0:T(8,128)(2,1)} collective-permute-done((bf16[128,2688]{1,0:T(8,128)(2,1)}, bf16[128,2688]{1,0:T(8,128)(2,1)}, u32[]{:S(2)}, u32[]{:S(2)}) %collective-permute-start.12) | collective-permute-done | bytes 688160 | tf_op jit(solution)/shard_map/ppermute | solution.py:176
  50.9 3.6 %project.2 = (bf16[1024,128]{1,0:T(8,128)(2,1)S(1)}, bf16[1024,128]{1,0:T(8,128)(2,1)S(1)}, bf16[256,2688]{1,0:T(8,128)(2,1)S(1)}) custom-call(s32[7]{0:T(128)S(1)} %stack.71.code, bf16[256,2688]{1,0:T(8,128)(2,1)S(1)} %copy-done, bf16[256,2688]{1,0:T(8,128)(2,1)S(1)} %collective-permute-done.9.refs_1_.a1, ...), custom_call_target="tpu_custom_call" | custom-call | tf_op jit(solution)/shard_map/project/pallas_call | solution.py:360
  55.8 5.7 %collective-permute-done.16 = bf16[4,256,256]{2,1,0:T(8,128)(2,1)S(1)} collective-permute-done((bf16[4,256,256]{2,1,0:T(8,128)(2,1)S(1)}, bf16[4,256,256]{2,1,0:T(8,128)(2,1)S(1)}, u32[]{:S(2)}, u32[]{:S(2)}) %collective-permute-start.16) | collective-permute-done | bytes 524320 | tf_op jit(solution)/shard_map/ppermute | solution.py:176
  61.5 3.6 %project.3 = (bf16[1024,128]{1,0:T(8,128)(2,1)S(1)}, bf16[1024,128]{1,0:T(8,128)(2,1)S(1)}, bf16[256,2688]{1,0:T(8,128)(2,1)S(1)}) custom-call(s32[7]{0:T(128)S(1)} %stack.71.code, bf16[256,2688]{1,0:T(8,128)(2,1)S(1)} %copy-done, bf16[256,2688]{1,0:T(8,128)(2,1)S(1)} %collective-permute-done.9.refs_1_.a1, ...), custom_call_target="tpu_custom_call" | custom-call | tf_op jit(solution)/shard_map/project/pallas_call | solution.py:360
  69.6 2.5 %collective-permute-done.15 = bf16[1024,128]{1,0:T(8,128)(2,1)S(1)} collective-permute-done((bf16[1024,128]{1,0:T(8,128)(2,1)S(1)}, bf16[1024,128]{1,0:T(8,128)(2,1)S(1)}, u32[]{:S(2)}, u32[]{:S(2)}) %collective-permute-start.15) | collective-permute-done | bytes 262176 | tf_op jit(solution)/shard_map/ppermute | solution.py:196
  74.2 2.7 %collective-permute-done.19.before_ref = bf16[1024,128]{1,0:T(8,128)(2,1)S(1)} collective-permute-done((bf16[1024,128]{1,0:T(8,128)(2,1)S(1)}, bf16[1024,128]{1,0:T(8,128)(2,1)S(1)}, u32[]{:S(2)}, u32[]{:S(2)}) %collective-permute-start.19) | collective-permute-done | bytes 262176 | tf_op jit(solution)/shard_map/ppermute | solution.py:176
  77.0 6.4 %attend_scores.1 = (bf16[4,1280,512]{2,1,0:T(8,128)(2,1)S(1)}, f32[4,8,512]{2,1,0:T(8,128)S(1)}, f32[1024,128]{1,0:T(8,128)S(1)}, bf16[1024,128]{1,0:T(8,128)(2,1)S(1)}) custom-call(s32[7]{0:T(128)S(1)} %stack.71.code, bf16[4,256,256]{2,1,0:T(8,128)(2,1)S(1)} %pad_maximum_fusion.4.q_ref, bf16[4,256,256]{2,1,0:T(8,128)(2,1)S(1)} %pad_maximum_fusion.5.go_ref, ...), custom_call_target="tpu_custom_call" | custom-call | tf_op jit(solution)/shard_map/attend_scores/pallas_call | solution.py:449
  83.4 3.3 %collective-permute-start.26 = (bf16[1024,128]{1,0:T(8,128)(2,1)S(1)}, bf16[1024,128]{1,0:T(8,128)(2,1)S(1)}, u32[]{:S(2)}, u32[]{:S(2)}) collective-permute-start(bf16[1024,128]{1,0:T(8,128)(2,1)S(1)} %get-tuple-element.108), channel_id=1, source_target_pairs={{8,0},{12,4},{10,2},{14,6},{16,8},{20,12},{18,10},{22,14},{24,16},... | collective-permute-start | bytes 786440 | tf_op jit(solution)/shard_map/ppermute | solution.py:176
  86.8 8.7 %attend_values.1 = (bf16[2,2,256,256]{3,2,1,0:T(8,128)(2,1)S(1)}, bf16[2,2,256,256]{3,2,1,0:T(8,128)(2,1)S(1)}, f32[1024,128]{1,0:T(8,128)S(1)}, bf16[1024,128]{1,0:T(8,128)(2,1)S(1)}) custom-call(s32[7]{0:T(128)S(1)} %stack.71.code, bf16[4,256,256]{2,1,0:T(8,128)(2,1)S(1)} %pad_maximum_fusion.4.q_ref, bf16[4,256,256]{2,1,0:T(8,128)(2,1)S(1)} %pad_maximum_fusion.5.go_ref, ...), custom_call_target="tpu_custom_call" | custom-call | tf_op jit(solution)/shard_map/attend_values/pallas_call | solution.py:550
  100.7 4.5 %collective-permute-done.27.theirs.refs_5_ = bf16[1024,128]{1,0:T(8,128)(2,1)S(1)} collective-permute-done((bf16[1024,128]{1,0:T(8,128)(2,1)S(1)}, bf16[1024,128]{1,0:T(8,128)(2,1)S(1)}, u32[]{:S(2)}, u32[]{:S(2)}) %collective-permute-start.27) | collective-permute-done | bytes 262176 | tf_op jit(solution)/shard_map/ppermute | solution.py:196
  105.2 2.4 %weight_grad.2 = (bf16[128,2688]{1,0:T(8,128)(2,1)S(1)}, bf16[128,2688]{1,0:T(8,128)(2,1)S(1)}) custom-call(s32[7]{0:T(128)S(1)} %stack.71.code, bf16[1024,128]{1,0:T(8,128)(2,1)S(1)} %add_convert_fusion.mine.refs_4_, bf16[1024,128]{1,0:T(8,128)(2,1)S(1)} %collective-permute-done.27.theirs.refs_5_, bf16[256,2688]{1,0:T(8,128)(2,1)S(1)} %copy-done, ...), custom_call_target="tpu_custom_call" | custom-call | flops 1409286144 | bytes 6881280 | tf_op jit(solution)/shard_map/weight_grad/pallas_call | solution.py:611
  112.3 2.9 %collective-permute-done.28.theirs.refs_1_ = bf16[1024,128]{1,0:T(8,128)(2,1)S(1)} collective-permute-done((bf16[1024,128]{1,0:T(8,128)(2,1)S(1)}, bf16[1024,128]{1,0:T(8,128)(2,1)S(1)}, u32[]{:S(2)}, u32[]{:S(2)}) %collective-permute-start.28) | collective-permute-done | bytes 262176 | tf_op jit(solution)/shard_map/ppermute | solution.py:196
  117.0 2.4 %weight_grad.3 = (bf16[128,2688]{1,0:T(8,128)(2,1)S(1)}, bf16[128,2688]{1,0:T(8,128)(2,1)S(1)}) custom-call(s32[7]{0:T(128)S(1)} %stack.71.code, bf16[1024,128]{1,0:T(8,128)(2,1)S(1)} %multiply_convert_fusion.mine.refs_0_, bf16[1024,128]{1,0:T(8,128)(2,1)S(1)} %collective-permute-done.28.theirs.refs_1_, bf16[256,2688]{1,0:T(8,128)(2,1)S(1)} %copy-done, ...), custom_call_target="tpu_custom_call" | custom-call | flops 1409286144 | bytes 6881280 | tf_op jit(solution)/shard_map/weight_grad/pallas_call | solution.py:611
  122.3 2.3 %input_grad.2 = bf16[256,2688]{1,0:T(8,128)(2,1)S(1)} custom-call(s32[7]{0:T(128)S(1)} %stack.71.code, bf16[1024,128]{1,0:T(8,128)(2,1)S(1)} %multiply_convert_fusion.mine.refs_0_, bf16[1024,128]{1,0:T(8,128)(2,1)S(1)} %collective-permute-done.28.theirs.refs_1_, bf16[1024,128]{1,0:T(8,128)(2,1)S(1)} %collective-permute-done.31.refs_2_, ...), custom_call_target="tpu_custom_call" | custom-call | tf_op jit(solution)/shard_map/input_grad/pallas_call | solution.py:641
  133.5 2.3 %input_grad.3.refs_0_ = bf16[256,2688]{1,0:T(8,128)(2,1)S(1)} custom-call(s32[7]{0:T(128)S(1)} %stack.71.code, bf16[1024,128]{1,0:T(8,128)(2,1)S(1)} %multiply_convert_fusion.mine.refs_0_, bf16[1024,128]{1,0:T(8,128)(2,1)S(1)} %collective-permute-done.28.theirs.refs_1_, bf16[1024,128]{1,0:T(8,128)(2,1)S(1)} %collective-permute-done.31.refs_2_, ...), custom_call_target="tpu_custom_call" | custom-call | tf_op jit(solution)/shard_map/input_grad/pallas_call | solution.py:641
  135.8 2.3 %collective-permute-done.36.b = bf16[128,2688]{1,0:T(8,128)(2,1)S(1)} collective-permute-done((bf16[128,2688]{1,0:T(8,128)(2,1)S(1)}, bf16[128,2688]{1,0:T(8,128)(2,1)S(1)}, u32[]{:S(2)}, u32[]{:S(2)}) %collective-permute-start.36) | collective-permute-done | bytes 688160 | tf_op jit(solution)/shard_map/ppermute | solution.py:176
  138.1 9.9 %collective-permute-done.35.refs_1_ = bf16[128,2688]{1,0:T(8,128)(2,1)S(1)} collective-permute-done((bf16[128,2688]{1,0:T(8,128)(2,1)S(1)}, bf16[128,2688]{1,0:T(8,128)(2,1)S(1)}, u32[]{:S(2)}, u32[]{:S(2)}) %collective-permute-start.35) | collective-permute-done | bytes 688160 | tf_op jit(solution)/shard_map/ppermute | solution.py:176
  151.2 4.9 %collective-permute-done.39.refs_1_ = bf16[128,2688]{1,0:T(8,128)(2,1)S(1)} collective-permute-done((bf16[128,2688]{1,0:T(8,128)(2,1)S(1)}, bf16[128,2688]{1,0:T(8,128)(2,1)S(1)}, u32[]{:S(2)}, u32[]{:S(2)}) %collective-permute-start.39) | collective-permute-done | bytes 688160 | tf_op jit(solution)/shard_map/ppermute | solution.py:176
  162.7 3.4 %collective-permute-done.44.other = bf16[64,2688]{1,0:T(8,128)(2,1)S(1)} collective-permute-done((bf16[64,2688]{1,0:T(8,128)(2,1)S(1)}, bf16[64,2688]{1,0:T(8,128)(2,1)S(1)}, u32[]{:S(2)}, u32[]{:S(2)}) %collective-permute-start.44) | collective-permute-done | bytes 344096 | tf_op jit(solution)/shard_map/ppermute | solution.py:176
  169.6 3.8 %collective-permute-done.45.other = bf16[64,2688]{1,0:T(8,128)(2,1)S(1)} collective-permute-done((bf16[64,2688]{1,0:T(8,128)(2,1)S(1)}, bf16[64,2688]{1,0:T(8,128)(2,1)S(1)}, u32[]{:S(2)}, u32[]{:S(2)}) %collective-permute-start.45) | collective-permute-done | bytes 344096 | tf_op jit(solution)/shard_map/ppermute | solution.py:176
  (125 shorter events, 75.9 us)
Async XLA Ops:
  4.6 32.4 %collective-permute-start = (bf16[256,2688]{1,0:T(8,128)(2,1)}, bf16[256,2688]{1,0:T(8,128)(2,1)S(1)}, u32[]{:S(2)}, u32[]{:S(2)}) collective-permute-start(bf16[256,2688]{1,0:T(8,128)(2,1)} %a0.3), channel_id=1, source_target_pairs={{0,4},{2,6},{4,0},{6,2},{8,12},{10,14},{12,8},{14,10},{16,20},{18,... | collective-permute-start | bytes 4128776 | tf_op jit(solution)/shard_map/ppermute | solution.py:176
  9.4 12.2 %collective-permute-start.2 = (bf16[128,2688]{1,0:T(8,128)(2,1)}, bf16[128,2688]{1,0:T(8,128)(2,1)}, u32[]{:S(2)}, u32[]{:S(2)}) collective-permute-start(bf16[128,2688]{1,0:T(8,128)(2,1)} %pad_maximum_fusion.refs_4_), channel_id=1, source_target_pairs={{0,8},{4,12},{26,18},{30,22},{10,2},{14,6},{16,24},{20,28},{1,9},{... | collective-permute-start | bytes 2064392 | tf_op jit(solution)/shard_map/ppermute | solution.py:176
  10.8 17.5 %collective-permute-start.8 = (bf16[128,2688]{1,0:T(8,128)(2,1)S(1)}, bf16[128,2688]{1,0:T(8,128)(2,1)}, u32[]{:S(2)}, u32[]{:S(2)}) collective-permute-start(bf16[128,2688]{1,0:T(8,128)(2,1)S(1)} %pad_maximum_fusion.1.refs_4_), channel_id=1, source_target_pairs={{10,18},{14,22},{16,8},{20,12},{11,19},{15,23},{17,9},{21,13}} | collective-permute-start | bytes 2064392 | tf_op jit(solution)/shard_map/ppermute | solution.py:176
  12.1 17.0 %collective-permute-start.7 = (bf16[128,2688]{1,0:T(8,128)(2,1)S(1)}, bf16[128,2688]{1,0:T(8,128)(2,1)}, u32[]{:S(2)}, u32[]{:S(2)}) collective-permute-start(bf16[128,2688]{1,0:T(8,128)(2,1)S(1)} %pad_maximum_fusion.1.refs_4_), channel_id=1, source_target_pairs={{0,8},{4,12},{26,18},{30,22},{10,2},{14,6},{16,24},{20,28},{1,9},{... | collective-permute-start | bytes 2064392 | tf_op jit(solution)/shard_map/ppermute | solution.py:176
  21.6 12.9 %collective-permute-start.4 = (bf16[128,2688]{1,0:T(8,128)(2,1)}, bf16[128,2688]{1,0:T(8,128)(2,1)}, u32[]{:S(2)}, u32[]{:S(2)}) collective-permute-start(bf16[128,2688]{1,0:T(8,128)(2,1)} %collective-permute-done.2.refs_5_), channel_id=1, source_target_pairs={{8,16},{12,20},{18,10},{22,14},{9,17},{13,21},{19,11},{23,15}} | collective-permute-start | bytes 2064392 | tf_op jit(solution)/shard_map/ppermute | solution.py:176
  32.4 14.8 %collective-permute-start.12 = (bf16[128,2688]{1,0:T(8,128)(2,1)}, bf16[128,2688]{1,0:T(8,128)(2,1)}, u32[]{:S(2)}, u32[]{:S(2)}) collective-permute-start(bf16[128,2688]{1,0:T(8,128)(2,1)} %collective-permute-done.8.refs_6_), channel_id=1, source_target_pairs={{8,0},{12,4},{18,26},{22,30},{9,1},{13,5},{19,27},{23,31}} | collective-permute-start | bytes 2064392 | tf_op jit(solution)/shard_map/ppermute | solution.py:176
  34.5 16.3 %collective-permute-start.9 = (bf16[256,2688]{1,0:T(8,128)(2,1)S(1)}, bf16[256,2688]{1,0:T(8,128)(2,1)S(1)}, u32[]{:S(2)}, u32[]{:S(2)}) collective-permute-start(bf16[256,2688]{1,0:T(8,128)(2,1)S(1)} %copy-done), channel_id=1, source_target_pairs={{0,2},{2,0},{4,6},{6,4},{8,10},{10,8},{12,14},{14,12},{16,18},{18,... | collective-permute-start | bytes 4128776 | tf_op jit(solution)/shard_map/ppermute | solution.py:176
  36.2 14.7 %collective-permute-start.14 = (bf16[128,2688]{1,0:T(8,128)(2,1)}, bf16[128,2688]{1,0:T(8,128)(2,1)S(1)}, u32[]{:S(2)}, u32[]{:S(2)}) collective-permute-start(bf16[128,2688]{1,0:T(8,128)(2,1)} %collective-permute-done.4.refs_7_), channel_id=1, source_target_pairs={{16,24},{20,28},{10,2},{14,6},{17,25},{21,29},{11,3},{15,7}} | collective-permute-start | bytes 2064392 | tf_op jit(solution)/shard_map/ppermute | solution.py:176
  36.9 13.9 %collective-permute-start.10 = (bf16[256,2688]{1,0:T(8,128)(2,1)S(1)}, bf16[256,2688]{1,0:T(8,128)(2,1)S(1)}, u32[]{:S(2)}, u32[]{:S(2)}) collective-permute-start(bf16[256,2688]{1,0:T(8,128)(2,1)S(1)} %collective-permute-done.refs_2_.a2), channel_id=1, source_target_pairs={{0,2},{2,0},{4,6},{6,4},{8,10},{10,8},{12,14},{14,12},{16,18},{18,... | collective-permute-start | bytes 4128776 | tf_op jit(solution)/shard_map/ppermute | solution.py:176
  47.1 14.3 %collective-permute-start.13 = (bf16[128,2688]{1,0:T(8,128)(2,1)}, bf16[128,2688]{1,0:T(8,128)(2,1)S(1)}, u32[]{:S(2)}, u32[]{:S(2)}) collective-permute-start(bf16[128,2688]{1,0:T(8,128)(2,1)} %collective-permute-done.11.refs_7_), channel_id=1, source_target_pairs={{16,24},{20,28},{10,2},{14,6},{17,25},{21,29},{11,3},{15,7}} | collective-permute-start | bytes 2064392 | tf_op jit(solution)/shard_map/ppermute | solution.py:176
  49.2 12.3 %collective-permute-start.16 = (bf16[4,256,256]{2,1,0:T(8,128)(2,1)S(1)}, bf16[4,256,256]{2,1,0:T(8,128)(2,1)S(1)}, u32[]{:S(2)}, u32[]{:S(2)}) collective-permute-start(bf16[4,256,256]{2,1,0:T(8,128)(2,1)S(1)} %pad_maximum_fusion.2), channel_id=1, source_target_pairs={{0,4},{2,6},{4,0},{6,2},{8,12},{10,14},{12,8},{14,10},{16,20},{18,... | collective-permute-start | bytes 1572872 | tf_op jit(solution)/shard_map/ppermute | solution.py:176
  54.5 12.7 %collective-permute-start.18 = (bf16[1024,128]{1,0:T(8,128)(2,1)S(1)}, bf16[1024,128]{1,0:T(8,128)(2,1)S(1)}, u32[]{:S(2)}, u32[]{:S(2)}) collective-permute-start(bf16[1024,128]{1,0:T(8,128)(2,1)S(1)} %get-tuple-element.86), channel_id=1, source_target_pairs={{0,1},{1,0},{2,3},{3,2},{4,5},{5,4},{6,7},{7,6},{8,9},{9,8},{10,11... | collective-permute-start | bytes 786440 | tf_op jit(solution)/shard_map/ppermute | solution.py:196
  66.6 20.2 %collective-permute-start.22 = (bf16[256,2688]{1,0:T(8,128)(2,1)S(1)}, bf16[256,2688]{1,0:T(8,128)(2,1)S(1)}, u32[]{:S(2)}, u32[]{:S(2)}) collective-permute-start(bf16[256,2688]{1,0:T(8,128)(2,1)S(1)} %get-tuple-element.100.refs_10_), channel_id=1, source_target_pairs={{0,2},{2,0},{4,6},{6,4},{8,10},{10,8},{12,14},{14,12},{16,18},{18,... | collective-permute-start | bytes 4128776 | tf_op jit(solution)/shard_map/ppermute | solution.py:176
  67.1 19.7 %collective-permute-start.21 = (bf16[256,2688]{1,0:T(8,128)(2,1)S(1)}, bf16[256,2688]{1,0:T(8,128)(2,1)S(1)}, u32[]{:S(2)}, u32[]{:S(2)}) collective-permute-start(bf16[256,2688]{1,0:T(8,128)(2,1)S(1)} %get-tuple-element.99.refs_8_), channel_id=1, source_target_pairs={{0,2},{2,0},{4,6},{6,4},{8,10},{10,8},{12,14},{14,12},{16,18},{18,... | collective-permute-start | bytes 4128776 | tf_op jit(solution)/shard_map/ppermute | solution.py:176
  72.2 14.6 %collective-permute-start.20 = (bf16[1024,128]{1,0:T(8,128)(2,1)S(1)}, bf16[1024,128]{1,0:T(8,128)(2,1)S(1)}, u32[]{:S(2)}, u32[]{:S(2)}) collective-permute-start(bf16[1024,128]{1,0:T(8,128)(2,1)S(1)} %add_convert_fusion.1.v_own), channel_id=1, source_target_pairs={{0,8},{4,12},{2,10},{6,14},{8,16},{12,20},{10,18},{14,22},{16,24},... | collective-permute-start | bytes 786440 | tf_op jit(solution)/shard_map/ppermute | solution.py:176
  83.4 13.7 %collective-permute-start.26 = (bf16[1024,128]{1,0:T(8,128)(2,1)S(1)}, bf16[1024,128]{1,0:T(8,128)(2,1)S(1)}, u32[]{:S(2)}, u32[]{:S(2)}) collective-permute-start(bf16[1024,128]{1,0:T(8,128)(2,1)S(1)} %get-tuple-element.108), channel_id=1, source_target_pairs={{8,0},{12,4},{10,2},{14,6},{16,8},{20,12},{18,10},{22,14},{24,16},... | collective-permute-start | bytes 786440 | tf_op jit(solution)/shard_map/ppermute | solution.py:176
  99.6 20.5 %collective-permute-start.24 = (bf16[2,2,256,256]{3,2,1,0:T(8,128)(2,1)S(1)}, bf16[2,2,256,256]{3,2,1,0:T(8,128)(2,1)S(1)}, u32[]{:S(2)}, u32[]{:S(2)}) collective-permute-start(bf16[2,2,256,256]{3,2,1,0:T(8,128)(2,1)S(1)} %pack.1), channel_id=1, source_target_pairs={{0,4},{2,6},{4,0},{6,2},{8,12},{10,14},{12,8},{14,10},{16,20},{18,... | collective-permute-start | bytes 1572872 | tf_op jit(solution)/shard_map/ppermute | solution.py:176
  108.8 16.9 %collective-permute-start.29 = (bf16[128,2688]{1,0:T(8,128)(2,1)S(1)}, bf16[128,2688]{1,0:T(8,128)(2,1)S(1)}, u32[]{:S(2)}, u32[]{:S(2)}) collective-permute-start(bf16[128,2688]{1,0:T(8,128)(2,1)S(1)} %get-tuple-element.115.refs_2_.a), channel_id=1, source_target_pairs={{24,16},{28,20},{2,10},{6,14},{25,17},{29,21},{3,11},{7,15}} | collective-permute-start | bytes 2064392 | tf_op jit(solution)/shard_map/ppermute | solution.py:176
  109.5 18.2 %collective-permute-start.30 = (bf16[128,2688]{1,0:T(8,128)(2,1)S(1)}, bf16[128,2688]{1,0:T(8,128)(2,1)S(1)}, u32[]{:S(2)}, u32[]{:S(2)}) collective-permute-start(bf16[128,2688]{1,0:T(8,128)(2,1)S(1)} %get-tuple-element.111.refs_0_), channel_id=1, source_target_pairs={{0,8},{4,12},{26,18},{30,22},{1,9},{5,13},{27,19},{31,23}} | collective-permute-start | bytes 2064392 | tf_op jit(solution)/shard_map/ppermute | solution.py:176
  124.7 34.5 %collective-permute-start.38 = (bf16[256,2688]{1,0:T(8,128)(2,1)S(1)}, bf16[256,2688]{1,0:T(8,128)(2,1)S(1)}, u32[]{:S(2)}, u32[]{:S(2)}) collective-permute-start(bf16[256,2688]{1,0:T(8,128)(2,1)S(1)} %input_grad.2), channel_id=1, source_target_pairs={{0,4},{2,6},{4,0},{6,2},{8,12},{10,14},{12,8},{14,10},{16,20},{18,... | collective-permute-start | bytes 4128776 | tf_op jit(solution)/shard_map/ppermute | solution.py:176
  129.4 18.7 %collective-permute-start.35 = (bf16[128,2688]{1,0:T(8,128)(2,1)S(1)}, bf16[128,2688]{1,0:T(8,128)(2,1)S(1)}, u32[]{:S(2)}, u32[]{:S(2)}) collective-permute-start(bf16[128,2688]{1,0:T(8,128)(2,1)S(1)} %get-tuple-element.120), channel_id=1, source_target_pairs={{16,8},{20,12},{10,18},{14,22},{17,9},{21,13},{11,19},{15,23}} | collective-permute-start | bytes 2064392 | tf_op jit(solution)/shard_map/ppermute | solution.py:176
  130.9 25.2 %collective-permute-start.39 = (bf16[128,2688]{1,0:T(8,128)(2,1)S(1)}, bf16[128,2688]{1,0:T(8,128)(2,1)S(1)}, u32[]{:S(2)}, u32[]{:S(2)}) collective-permute-start(bf16[128,2688]{1,0:T(8,128)(2,1)S(1)} %sums.6), channel_id=1, source_target_pairs={{16,8},{20,12},{10,18},{14,22},{17,9},{21,13},{11,19},{15,23}} | collective-permute-start | bytes 2064392 | tf_op jit(solution)/shard_map/ppermute | solution.py:176
  132.2 23.9 %collective-permute-start.40 = (bf16[128,2688]{1,0:T(8,128)(2,1)S(1)}, bf16[128,2688]{1,0:T(8,128)(2,1)S(1)}, u32[]{:S(2)}, u32[]{:S(2)}) collective-permute-start(bf16[128,2688]{1,0:T(8,128)(2,1)S(1)} %get-tuple-element.129.refs_0_), channel_id=1, source_target_pairs={{0,8},{4,12},{26,18},{30,22},{1,9},{5,13},{27,19},{31,23}} | collective-permute-start | bytes 2064392 | tf_op jit(solution)/shard_map/ppermute | solution.py:176
  148.2 12.3 %collective-permute-start.43 = (bf16[128,2688]{1,0:T(8,128)(2,1)S(1)}, bf16[128,2688]{1,0:T(8,128)(2,1)S(1)}, u32[]{:S(2)}, u32[]{:S(2)}) collective-permute-start(bf16[128,2688]{1,0:T(8,128)(2,1)S(1)} %sums.7), channel_id=1, source_target_pairs={{8,0},{12,4},{18,26},{22,30},{2,10},{6,14},{24,16},{28,20},{9,1},{... | collective-permute-start | bytes 2064392 | tf_op jit(solution)/shard_map/ppermute | solution.py:176
  (28 other events, 259.9 us)

commit v5 on v4

--- a/solution.py
+++ b/solution.py
@@ -412,24 +412,23 @@
         heads.append(jnp.concatenate([query.T.astype(jnp.bfloat16), query_mark[...]], axis=0))
         grads.append(go_ref[0, :, lanes].astype(jnp.float32).T)
     query_t = jnp.concatenate(heads, axis=1)
-    total = jnp.zeros((1, 2 * rows), jnp.float32)
-    es = []
-    for c in range(chunks):
-        begin = pl.multiple_of((block + c) * rows, rows)
-        e = jnp.exp(dot(keys_v[pl.ds(begin, rows), :], query_t))
-        if c == 0:
-            e = jnp.where(behind, 0.0, e)
-        if c == chunks - 1:
-            e = jnp.where(behind, e, 0.0)
-        total = total + jnp.sum(e, axis=0, keepdims=True)
-        es.append(e.astype(jnp.bfloat16))
-        e_ref[0, c * rows : (c + 1) * rows, :] = es[-1]
+    span = pl.ds(pl.multiple_of(block * rows, rows), chunks * rows)
+    e = jnp.exp(dot(keys_v[span, :], query_t))
+    e = jnp.concatenate(
+        [
+            jnp.where(behind, 0.0, e[:rows]),
+            e[rows:-rows],
+            jnp.where(behind, e[-rows:], 0.0),
+        ],
+        axis=0,
+    )
+    total = jnp.sum(e, axis=0, keepdims=True)
+    e = e.astype(jnp.bfloat16)
+    e_ref[0] = e
     inverse = 1.0 / total
     stat_ref[0] = jnp.broadcast_to(inverse, stat_ref.shape[1:])
     grad = (jnp.concatenate(grads, axis=1) * inverse).T.astype(jnp.bfloat16)
-    for c in range(chunks):
-        span = pl.ds(pl.multiple_of((block + c) * rows, rows), rows)
-        acc[span, :] = acc[span, :] + dot(es[c], grad)
+    acc[span, :] = acc[span, :] + dot(e, grad)
 
     @pl.when(block == pl.num_programs(0) - 1)
     def _():
@@ -521,14 +520,10 @@
     out_t = dot(values_t[:, span], e) * inverse
     along = jnp.sum(out_t * grad_t, axis=0, keepdims=True) * inverse
     scaled = (grad_t * inverse).astype(jnp.bfloat16)
-    parts = []
-    for c in range(span_rows // rows):
-        here = pl.ds(pl.multiple_of((block + c) * rows, rows), rows)
-        dprob = dot(values_v[here, :], scaled)
-        dscore = e[c * rows : (c + 1) * rows] * (dprob - along).astype(jnp.bfloat16)
-        acc[here, :] = acc[here, :] + dot(dscore, queries)
-        parts.append(dscore)
-    dquery_t = dot(keys_t[:, span], jnp.concatenate(parts, axis=0))
+    dprob = dot(values_v[span, :], scaled)
+    dscore = e * (dprob - along).astype(jnp.bfloat16)
+    acc[span, :] = acc[span, :] + dot(dscore, queries)
+    dquery_t = dot(keys_t[:, span], dscore)
     for g in range(2):
         lanes = slice(g * HD, (g + 1) * HD)
         across = slice(g * rows, (g + 1) * rows)

time: 176 us -> 174 us (0.989)
  transfers between devices with their start and end apart: 46 -> 46, of which waited for: 22 -> 22; matrix products, arithmetic and copies ran while one was open for 4% -> 4% of each run, Pallas kernels for 22% -> 21%
where the time goes in v5:
time: 174 us; the launch traced here: 173 us
  waiting for transfers between devices  63.6 us (37%)
  starting transfers between devices  62.2 us (36%)
  Pallas kernels  38.8 us (22%)
  other arithmetic  5.18 us (3%)
  local copies, waits for them, and re-layouts  2.05 us (1%)
    ppermute x42, starting transfers between devices, move(): return lax.ppermute(array, 'seq', [(at(*a), at(*b)) for a, b in rule])  58.7 us
    ppermute x42, waiting for transfers between devices, move(): return lax.ppermute(array, 'seq', [(at(*a), at(*b)) for a, b in rule])  53.7 us
    ppermute x4, waiting for transfers between devices, swap_uly(): return lax.ppermute(array, 'uly', [(0, 1), (1, 0)])  9.95 us
    pallas_call x2, Pallas kernels, project(): call(project_kernel, [shaped((4 * rows, width)), shaped((4 * rows, width)...  7.17 us
    pallas_call x1, Pallas kernels, attend_values(): call(values_kernel, [shaped((2, 2, rows, 2 * HD)), shaped((2, 2, rows, 2...  7.03 us
    pallas_call x1, Pallas kernels, attend_scores(): call(scores_kernel, [shaped((blocks, span, 2 * rows)), shaped((blocks, 8,...  6.45 us
    pallas_call x2, Pallas kernels, weight_grad(): call(weight_grad_kernel, [shaped((width, features)), shaped((width, featu...  4.81 us
    pallas_call x2, Pallas kernels, input_grad(): call(functools.partial(input_grad_kernel, piece), shaped((rows, features)...  4.69 us
  transfers between devices with their start and end apart: 46, of which 22 were waited for; matrix products, arithmetic and copies ran while one was open for 4% of the time, Pallas kernels for 21%

profile of v5, /device:TPU:17, one launch (start us, length us, event | category | flops | bytes accessed | tf_op | source)
XLA Modules:
  0.0 173.2 jit_solution(3863192920710538610)
XLA Ops:
  0.6 2.6 %collective-permute-start.6 = (bf16[64,2688]{1,0:T(8,128)(2,1)}, bf16[64,2688]{1,0:T(8,128)(2,1)S(1)}, u32[]{:S(2)}, u32[]{:S(2)}) collective-permute-start(bf16[64,2688]{1,0:T(8,128)(2,1)} %bitcast.36), channel_id=1, source_target_pairs={{2,0},{6,4},{8,10},{12,14},{18,16},{22,20},{24,26},{28,30},{3,1},{... | collective-permute-start | bytes 1032200 | tf_op jit(solution)/shard_map/ppermute | solution.py:176
  15.5 4.9 %collective-permute-done.3.refs_6_ = bf16[128,2688]{1,0:T(8,128)(2,1)} collective-permute-done((bf16[128,2688]{1,0:T(8,128)(2,1)}, bf16[128,2688]{1,0:T(8,128)(2,1)}, u32[]{:S(2)}, u32[]{:S(2)}) %collective-permute-start.3) | collective-permute-done | bytes 688160 | tf_op jit(solution)/shard_map/ppermute | solution.py:176
  21.6 3.0 %collective-permute-start.4 = (bf16[128,2688]{1,0:T(8,128)(2,1)}, bf16[128,2688]{1,0:T(8,128)(2,1)}, u32[]{:S(2)}, u32[]{:S(2)}) collective-permute-start(bf16[128,2688]{1,0:T(8,128)(2,1)} %collective-permute-done.2.refs_5_), channel_id=1, source_target_pairs={{8,16},{12,20},{18,10},{22,14},{9,17},{13,21},{19,11},{23,15}} | collective-permute-start | bytes 2064392 | tf_op jit(solution)/shard_map/ppermute | solution.py:176
  29.1 3.3 %collective-permute-start.11 = (bf16[128,2688]{1,0:T(8,128)(2,1)}, bf16[128,2688]{1,0:T(8,128)(2,1)}, u32[]{:S(2)}, u32[]{:S(2)}) collective-permute-start(bf16[128,2688]{1,0:T(8,128)(2,1)} %collective-permute-done.7.refs_5_), channel_id=1, source_target_pairs={{8,16},{12,20},{18,10},{22,14},{9,17},{13,21},{19,11},{23,15}} | collective-permute-start | bytes 2064392 | tf_op jit(solution)/shard_map/ppermute | solution.py:176
  40.9 6.2 %collective-permute-done.12.refs_8_ = bf16[128,2688]{1,0:T(8,128)(2,1)} collective-permute-done((bf16[128,2688]{1,0:T(8,128)(2,1)}, bf16[128,2688]{1,0:T(8,128)(2,1)}, u32[]{:S(2)}, u32[]{:S(2)}) %collective-permute-start.12) | collective-permute-done | bytes 688160 | tf_op jit(solution)/shard_map/ppermute | solution.py:176
  50.9 3.6 %project.2 = (bf16[1024,128]{1,0:T(8,128)(2,1)S(1)}, bf16[1024,128]{1,0:T(8,128)(2,1)S(1)}, bf16[256,2688]{1,0:T(8,128)(2,1)S(1)}) custom-call(s32[7]{0:T(128)S(1)} %stack.71.code, bf16[256,2688]{1,0:T(8,128)(2,1)S(1)} %copy-done, bf16[256,2688]{1,0:T(8,128)(2,1)S(1)} %collective-permute-done.9.refs_1_.a1, ...), custom_call_target="tpu_custom_call" | custom-call | tf_op jit(solution)/shard_map/project/pallas_call | solution.py:360
  55.8 5.7 %collective-permute-done.16 = bf16[4,256,256]{2,1,0:T(8,128)(2,1)S(1)} collective-permute-done((bf16[4,256,256]{2,1,0:T(8,128)(2,1)S(1)}, bf16[4,256,256]{2,1,0:T(8,128)(2,1)S(1)}, u32[]{:S(2)}, u32[]{:S(2)}) %collective-permute-start.16) | collective-permute-done | bytes 524320 | tf_op jit(solution)/shard_map/ppermute | solution.py:176
  61.5 3.6 %project.3 = (bf16[1024,128]{1,0:T(8,128)(2,1)S(1)}, bf16[1024,128]{1,0:T(8,128)(2,1)S(1)}, bf16[256,2688]{1,0:T(8,128)(2,1)S(1)}) custom-call(s32[7]{0:T(128)S(1)} %stack.71.code, bf16[256,2688]{1,0:T(8,128)(2,1)S(1)} %copy-done, bf16[256,2688]{1,0:T(8,128)(2,1)S(1)} %collective-permute-done.9.refs_1_.a1, ...), custom_call_target="tpu_custom_call" | custom-call | tf_op jit(solution)/shard_map/project/pallas_call | solution.py:360
  69.6 2.5 %collective-permute-done.15 = bf16[1024,128]{1,0:T(8,128)(2,1)S(1)} collective-permute-done((bf16[1024,128]{1,0:T(8,128)(2,1)S(1)}, bf16[1024,128]{1,0:T(8,128)(2,1)S(1)}, u32[]{:S(2)}, u32[]{:S(2)}) %collective-permute-start.15) | collective-permute-done | bytes 262176 | tf_op jit(solution)/shard_map/ppermute | solution.py:196
  74.2 2.7 %collective-permute-done.19.before_ref = bf16[1024,128]{1,0:T(8,128)(2,1)S(1)} collective-permute-done((bf16[1024,128]{1,0:T(8,128)(2,1)S(1)}, bf16[1024,128]{1,0:T(8,128)(2,1)S(1)}, u32[]{:S(2)}, u32[]{:S(2)}) %collective-permute-start.19) | collective-permute-done | bytes 262176 | tf_op jit(solution)/shard_map/ppermute | solution.py:176
  77.0 6.4 %attend_scores.1 = (bf16[4,1280,512]{2,1,0:T(8,128)(2,1)S(1)}, f32[4,8,512]{2,1,0:T(8,128)S(1)}, f32[1024,128]{1,0:T(8,128)S(1)}, bf16[1024,128]{1,0:T(8,128)(2,1)S(1)}) custom-call(s32[7]{0:T(128)S(1)} %stack.71.code, bf16[4,256,256]{2,1,0:T(8,128)(2,1)S(1)} %pad_maximum_fusion.4.q_ref, bf16[4,256,256]{2,1,0:T(8,128)(2,1)S(1)} %pad_maximum_fusion.5.go_ref, ...), custom_call_target="tpu_custom_call" | custom-call | tf_op jit(solution)/shard_map/attend_scores/pallas_call | solution.py:448
  83.4 3.3 %collective-permute-start.26 = (bf16[1024,128]{1,0:T(8,128)(2,1)S(1)}, bf16[1024,128]{1,0:T(8,128)(2,1)S(1)}, u32[]{:S(2)}, u32[]{:S(2)}) collective-permute-start(bf16[1024,128]{1,0:T(8,128)(2,1)S(1)} %get-tuple-element.108), channel_id=1, source_target_pairs={{8,0},{12,4},{10,2},{14,6},{16,8},{20,12},{18,10},{22,14},{24,16},... | collective-permute-start | bytes 786440 | tf_op jit(solution)/shard_map/ppermute | solution.py:176
  86.8 7.0 %attend_values.1 = (bf16[2,2,256,256]{3,2,1,0:T(8,128)(2,1)S(1)}, bf16[2,2,256,256]{3,2,1,0:T(8,128)(2,1)S(1)}, f32[1024,128]{1,0:T(8,128)S(1)}, bf16[1024,128]{1,0:T(8,128)(2,1)S(1)}) custom-call(s32[7]{0:T(128)S(1)} %stack.71.code, bf16[4,256,256]{2,1,0:T(8,128)(2,1)S(1)} %pad_maximum_fusion.4.q_ref, bf16[4,256,256]{2,1,0:T(8,128)(2,1)S(1)} %pad_maximum_fusion.5.go_ref, ...), custom_call_target="tpu_custom_call" | custom-call | tf_op jit(solution)/shard_map/attend_values/pallas_call | solution.py:545
  99.0 4.5 %collective-permute-done.27.theirs.refs_5_ = bf16[1024,128]{1,0:T(8,128)(2,1)S(1)} collective-permute-done((bf16[1024,128]{1,0:T(8,128)(2,1)S(1)}, bf16[1024,128]{1,0:T(8,128)(2,1)S(1)}, u32[]{:S(2)}, u32[]{:S(2)}) %collective-permute-start.27) | collective-permute-done | bytes 262176 | tf_op jit(solution)/shard_map/ppermute | solution.py:196
  103.5 2.4 %weight_grad.2 = (bf16[128,2688]{1,0:T(8,128)(2,1)S(1)}, bf16[128,2688]{1,0:T(8,128)(2,1)S(1)}) custom-call(s32[7]{0:T(128)S(1)} %stack.71.code, bf16[1024,128]{1,0:T(8,128)(2,1)S(1)} %add_convert_fusion.mine.refs_4_, bf16[1024,128]{1,0:T(8,128)(2,1)S(1)} %collective-permute-done.27.theirs.refs_5_, bf16[256,2688]{1,0:T(8,128)(2,1)S(1)} %copy-done, ...), custom_call_target="tpu_custom_call" | custom-call | flops 1409286144 | bytes 6881280 | tf_op jit(solution)/shard_map/weight_grad/pallas_call | solution.py:606
  110.7 3.0 %collective-permute-done.28.theirs.refs_1_ = bf16[1024,128]{1,0:T(8,128)(2,1)S(1)} collective-permute-done((bf16[1024,128]{1,0:T(8,128)(2,1)S(1)}, bf16[1024,128]{1,0:T(8,128)(2,1)S(1)}, u32[]{:S(2)}, u32[]{:S(2)}) %collective-permute-start.28) | collective-permute-done | bytes 262176 | tf_op jit(solution)/shard_map/ppermute | solution.py:196
  115.3 2.4 %weight_grad.3 = (bf16[128,2688]{1,0:T(8,128)(2,1)S(1)}, bf16[128,2688]{1,0:T(8,128)(2,1)S(1)}) custom-call(s32[7]{0:T(128)S(1)} %stack.71.code, bf16[1024,128]{1,0:T(8,128)(2,1)S(1)} %multiply_convert_fusion.mine.refs_0_, bf16[1024,128]{1,0:T(8,128)(2,1)S(1)} %collective-permute-done.28.theirs.refs_1_, bf16[256,2688]{1,0:T(8,128)(2,1)S(1)} %copy-done, ...), custom_call_target="tpu_custom_call" | custom-call | flops 1409286144 | bytes 6881280 | tf_op jit(solution)/shard_map/weight_grad/pallas_call | solution.py:606
  120.7 2.3 %input_grad.2 = bf16[256,2688]{1,0:T(8,128)(2,1)S(1)} custom-call(s32[7]{0:T(128)S(1)} %stack.71.code, bf16[1024,128]{1,0:T(8,128)(2,1)S(1)} %multiply_convert_fusion.mine.refs_0_, bf16[1024,128]{1,0:T(8,128)(2,1)S(1)} %collective-permute-done.28.theirs.refs_1_, bf16[1024,128]{1,0:T(8,128)(2,1)S(1)} %collective-permute-done.31.refs_2_, ...), custom_call_target="tpu_custom_call" | custom-call | tf_op jit(solution)/shard_map/input_grad/pallas_call | solution.py:636
  131.8 2.3 %input_grad.3.refs_0_ = bf16[256,2688]{1,0:T(8,128)(2,1)S(1)} custom-call(s32[7]{0:T(128)S(1)} %stack.71.code, bf16[1024,128]{1,0:T(8,128)(2,1)S(1)} %multiply_convert_fusion.mine.refs_0_, bf16[1024,128]{1,0:T(8,128)(2,1)S(1)} %collective-permute-done.28.theirs.refs_1_, bf16[1024,128]{1,0:T(8,128)(2,1)S(1)} %collective-permute-done.31.refs_2_, ...), custom_call_target="tpu_custom_call" | custom-call | tf_op jit(solution)/shard_map/input_grad/pallas_call | solution.py:636
  134.2 2.3 %collective-permute-done.36.b = bf16[128,2688]{1,0:T(8,128)(2,1)S(1)} collective-permute-done((bf16[128,2688]{1,0:T(8,128)(2,1)S(1)}, bf16[128,2688]{1,0:T(8,128)(2,1)S(1)}, u32[]{:S(2)}, u32[]{:S(2)}) %collective-permute-start.36) | collective-permute-done | bytes 688160 | tf_op jit(solution)/shard_map/ppermute | solution.py:176
  136.5 9.9 %collective-permute-done.35.refs_1_ = bf16[128,2688]{1,0:T(8,128)(2,1)S(1)} collective-permute-done((bf16[128,2688]{1,0:T(8,128)(2,1)S(1)}, bf16[128,2688]{1,0:T(8,128)(2,1)S(1)}, u32[]{:S(2)}, u32[]{:S(2)}) %collective-permute-start.35) | collective-permute-done | bytes 688160 | tf_op jit(solution)/shard_map/ppermute | solution.py:176
  149.6 4.9 %collective-permute-done.39.refs_1_ = bf16[128,2688]{1,0:T(8,128)(2,1)S(1)} collective-permute-done((bf16[128,2688]{1,0:T(8,128)(2,1)S(1)}, bf16[128,2688]{1,0:T(8,128)(2,1)S(1)}, u32[]{:S(2)}, u32[]{:S(2)}) %collective-permute-start.39) | collective-permute-done | bytes 688160 | tf_op jit(solution)/shard_map/ppermute | solution.py:176
  161.0 3.4 %collective-permute-done.44.other = bf16[64,2688]{1,0:T(8,128)(2,1)S(1)} collective-permute-done((bf16[64,2688]{1,0:T(8,128)(2,1)S(1)}, bf16[64,2688]{1,0:T(8,128)(2,1)S(1)}, u32[]{:S(2)}, u32[]{:S(2)}) %collective-permute-start.44) | collective-permute-done | bytes 344096 | tf_op jit(solution)/shard_map/ppermute | solution.py:176
  168.0 3.8 %collective-permute-done.45.other = bf16[64,2688]{1,0:T(8,128)(2,1)S(1)} collective-permute-done((bf16[64,2688]{1,0:T(8,128)(2,1)S(1)}, bf16[64,2688]{1,0:T(8,128)(2,1)S(1)}, u32[]{:S(2)}, u32[]{:S(2)}) %collective-permute-start.45) | collective-permute-done | bytes 344096 | tf_op jit(solution)/shard_map/ppermute | solution.py:176
  (125 shorter events, 75.8 us)
Async XLA Ops:
  4.6 32.4 %collective-permute-start = (bf16[256,2688]{1,0:T(8,128)(2,1)}, bf16[256,2688]{1,0:T(8,128)(2,1)S(1)}, u32[]{:S(2)}, u32[]{:S(2)}) collective-permute-start(bf16[256,2688]{1,0:T(8,128)(2,1)} %a0.3), channel_id=1, source_target_pairs={{0,4},{2,6},{4,0},{6,2},{8,12},{10,14},{12,8},{14,10},{16,20},{18,... | collective-permute-start | bytes 4128776 | tf_op jit(solution)/shard_map/ppermute | solution.py:176
  8.2 12.2 %collective-permute-start.3 = (bf16[128,2688]{1,0:T(8,128)(2,1)}, bf16[128,2688]{1,0:T(8,128)(2,1)}, u32[]{:S(2)}, u32[]{:S(2)}) collective-permute-start(bf16[128,2688]{1,0:T(8,128)(2,1)} %pad_maximum_fusion.refs_4_), channel_id=1, source_target_pairs={{10,18},{14,22},{16,8},{20,12},{11,19},{15,23},{17,9},{21,13}} | collective-permute-start | bytes 2064392 | tf_op jit(solution)/shard_map/ppermute | solution.py:176
  9.4 12.2 %collective-permute-start.2 = (bf16[128,2688]{1,0:T(8,128)(2,1)}, bf16[128,2688]{1,0:T(8,128)(2,1)}, u32[]{:S(2)}, u32[]{:S(2)}) collective-permute-start(bf16[128,2688]{1,0:T(8,128)(2,1)} %pad_maximum_fusion.refs_4_), channel_id=1, source_target_pairs={{0,8},{4,12},{26,18},{30,22},{10,2},{14,6},{16,24},{20,28},{1,9},{... | collective-permute-start | bytes 2064392 | tf_op jit(solution)/shard_map/ppermute | solution.py:176
  10.8 17.5 %collective-permute-start.8 = (bf16[128,2688]{1,0:T(8,128)(2,1)S(1)}, bf16[128,2688]{1,0:T(8,128)(2,1)}, u32[]{:S(2)}, u32[]{:S(2)}) collective-permute-start(bf16[128,2688]{1,0:T(8,128)(2,1)S(1)} %pad_maximum_fusion.1.refs_4_), channel_id=1, source_target_pairs={{10,18},{14,22},{16,8},{20,12},{11,19},{15,23},{17,9},{21,13}} | collective-permute-start | bytes 2064392 | tf_op jit(solution)/shard_map/ppermute | solution.py:176
  12.1 17.0 %collective-permute-start.7 = (bf16[128,2688]{1,0:T(8,128)(2,1)S(1)}, bf16[128,2688]{1,0:T(8,128)(2,1)}, u32[]{:S(2)}, u32[]{:S(2)}) collective-permute-start(bf16[128,2688]{1,0:T(8,128)(2,1)S(1)} %pad_maximum_fusion.1.refs_4_), channel_id=1, source_target_pairs={{0,8},{4,12},{26,18},{30,22},{10,2},{14,6},{16,24},{20,28},{1,9},{... | collective-permute-start | bytes 2064392 | tf_op jit(solution)/shard_map/ppermute | solution.py:176
  21.6 12.9 %collective-permute-start.4 = (bf16[128,2688]{1,0:T(8,128)(2,1)}, bf16[128,2688]{1,0:T(8,128)(2,1)}, u32[]{:S(2)}, u32[]{:S(2)}) collective-permute-start(bf16[128,2688]{1,0:T(8,128)(2,1)} %collective-permute-done.2.refs_5_), channel_id=1, source_target_pairs={{8,16},{12,20},{18,10},{22,14},{9,17},{13,21},{19,11},{23,15}} | collective-permute-start | bytes 2064392 | tf_op jit(solution)/shard_map/ppermute | solution.py:176
  32.4 14.8 %collective-permute-start.12 = (bf16[128,2688]{1,0:T(8,128)(2,1)}, bf16[128,2688]{1,0:T(8,128)(2,1)}, u32[]{:S(2)}, u32[]{:S(2)}) collective-permute-start(bf16[128,2688]{1,0:T(8,128)(2,1)} %collective-permute-done.8.refs_6_), channel_id=1, source_target_pairs={{8,0},{12,4},{18,26},{22,30},{9,1},{13,5},{19,27},{23,31}} | collective-permute-start | bytes 2064392 | tf_op jit(solution)/shard_map/ppermute | solution.py:176
  34.5 16.3 %collective-permute-start.9 = (bf16[256,2688]{1,0:T(8,128)(2,1)S(1)}, bf16[256,2688]{1,0:T(8,128)(2,1)S(1)}, u32[]{:S(2)}, u32[]{:S(2)}) collective-permute-start(bf16[256,2688]{1,0:T(8,128)(2,1)S(1)} %copy-done), channel_id=1, source_target_pairs={{0,2},{2,0},{4,6},{6,4},{8,10},{10,8},{12,14},{14,12},{16,18},{18,... | collective-permute-start | bytes 4128776 | tf_op jit(solution)/shard_map/ppermute | solution.py:176
  36.2 14.7 %collective-permute-start.14 = (bf16[128,2688]{1,0:T(8,128)(2,1)}, bf16[128,2688]{1,0:T(8,128)(2,1)S(1)}, u32[]{:S(2)}, u32[]{:S(2)}) collective-permute-start(bf16[128,2688]{1,0:T(8,128)(2,1)} %collective-permute-done.4.refs_7_), channel_id=1, source_target_pairs={{16,24},{20,28},{10,2},{14,6},{17,25},{21,29},{11,3},{15,7}} | collective-permute-start | bytes 2064392 | tf_op jit(solution)/shard_map/ppermute | solution.py:176
  36.9 13.9 %collective-permute-start.10 = (bf16[256,2688]{1,0:T(8,128)(2,1)S(1)}, bf16[256,2688]{1,0:T(8,128)(2,1)S(1)}, u32[]{:S(2)}, u32[]{:S(2)}) collective-permute-start(bf16[256,2688]{1,0:T(8,128)(2,1)S(1)} %collective-permute-done.refs_2_.a2), channel_id=1, source_target_pairs={{0,2},{2,0},{4,6},{6,4},{8,10},{10,8},{12,14},{14,12},{16,18},{18,... | collective-permute-start | bytes 4128776 | tf_op jit(solution)/shard_map/ppermute | solution.py:176
  47.1 14.3 %collective-permute-start.13 = (bf16[128,2688]{1,0:T(8,128)(2,1)}, bf16[128,2688]{1,0:T(8,128)(2,1)S(1)}, u32[]{:S(2)}, u32[]{:S(2)}) collective-permute-start(bf16[128,2688]{1,0:T(8,128)(2,1)} %collective-permute-done.11.refs_7_), channel_id=1, source_target_pairs={{16,24},{20,28},{10,2},{14,6},{17,25},{21,29},{11,3},{15,7}} | collective-permute-start | bytes 2064392 | tf_op jit(solution)/shard_map/ppermute | solution.py:176
  49.2 12.3 %collective-permute-start.16 = (bf16[4,256,256]{2,1,0:T(8,128)(2,1)S(1)}, bf16[4,256,256]{2,1,0:T(8,128)(2,1)S(1)}, u32[]{:S(2)}, u32[]{:S(2)}) collective-permute-start(bf16[4,256,256]{2,1,0:T(8,128)(2,1)S(1)} %pad_maximum_fusion.2), channel_id=1, source_target_pairs={{0,4},{2,6},{4,0},{6,2},{8,12},{10,14},{12,8},{14,10},{16,20},{18,... | collective-permute-start | bytes 1572872 | tf_op jit(solution)/shard_map/ppermute | solution.py:176
  54.5 12.7 %collective-permute-start.18 = (bf16[1024,128]{1,0:T(8,128)(2,1)S(1)}, bf16[1024,128]{1,0:T(8,128)(2,1)S(1)}, u32[]{:S(2)}, u32[]{:S(2)}) collective-permute-start(bf16[1024,128]{1,0:T(8,128)(2,1)S(1)} %get-tuple-element.86), channel_id=1, source_target_pairs={{0,1},{1,0},{2,3},{3,2},{4,5},{5,4},{6,7},{7,6},{8,9},{9,8},{10,11... | collective-permute-start | bytes 786440 | tf_op jit(solution)/shard_map/ppermute | solution.py:196
  66.6 20.2 %collective-permute-start.22 = (bf16[256,2688]{1,0:T(8,128)(2,1)S(1)}, bf16[256,2688]{1,0:T(8,128)(2,1)S(1)}, u32[]{:S(2)}, u32[]{:S(2)}) collective-permute-start(bf16[256,2688]{1,0:T(8,128)(2,1)S(1)} %get-tuple-element.100.refs_10_), channel_id=1, source_target_pairs={{0,2},{2,0},{4,6},{6,4},{8,10},{10,8},{12,14},{14,12},{16,18},{18,... | collective-permute-start | bytes 4128776 | tf_op jit(solution)/shard_map/ppermute | solution.py:176
  67.1 19.7 %collective-permute-start.21 = (bf16[256,2688]{1,0:T(8,128)(2,1)S(1)}, bf16[256,2688]{1,0:T(8,128)(2,1)S(1)}, u32[]{:S(2)}, u32[]{:S(2)}) collective-permute-start(bf16[256,2688]{1,0:T(8,128)(2,1)S(1)} %get-tuple-element.99.refs_8_), channel_id=1, source_target_pairs={{0,2},{2,0},{4,6},{6,4},{8,10},{10,8},{12,14},{14,12},{16,18},{18,... | collective-permute-start | bytes 4128776 | tf_op jit(solution)/shard_map/ppermute | solution.py:176
  72.2 14.6 %collective-permute-start.20 = (bf16[1024,128]{1,0:T(8,128)(2,1)S(1)}, bf16[1024,128]{1,0:T(8,128)(2,1)S(1)}, u32[]{:S(2)}, u32[]{:S(2)}) collective-permute-start(bf16[1024,128]{1,0:T(8,128)(2,1)S(1)} %add_convert_fusion.1.v_own), channel_id=1, source_target_pairs={{0,8},{4,12},{2,10},{6,14},{8,16},{12,20},{10,18},{14,22},{16,24},... | collective-permute-start | bytes 786440 | tf_op jit(solution)/shard_map/ppermute | solution.py:176
  98.0 20.5 %collective-permute-start.24 = (bf16[2,2,256,256]{3,2,1,0:T(8,128)(2,1)S(1)}, bf16[2,2,256,256]{3,2,1,0:T(8,128)(2,1)S(1)}, u32[]{:S(2)}, u32[]{:S(2)}) collective-permute-start(bf16[2,2,256,256]{3,2,1,0:T(8,128)(2,1)S(1)} %pack.1), channel_id=1, source_target_pairs={{0,4},{2,6},{4,0},{6,2},{8,12},{10,14},{12,8},{14,10},{16,20},{18,... | collective-permute-start | bytes 1572872 | tf_op jit(solution)/shard_map/ppermute | solution.py:176
  107.2 16.9 %collective-permute-start.29 = (bf16[128,2688]{1,0:T(8,128)(2,1)S(1)}, bf16[128,2688]{1,0:T(8,128)(2,1)S(1)}, u32[]{:S(2)}, u32[]{:S(2)}) collective-permute-start(bf16[128,2688]{1,0:T(8,128)(2,1)S(1)} %get-tuple-element.115.refs_2_.a), channel_id=1, source_target_pairs={{24,16},{28,20},{2,10},{6,14},{25,17},{29,21},{3,11},{7,15}} | collective-permute-start | bytes 2064392 | tf_op jit(solution)/shard_map/ppermute | solution.py:176
  107.9 18.2 %collective-permute-start.30 = (bf16[128,2688]{1,0:T(8,128)(2,1)S(1)}, bf16[128,2688]{1,0:T(8,128)(2,1)S(1)}, u32[]{:S(2)}, u32[]{:S(2)}) collective-permute-start(bf16[128,2688]{1,0:T(8,128)(2,1)S(1)} %get-tuple-element.111.refs_0_), channel_id=1, source_target_pairs={{0,8},{4,12},{26,18},{30,22},{1,9},{5,13},{27,19},{31,23}} | collective-permute-start | bytes 2064392 | tf_op jit(solution)/shard_map/ppermute | solution.py:176
  123.0 34.4 %collective-permute-start.38 = (bf16[256,2688]{1,0:T(8,128)(2,1)S(1)}, bf16[256,2688]{1,0:T(8,128)(2,1)S(1)}, u32[]{:S(2)}, u32[]{:S(2)}) collective-permute-start(bf16[256,2688]{1,0:T(8,128)(2,1)S(1)} %input_grad.2), channel_id=1, source_target_pairs={{0,4},{2,6},{4,0},{6,2},{8,12},{10,14},{12,8},{14,10},{16,20},{18,... | collective-permute-start | bytes 4128776 | tf_op jit(solution)/shard_map/ppermute | solution.py:176
  127.7 18.7 %collective-permute-start.35 = (bf16[128,2688]{1,0:T(8,128)(2,1)S(1)}, bf16[128,2688]{1,0:T(8,128)(2,1)S(1)}, u32[]{:S(2)}, u32[]{:S(2)}) collective-permute-start(bf16[128,2688]{1,0:T(8,128)(2,1)S(1)} %get-tuple-element.120), channel_id=1, source_target_pairs={{16,8},{20,12},{10,18},{14,22},{17,9},{21,13},{11,19},{15,23}} | collective-permute-start | bytes 2064392 | tf_op jit(solution)/shard_map/ppermute | solution.py:176
  129.2 25.2 %collective-permute-start.39 = (bf16[128,2688]{1,0:T(8,128)(2,1)S(1)}, bf16[128,2688]{1,0:T(8,128)(2,1)S(1)}, u32[]{:S(2)}, u32[]{:S(2)}) collective-permute-start(bf16[128,2688]{1,0:T(8,128)(2,1)S(1)} %sums.6), channel_id=1, source_target_pairs={{16,8},{20,12},{10,18},{14,22},{17,9},{21,13},{11,19},{15,23}} | collective-permute-start | bytes 2064392 | tf_op jit(solution)/shard_map/ppermute | solution.py:176
  130.5 23.9 %collective-permute-start.40 = (bf16[128,2688]{1,0:T(8,128)(2,1)S(1)}, bf16[128,2688]{1,0:T(8,128)(2,1)S(1)}, u32[]{:S(2)}, u32[]{:S(2)}) collective-permute-start(bf16[128,2688]{1,0:T(8,128)(2,1)S(1)} %get-tuple-element.129.refs_0_), channel_id=1, source_target_pairs={{0,8},{4,12},{26,18},{30,22},{1,9},{5,13},{27,19},{31,23}} | collective-permute-start | bytes 2064392 | tf_op jit(solution)/shard_map/ppermute | solution.py:176
  146.6 12.3 %collective-permute-start.43 = (bf16[128,2688]{1,0:T(8,128)(2,1)S(1)}, bf16[128,2688]{1,0:T(8,128)(2,1)S(1)}, u32[]{:S(2)}, u32[]{:S(2)}) collective-permute-start(bf16[128,2688]{1,0:T(8,128)(2,1)S(1)} %sums.7), channel_id=1, source_target_pairs={{8,0},{12,4},{18,26},{22,30},{2,10},{6,14},{24,16},{28,20},{9,1},{... | collective-permute-start | bytes 2064392 | tf_op jit(solution)/shard_map/ppermute | solution.py:176
  (28 other events, 259.8 us)

commit v6 on v5

--- a/solution.py
+++ b/solution.py
@@ -196,12 +196,12 @@
     return lax.ppermute(array, "uly", [(0, 1), (1, 0)])
 
 
-def call(kernel, out_shape, vmem, flops=0, accessed=0, **rest):
+def call(kernel, out_shape, vmem, **rest):
     return pl.pallas_call(
         kernel,
         out_shape=out_shape,
         compiler_params=pltpu.CompilerParams(vmem_limit_bytes=vmem * MIB),
-        cost_estimate=pl.CostEstimate(flops=flops, bytes_accessed=accessed, transcendentals=0),
+        cost_estimate=pl.CostEstimate(flops=0, bytes_accessed=0, transcendentals=0),
         **rest,
     )
 
@@ -607,8 +607,6 @@
         weight_grad_kernel,
         [shaped((width, features)), shaped((width, features))],
         12,
-        2 * 4 * rows * features * 2 * width,
-        4 * rows * features * 2 + 2 * width * features * 2,
         in_specs=[SMEM] + [VMEM] * 6,
         out_specs=[VMEM, VMEM],
         name="weight_grad",

time: 174 us -> 174 us (level)
  no operation moved by 1% of the time
where the time goes in v6:
time: 174 us; the launch traced here: 173 us
  waiting for transfers between devices  63.6 us (37%)
  starting transfers between devices  62.2 us (36%)
  Pallas kernels  38.8 us (22%)
  other arithmetic  5.18 us (3%)
  local copies, waits for them, and re-layouts  2.05 us (1%)
    ppermute x42, starting transfers between devices, move(): return lax.ppermute(array, 'seq', [(at(*a), at(*b)) for a, b in rule])  58.7 us
    ppermute x42, waiting for transfers between devices, move(): return lax.ppermute(array, 'seq', [(at(*a), at(*b)) for a, b in rule])  53.7 us
    ppermute x4, waiting for transfers between devices, swap_uly(): return lax.ppermute(array, 'uly', [(0, 1), (1, 0)])  9.95 us
    pallas_call x2, Pallas kernels, project(): call(project_kernel, [shaped((4 * rows, width)), shaped((4 * rows, width)...  7.17 us
    pallas_call x1, Pallas kernels, attend_values(): call(values_kernel, [shaped((2, 2, rows, 2 * HD)), shaped((2, 2, rows, 2...  7.03 us
    pallas_call x1, Pallas kernels, attend_scores(): call(scores_kernel, [shaped((blocks, span, 2 * rows)), shaped((blocks, 8,...  6.45 us
    pallas_call x2, Pallas kernels, weight_grad(): call(weight_grad_kernel, [shaped((width, features)), shaped((width, featu...  4.81 us
    pallas_call x2, Pallas kernels, input_grad(): call(functools.partial(input_grad_kernel, piece), shaped((rows, features)...  4.69 us
  transfers between devices with their start and end apart: 46, of which 22 were waited for; matrix products, arithmetic and copies ran while one was open for 4% of the time, Pallas kernels for 21%

profile of v6, /device:TPU:17, one launch (start us, length us, event | category | flops | bytes accessed | tf_op | source)
XLA Modules:
  0.0 173.2 jit_solution(3863192920710538610)
XLA Ops:
  0.6 2.6 %collective-permute-start.6 = (bf16[64,2688]{1,0:T(8,128)(2,1)}, bf16[64,2688]{1,0:T(8,128)(2,1)S(1)}, u32[]{:S(2)}, u32[]{:S(2)}) collective-permute-start(bf16[64,2688]{1,0:T(8,128)(2,1)} %bitcast.36), channel_id=1, source_target_pairs={{2,0},{6,4},{8,10},{12,14},{18,16},{22,20},{24,26},{28,30},{3,1},{... | collective-permute-start | bytes 1032200 | tf_op jit(solution)/shard_map/ppermute | solution.py:176
  15.5 4.9 %collective-permute-done.3.refs_6_ = bf16[128,2688]{1,0:T(8,128)(2,1)} collective-permute-done((bf16[128,2688]{1,0:T(8,128)(2,1)}, bf16[128,2688]{1,0:T(8,128)(2,1)}, u32[]{:S(2)}, u32[]{:S(2)}) %collective-permute-start.3) | collective-permute-done | bytes 688160 | tf_op jit(solution)/shard_map/ppermute | solution.py:176
  21.6 3.0 %collective-permute-start.4 = (bf16[128,2688]{1,0:T(8,128)(2,1)}, bf16[128,2688]{1,0:T(8,128)(2,1)}, u32[]{:S(2)}, u32[]{:S(2)}) collective-permute-start(bf16[128,2688]{1,0:T(8,128)(2,1)} %collective-permute-done.2.refs_5_), channel_id=1, source_target_pairs={{8,16},{12,20},{18,10},{22,14},{9,17},{13,21},{19,11},{23,15}} | collective-permute-start | bytes 2064392 | tf_op jit(solution)/shard_map/ppermute | solution.py:176
  29.1 3.3 %collective-permute-start.11 = (bf16[128,2688]{1,0:T(8,128)(2,1)}, bf16[128,2688]{1,0:T(8,128)(2,1)}, u32[]{:S(2)}, u32[]{:S(2)}) collective-permute-start(bf16[128,2688]{1,0:T(8,128)(2,1)} %collective-permute-done.7.refs_5_), channel_id=1, source_target_pairs={{8,16},{12,20},{18,10},{22,14},{9,17},{13,21},{19,11},{23,15}} | collective-permute-start | bytes 2064392 | tf_op jit(solution)/shard_map/ppermute | solution.py:176
  40.9 6.2 %collective-permute-done.12.refs_8_ = bf16[128,2688]{1,0:T(8,128)(2,1)} collective-permute-done((bf16[128,2688]{1,0:T(8,128)(2,1)}, bf16[128,2688]{1,0:T(8,128)(2,1)}, u32[]{:S(2)}, u32[]{:S(2)}) %collective-permute-start.12) | collective-permute-done | bytes 688160 | tf_op jit(solution)/shard_map/ppermute | solution.py:176
  50.9 3.6 %project.2 = (bf16[1024,128]{1,0:T(8,128)(2,1)S(1)}, bf16[1024,128]{1,0:T(8,128)(2,1)S(1)}, bf16[256,2688]{1,0:T(8,128)(2,1)S(1)}) custom-call(s32[7]{0:T(128)S(1)} %stack.71.code, bf16[256,2688]{1,0:T(8,128)(2,1)S(1)} %copy-done, bf16[256,2688]{1,0:T(8,128)(2,1)S(1)} %collective-permute-done.9.refs_1_.a1, ...), custom_call_target="tpu_custom_call" | custom-call | tf_op jit(solution)/shard_map/project/pallas_call | solution.py:360
  55.8 5.7 %collective-permute-done.16 = bf16[4,256,256]{2,1,0:T(8,128)(2,1)S(1)} collective-permute-done((bf16[4,256,256]{2,1,0:T(8,128)(2,1)S(1)}, bf16[4,256,256]{2,1,0:T(8,128)(2,1)S(1)}, u32[]{:S(2)}, u32[]{:S(2)}) %collective-permute-start.16) | collective-permute-done | bytes 524320 | tf_op jit(solution)/shard_map/ppermute | solution.py:176
  61.5 3.6 %project.3 = (bf16[1024,128]{1,0:T(8,128)(2,1)S(1)}, bf16[1024,128]{1,0:T(8,128)(2,1)S(1)}, bf16[256,2688]{1,0:T(8,128)(2,1)S(1)}) custom-call(s32[7]{0:T(128)S(1)} %stack.71.code, bf16[256,2688]{1,0:T(8,128)(2,1)S(1)} %copy-done, bf16[256,2688]{1,0:T(8,128)(2,1)S(1)} %collective-permute-done.9.refs_1_.a1, ...), custom_call_target="tpu_custom_call" | custom-call | tf_op jit(solution)/shard_map/project/pallas_call | solution.py:360
  69.6 2.5 %collective-permute-done.15 = bf16[1024,128]{1,0:T(8,128)(2,1)S(1)} collective-permute-done((bf16[1024,128]{1,0:T(8,128)(2,1)S(1)}, bf16[1024,128]{1,0:T(8,128)(2,1)S(1)}, u32[]{:S(2)}, u32[]{:S(2)}) %collective-permute-start.15) | collective-permute-done | bytes 262176 | tf_op jit(solution)/shard_map/ppermute | solution.py:196
  74.2 2.7 %collective-permute-done.19.before_ref = bf16[1024,128]{1,0:T(8,128)(2,1)S(1)} collective-permute-done((bf16[1024,128]{1,0:T(8,128)(2,1)S(1)}, bf16[1024,128]{1,0:T(8,128)(2,1)S(1)}, u32[]{:S(2)}, u32[]{:S(2)}) %collective-permute-start.19) | collective-permute-done | bytes 262176 | tf_op jit(solution)/shard_map/ppermute | solution.py:176
  77.0 6.4 %attend_scores.1 = (bf16[4,1280,512]{2,1,0:T(8,128)(2,1)S(1)}, f32[4,8,512]{2,1,0:T(8,128)S(1)}, f32[1024,128]{1,0:T(8,128)S(1)}, bf16[1024,128]{1,0:T(8,128)(2,1)S(1)}) custom-call(s32[7]{0:T(128)S(1)} %stack.71.code, bf16[4,256,256]{2,1,0:T(8,128)(2,1)S(1)} %pad_maximum_fusion.4.q_ref, bf16[4,256,256]{2,1,0:T(8,128)(2,1)S(1)} %pad_maximum_fusion.5.go_ref, ...), custom_call_target="tpu_custom_call" | custom-call | tf_op jit(solution)/shard_map/attend_scores/pallas_call | solution.py:448
  83.4 3.3 %collective-permute-start.26 = (bf16[1024,128]{1,0:T(8,128)(2,1)S(1)}, bf16[1024,128]{1,0:T(8,128)(2,1)S(1)}, u32[]{:S(2)}, u32[]{:S(2)}) collective-permute-start(bf16[1024,128]{1,0:T(8,128)(2,1)S(1)} %get-tuple-element.108), channel_id=1, source_target_pairs={{8,0},{12,4},{10,2},{14,6},{16,8},{20,12},{18,10},{22,14},{24,16},... | collective-permute-start | bytes 786440 | tf_op jit(solution)/shard_map/ppermute | solution.py:176
  86.8 7.0 %attend_values.1 = (bf16[2,2,256,256]{3,2,1,0:T(8,128)(2,1)S(1)}, bf16[2,2,256,256]{3,2,1,0:T(8,128)(2,1)S(1)}, f32[1024,128]{1,0:T(8,128)S(1)}, bf16[1024,128]{1,0:T(8,128)(2,1)S(1)}) custom-call(s32[7]{0:T(128)S(1)} %stack.71.code, bf16[4,256,256]{2,1,0:T(8,128)(2,1)S(1)} %pad_maximum_fusion.4.q_ref, bf16[4,256,256]{2,1,0:T(8,128)(2,1)S(1)} %pad_maximum_fusion.5.go_ref, ...), custom_call_target="tpu_custom_call" | custom-call | tf_op jit(solution)/shard_map/attend_values/pallas_call | solution.py:545
  99.0 4.5 %collective-permute-done.27.theirs.refs_5_ = bf16[1024,128]{1,0:T(8,128)(2,1)S(1)} collective-permute-done((bf16[1024,128]{1,0:T(8,128)(2,1)S(1)}, bf16[1024,128]{1,0:T(8,128)(2,1)S(1)}, u32[]{:S(2)}, u32[]{:S(2)}) %collective-permute-start.27) | collective-permute-done | bytes 262176 | tf_op jit(solution)/shard_map/ppermute | solution.py:196
  103.5 2.4 %weight_grad.2 = (bf16[128,2688]{1,0:T(8,128)(2,1)S(1)}, bf16[128,2688]{1,0:T(8,128)(2,1)S(1)}) custom-call(s32[7]{0:T(128)S(1)} %stack.71.code, bf16[1024,128]{1,0:T(8,128)(2,1)S(1)} %add_convert_fusion.mine.refs_4_, bf16[1024,128]{1,0:T(8,128)(2,1)S(1)} %collective-permute-done.27.theirs.refs_5_, bf16[256,2688]{1,0:T(8,128)(2,1)S(1)} %copy-done, ...), custom_call_target="tpu_custom_call" | custom-call | tf_op jit(solution)/shard_map/weight_grad/pallas_call | solution.py:606
  110.7 3.0 %collective-permute-done.28.theirs.refs_1_ = bf16[1024,128]{1,0:T(8,128)(2,1)S(1)} collective-permute-done((bf16[1024,128]{1,0:T(8,128)(2,1)S(1)}, bf16[1024,128]{1,0:T(8,128)(2,1)S(1)}, u32[]{:S(2)}, u32[]{:S(2)}) %collective-permute-start.28) | collective-permute-done | bytes 262176 | tf_op jit(solution)/shard_map/ppermute | solution.py:196
  115.3 2.4 %weight_grad.3 = (bf16[128,2688]{1,0:T(8,128)(2,1)S(1)}, bf16[128,2688]{1,0:T(8,128)(2,1)S(1)}) custom-call(s32[7]{0:T(128)S(1)} %stack.71.code, bf16[1024,128]{1,0:T(8,128)(2,1)S(1)} %multiply_convert_fusion.mine.refs_0_, bf16[1024,128]{1,0:T(8,128)(2,1)S(1)} %collective-permute-done.28.theirs.refs_1_, bf16[256,2688]{1,0:T(8,128)(2,1)S(1)} %copy-done, ...), custom_call_target="tpu_custom_call" | custom-call | tf_op jit(solution)/shard_map/weight_grad/pallas_call | solution.py:606
  120.7 2.3 %input_grad.2 = bf16[256,2688]{1,0:T(8,128)(2,1)S(1)} custom-call(s32[7]{0:T(128)S(1)} %stack.71.code, bf16[1024,128]{1,0:T(8,128)(2,1)S(1)} %multiply_convert_fusion.mine.refs_0_, bf16[1024,128]{1,0:T(8,128)(2,1)S(1)} %collective-permute-done.28.theirs.refs_1_, bf16[1024,128]{1,0:T(8,128)(2,1)S(1)} %collective-permute-done.31.refs_2_, ...), custom_call_target="tpu_custom_call" | custom-call | tf_op jit(solution)/shard_map/input_grad/pallas_call | solution.py:634
  131.8 2.3 %input_grad.3.refs_0_ = bf16[256,2688]{1,0:T(8,128)(2,1)S(1)} custom-call(s32[7]{0:T(128)S(1)} %stack.71.code, bf16[1024,128]{1,0:T(8,128)(2,1)S(1)} %multiply_convert_fusion.mine.refs_0_, bf16[1024,128]{1,0:T(8,128)(2,1)S(1)} %collective-permute-done.28.theirs.refs_1_, bf16[1024,128]{1,0:T(8,128)(2,1)S(1)} %collective-permute-done.31.refs_2_, ...), custom_call_target="tpu_custom_call" | custom-call | tf_op jit(solution)/shard_map/input_grad/pallas_call | solution.py:634
  134.2 2.3 %collective-permute-done.36.b = bf16[128,2688]{1,0:T(8,128)(2,1)S(1)} collective-permute-done((bf16[128,2688]{1,0:T(8,128)(2,1)S(1)}, bf16[128,2688]{1,0:T(8,128)(2,1)S(1)}, u32[]{:S(2)}, u32[]{:S(2)}) %collective-permute-start.36) | collective-permute-done | bytes 688160 | tf_op jit(solution)/shard_map/ppermute | solution.py:176
  136.5 9.9 %collective-permute-done.35.refs_1_ = bf16[128,2688]{1,0:T(8,128)(2,1)S(1)} collective-permute-done((bf16[128,2688]{1,0:T(8,128)(2,1)S(1)}, bf16[128,2688]{1,0:T(8,128)(2,1)S(1)}, u32[]{:S(2)}, u32[]{:S(2)}) %collective-permute-start.35) | collective-permute-done | bytes 688160 | tf_op jit(solution)/shard_map/ppermute | solution.py:176
  149.6 4.9 %collective-permute-done.39.refs_1_ = bf16[128,2688]{1,0:T(8,128)(2,1)S(1)} collective-permute-done((bf16[128,2688]{1,0:T(8,128)(2,1)S(1)}, bf16[128,2688]{1,0:T(8,128)(2,1)S(1)}, u32[]{:S(2)}, u32[]{:S(2)}) %collective-permute-start.39) | collective-permute-done | bytes 688160 | tf_op jit(solution)/shard_map/ppermute | solution.py:176
  161.0 3.4 %collective-permute-done.44.other = bf16[64,2688]{1,0:T(8,128)(2,1)S(1)} collective-permute-done((bf16[64,2688]{1,0:T(8,128)(2,1)S(1)}, bf16[64,2688]{1,0:T(8,128)(2,1)S(1)}, u32[]{:S(2)}, u32[]{:S(2)}) %collective-permute-start.44) | collective-permute-done | bytes 344096 | tf_op jit(solution)/shard_map/ppermute | solution.py:176
  168.0 3.8 %collective-permute-done.45.other = bf16[64,2688]{1,0:T(8,128)(2,1)S(1)} collective-permute-done((bf16[64,2688]{1,0:T(8,128)(2,1)S(1)}, bf16[64,2688]{1,0:T(8,128)(2,1)S(1)}, u32[]{:S(2)}, u32[]{:S(2)}) %collective-permute-start.45) | collective-permute-done | bytes 344096 | tf_op jit(solution)/shard_map/ppermute | solution.py:176
  (125 shorter events, 75.8 us)
Async XLA Ops:
  4.6 32.4 %collective-permute-start = (bf16[256,2688]{1,0:T(8,128)(2,1)}, bf16[256,2688]{1,0:T(8,128)(2,1)S(1)}, u32[]{:S(2)}, u32[]{:S(2)}) collective-permute-start(bf16[256,2688]{1,0:T(8,128)(2,1)} %a0.3), channel_id=1, source_target_pairs={{0,4},{2,6},{4,0},{6,2},{8,12},{10,14},{12,8},{14,10},{16,20},{18,... | collective-permute-start | bytes 4128776 | tf_op jit(solution)/shard_map/ppermute | solution.py:176
  8.2 12.2 %collective-permute-start.3 = (bf16[128,2688]{1,0:T(8,128)(2,1)}, bf16[128,2688]{1,0:T(8,128)(2,1)}, u32[]{:S(2)}, u32[]{:S(2)}) collective-permute-start(bf16[128,2688]{1,0:T(8,128)(2,1)} %pad_maximum_fusion.refs_4_), channel_id=1, source_target_pairs={{10,18},{14,22},{16,8},{20,12},{11,19},{15,23},{17,9},{21,13}} | collective-permute-start | bytes 2064392 | tf_op jit(solution)/shard_map/ppermute | solution.py:176
  9.4 12.2 %collective-permute-start.2 = (bf16[128,2688]{1,0:T(8,128)(2,1)}, bf16[128,2688]{1,0:T(8,128)(2,1)}, u32[]{:S(2)}, u32[]{:S(2)}) collective-permute-start(bf16[128,2688]{1,0:T(8,128)(2,1)} %pad_maximum_fusion.refs_4_), channel_id=1, source_target_pairs={{0,8},{4,12},{26,18},{30,22},{10,2},{14,6},{16,24},{20,28},{1,9},{... | collective-permute-start | bytes 2064392 | tf_op jit(solution)/shard_map/ppermute | solution.py:176
  10.8 17.5 %collective-permute-start.8 = (bf16[128,2688]{1,0:T(8,128)(2,1)S(1)}, bf16[128,2688]{1,0:T(8,128)(2,1)}, u32[]{:S(2)}, u32[]{:S(2)}) collective-permute-start(bf16[128,2688]{1,0:T(8,128)(2,1)S(1)} %pad_maximum_fusion.1.refs_4_), channel_id=1, source_target_pairs={{10,18},{14,22},{16,8},{20,12},{11,19},{15,23},{17,9},{21,13}} | collective-permute-start | bytes 2064392 | tf_op jit(solution)/shard_map/ppermute | solution.py:176
  12.1 17.0 %collective-permute-start.7 = (bf16[128,2688]{1,0:T(8,128)(2,1)S(1)}, bf16[128,2688]{1,0:T(8,128)(2,1)}, u32[]{:S(2)}, u32[]{:S(2)}) collective-permute-start(bf16[128,2688]{1,0:T(8,128)(2,1)S(1)} %pad_maximum_fusion.1.refs_4_), channel_id=1, source_target_pairs={{0,8},{4,12},{26,18},{30,22},{10,2},{14,6},{16,24},{20,28},{1,9},{... | collective-permute-start | bytes 2064392 | tf_op jit(solution)/shard_map/ppermute | solution.py:176
  21.6 12.9 %collective-permute-start.4 = (bf16[128,2688]{1,0:T(8,128)(2,1)}, bf16[128,2688]{1,0:T(8,128)(2,1)}, u32[]{:S(2)}, u32[]{:S(2)}) collective-permute-start(bf16[128,2688]{1,0:T(8,128)(2,1)} %collective-permute-done.2.refs_5_), channel_id=1, source_target_pairs={{8,16},{12,20},{18,10},{22,14},{9,17},{13,21},{19,11},{23,15}} | collective-permute-start | bytes 2064392 | tf_op jit(solution)/shard_map/ppermute | solution.py:176
  32.4 14.8 %collective-permute-start.12 = (bf16[128,2688]{1,0:T(8,128)(2,1)}, bf16[128,2688]{1,0:T(8,128)(2,1)}, u32[]{:S(2)}, u32[]{:S(2)}) collective-permute-start(bf16[128,2688]{1,0:T(8,128)(2,1)} %collective-permute-done.8.refs_6_), channel_id=1, source_target_pairs={{8,0},{12,4},{18,26},{22,30},{9,1},{13,5},{19,27},{23,31}} | collective-permute-start | bytes 2064392 | tf_op jit(solution)/shard_map/ppermute | solution.py:176
  34.5 16.3 %collective-permute-start.9 = (bf16[256,2688]{1,0:T(8,128)(2,1)S(1)}, bf16[256,2688]{1,0:T(8,128)(2,1)S(1)}, u32[]{:S(2)}, u32[]{:S(2)}) collective-permute-start(bf16[256,2688]{1,0:T(8,128)(2,1)S(1)} %copy-done), channel_id=1, source_target_pairs={{0,2},{2,0},{4,6},{6,4},{8,10},{10,8},{12,14},{14,12},{16,18},{18,... | collective-permute-start | bytes 4128776 | tf_op jit(solution)/shard_map/ppermute | solution.py:176
  36.2 14.7 %collective-permute-start.14 = (bf16[128,2688]{1,0:T(8,128)(2,1)}, bf16[128,2688]{1,0:T(8,128)(2,1)S(1)}, u32[]{:S(2)}, u32[]{:S(2)}) collective-permute-start(bf16[128,2688]{1,0:T(8,128)(2,1)} %collective-permute-done.4.refs_7_), channel_id=1, source_target_pairs={{16,24},{20,28},{10,2},{14,6},{17,25},{21,29},{11,3},{15,7}} | collective-permute-start | bytes 2064392 | tf_op jit(solution)/shard_map/ppermute | solution.py:176
  36.9 13.9 %collective-permute-start.10 = (bf16[256,2688]{1,0:T(8,128)(2,1)S(1)}, bf16[256,2688]{1,0:T(8,128)(2,1)S(1)}, u32[]{:S(2)}, u32[]{:S(2)}) collective-permute-start(bf16[256,2688]{1,0:T(8,128)(2,1)S(1)} %collective-permute-done.refs_2_.a2), channel_id=1, source_target_pairs={{0,2},{2,0},{4,6},{6,4},{8,10},{10,8},{12,14},{14,12},{16,18},{18,... | collective-permute-start | bytes 4128776 | tf_op jit(solution)/shard_map/ppermute | solution.py:176
  47.1 14.3 %collective-permute-start.13 = (bf16[128,2688]{1,0:T(8,128)(2,1)}, bf16[128,2688]{1,0:T(8,128)(2,1)S(1)}, u32[]{:S(2)}, u32[]{:S(2)}) collective-permute-start(bf16[128,2688]{1,0:T(8,128)(2,1)} %collective-permute-done.11.refs_7_), channel_id=1, source_target_pairs={{16,24},{20,28},{10,2},{14,6},{17,25},{21,29},{11,3},{15,7}} | collective-permute-start | bytes 2064392 | tf_op jit(solution)/shard_map/ppermute | solution.py:176
  49.2 12.3 %collective-permute-start.16 = (bf16[4,256,256]{2,1,0:T(8,128)(2,1)S(1)}, bf16[4,256,256]{2,1,0:T(8,128)(2,1)S(1)}, u32[]{:S(2)}, u32[]{:S(2)}) collective-permute-start(bf16[4,256,256]{2,1,0:T(8,128)(2,1)S(1)} %pad_maximum_fusion.2), channel_id=1, source_target_pairs={{0,4},{2,6},{4,0},{6,2},{8,12},{10,14},{12,8},{14,10},{16,20},{18,... | collective-permute-start | bytes 1572872 | tf_op jit(solution)/shard_map/ppermute | solution.py:176
  54.5 12.7 %collective-permute-start.18 = (bf16[1024,128]{1,0:T(8,128)(2,1)S(1)}, bf16[1024,128]{1,0:T(8,128)(2,1)S(1)}, u32[]{:S(2)}, u32[]{:S(2)}) collective-permute-start(bf16[1024,128]{1,0:T(8,128)(2,1)S(1)} %get-tuple-element.86), channel_id=1, source_target_pairs={{0,1},{1,0},{2,3},{3,2},{4,5},{5,4},{6,7},{7,6},{8,9},{9,8},{10,11... | collective-permute-start | bytes 786440 | tf_op jit(solution)/shard_map/ppermute | solution.py:196
  66.6 20.2 %collective-permute-start.22 = (bf16[256,2688]{1,0:T(8,128)(2,1)S(1)}, bf16[256,2688]{1,0:T(8,128)(2,1)S(1)}, u32[]{:S(2)}, u32[]{:S(2)}) collective-permute-start(bf16[256,2688]{1,0:T(8,128)(2,1)S(1)} %get-tuple-element.100.refs_10_), channel_id=1, source_target_pairs={{0,2},{2,0},{4,6},{6,4},{8,10},{10,8},{12,14},{14,12},{16,18},{18,... | collective-permute-start | bytes 4128776 | tf_op jit(solution)/shard_map/ppermute | solution.py:176
  67.1 19.7 %collective-permute-start.21 = (bf16[256,2688]{1,0:T(8,128)(2,1)S(1)}, bf16[256,2688]{1,0:T(8,128)(2,1)S(1)}, u32[]{:S(2)}, u32[]{:S(2)}) collective-permute-start(bf16[256,2688]{1,0:T(8,128)(2,1)S(1)} %get-tuple-element.99.refs_8_), channel_id=1, source_target_pairs={{0,2},{2,0},{4,6},{6,4},{8,10},{10,8},{12,14},{14,12},{16,18},{18,... | collective-permute-start | bytes 4128776 | tf_op jit(solution)/shard_map/ppermute | solution.py:176
  72.2 14.6 %collective-permute-start.20 = (bf16[1024,128]{1,0:T(8,128)(2,1)S(1)}, bf16[1024,128]{1,0:T(8,128)(2,1)S(1)}, u32[]{:S(2)}, u32[]{:S(2)}) collective-permute-start(bf16[1024,128]{1,0:T(8,128)(2,1)S(1)} %add_convert_fusion.1.v_own), channel_id=1, source_target_pairs={{0,8},{4,12},{2,10},{6,14},{8,16},{12,20},{10,18},{14,22},{16,24},... | collective-permute-start | bytes 786440 | tf_op jit(solution)/shard_map/ppermute | solution.py:176
  98.0 20.5 %collective-permute-start.24 = (bf16[2,2,256,256]{3,2,1,0:T(8,128)(2,1)S(1)}, bf16[2,2,256,256]{3,2,1,0:T(8,128)(2,1)S(1)}, u32[]{:S(2)}, u32[]{:S(2)}) collective-permute-start(bf16[2,2,256,256]{3,2,1,0:T(8,128)(2,1)S(1)} %pack.1), channel_id=1, source_target_pairs={{0,4},{2,6},{4,0},{6,2},{8,12},{10,14},{12,8},{14,10},{16,20},{18,... | collective-permute-start | bytes 1572872 | tf_op jit(solution)/shard_map/ppermute | solution.py:176
  107.2 16.9 %collective-permute-start.29 = (bf16[128,2688]{1,0:T(8,128)(2,1)S(1)}, bf16[128,2688]{1,0:T(8,128)(2,1)S(1)}, u32[]{:S(2)}, u32[]{:S(2)}) collective-permute-start(bf16[128,2688]{1,0:T(8,128)(2,1)S(1)} %get-tuple-element.115.refs_2_.a), channel_id=1, source_target_pairs={{24,16},{28,20},{2,10},{6,14},{25,17},{29,21},{3,11},{7,15}} | collective-permute-start | bytes 2064392 | tf_op jit(solution)/shard_map/ppermute | solution.py:176
  107.9 18.2 %collective-permute-start.30 = (bf16[128,2688]{1,0:T(8,128)(2,1)S(1)}, bf16[128,2688]{1,0:T(8,128)(2,1)S(1)}, u32[]{:S(2)}, u32[]{:S(2)}) collective-permute-start(bf16[128,2688]{1,0:T(8,128)(2,1)S(1)} %get-tuple-element.111.refs_0_), channel_id=1, source_target_pairs={{0,8},{4,12},{26,18},{30,22},{1,9},{5,13},{27,19},{31,23}} | collective-permute-start | bytes 2064392 | tf_op jit(solution)/shard_map/ppermute | solution.py:176
  123.0 34.4 %collective-permute-start.38 = (bf16[256,2688]{1,0:T(8,128)(2,1)S(1)}, bf16[256,2688]{1,0:T(8,128)(2,1)S(1)}, u32[]{:S(2)}, u32[]{:S(2)}) collective-permute-start(bf16[256,2688]{1,0:T(8,128)(2,1)S(1)} %input_grad.2), channel_id=1, source_target_pairs={{0,4},{2,6},{4,0},{6,2},{8,12},{10,14},{12,8},{14,10},{16,20},{18,... | collective-permute-start | bytes 4128776 | tf_op jit(solution)/shard_map/ppermute | solution.py:176
  127.7 18.7 %collective-permute-start.35 = (bf16[128,2688]{1,0:T(8,128)(2,1)S(1)}, bf16[128,2688]{1,0:T(8,128)(2,1)S(1)}, u32[]{:S(2)}, u32[]{:S(2)}) collective-permute-start(bf16[128,2688]{1,0:T(8,128)(2,1)S(1)} %get-tuple-element.120), channel_id=1, source_target_pairs={{16,8},{20,12},{10,18},{14,22},{17,9},{21,13},{11,19},{15,23}} | collective-permute-start | bytes 2064392 | tf_op jit(solution)/shard_map/ppermute | solution.py:176
  129.2 25.2 %collective-permute-start.39 = (bf16[128,2688]{1,0:T(8,128)(2,1)S(1)}, bf16[128,2688]{1,0:T(8,128)(2,1)S(1)}, u32[]{:S(2)}, u32[]{:S(2)}) collective-permute-start(bf16[128,2688]{1,0:T(8,128)(2,1)S(1)} %sums.6), channel_id=1, source_target_pairs={{16,8},{20,12},{10,18},{14,22},{17,9},{21,13},{11,19},{15,23}} | collective-permute-start | bytes 2064392 | tf_op jit(solution)/shard_map/ppermute | solution.py:176
  130.5 23.9 %collective-permute-start.40 = (bf16[128,2688]{1,0:T(8,128)(2,1)S(1)}, bf16[128,2688]{1,0:T(8,128)(2,1)S(1)}, u32[]{:S(2)}, u32[]{:S(2)}) collective-permute-start(bf16[128,2688]{1,0:T(8,128)(2,1)S(1)} %get-tuple-element.129.refs_0_), channel_id=1, source_target_pairs={{0,8},{4,12},{26,18},{30,22},{1,9},{5,13},{27,19},{31,23}} | collective-permute-start | bytes 2064392 | tf_op jit(solution)/shard_map/ppermute | solution.py:176
  146.6 12.3 %collective-permute-start.43 = (bf16[128,2688]{1,0:T(8,128)(2,1)S(1)}, bf16[128,2688]{1,0:T(8,128)(2,1)S(1)}, u32[]{:S(2)}, u32[]{:S(2)}) collective-permute-start(bf16[128,2688]{1,0:T(8,128)(2,1)S(1)} %sums.7), channel_id=1, source_target_pairs={{8,0},{12,4},{18,26},{22,30},{2,10},{6,14},{24,16},{28,20},{9,1},{... | collective-permute-start | bytes 2064392 | tf_op jit(solution)/shard_map/ppermute | solution.py:176
  (28 other events, 259.8 us)

commit v7 on v6

--- a/solution.py
+++ b/solution.py
@@ -162,6 +162,7 @@
 
 MIB = 1 << 20
 MASKED = 16384.0
+LOG2_E = 1.4426950408889634
 NT = (((1,), (1,)), ((), ()))
 HBM = pl.BlockSpec(memory_space=pltpu.HBM)
 SMEM = pl.BlockSpec(memory_space=pltpu.SMEM)
@@ -408,12 +409,12 @@
     heads, grads = [], []
     for g in range(2):
         lanes = slice(g * HD, (g + 1) * HD)
-        query = normalized(q_ref[0, :, lanes].astype(jnp.float32), gain_ref[...], query_scale)
+        query = normalized(q_ref[0, :, lanes].astype(jnp.float32), gain_ref[...], query_scale * LOG2_E)
         heads.append(jnp.concatenate([query.T.astype(jnp.bfloat16), query_mark[...]], axis=0))
         grads.append(go_ref[0, :, lanes].astype(jnp.float32).T)
     query_t = jnp.concatenate(heads, axis=1)
     span = pl.ds(pl.multiple_of(block * rows, rows), chunks * rows)
-    e = jnp.exp(dot(keys_v[span, :], query_t))
+    e = jnp.exp2(dot(keys_v[span, :], query_t))
     e = jnp.concatenate(
         [
             jnp.where(behind, 0.0, e[:rows]),

time: 174 us -> 174 us (level)
  no operation moved by 1% of the time
where the time goes in v7:
time: 174 us; the launch traced here: 173 us
  waiting for transfers between devices  63.6 us (37%)
  starting transfers between devices  62.3 us (36%)
  Pallas kernels  38.7 us (22%)
  other arithmetic  5.18 us (3%)
  local copies, waits for them, and re-layouts  2.05 us (1%)
    ppermute x42, starting transfers between devices, move(): return lax.ppermute(array, 'seq', [(at(*a), at(*b)) for a, b in rule])  58.7 us
    ppermute x42, waiting for transfers between devices, move(): return lax.ppermute(array, 'seq', [(at(*a), at(*b)) for a, b in rule])  53.7 us
    ppermute x4, waiting for transfers between devices, swap_uly(): return lax.ppermute(array, 'uly', [(0, 1), (1, 0)])  9.92 us
    pallas_call x2, Pallas kernels, project(): call(project_kernel, [shaped((4 * rows, width)), shaped((4 * rows, width)...  7.17 us
    pallas_call x1, Pallas kernels, attend_values(): call(values_kernel, [shaped((2, 2, rows, 2 * HD)), shaped((2, 2, rows, 2...  7.03 us
    pallas_call x1, Pallas kernels, attend_scores(): call(scores_kernel, [shaped((blocks, span, 2 * rows)), shaped((blocks, 8,...  6.34 us
    pallas_call x2, Pallas kernels, weight_grad(): call(weight_grad_kernel, [shaped((width, features)), shaped((width, featu...  4.8 us
    pallas_call x2, Pallas kernels, input_grad(): call(functools.partial(input_grad_kernel, piece), shaped((rows, features)...  4.69 us
  transfers between devices with their start and end apart: 46, of which 22 were waited for; matrix products, arithmetic and copies ran while one was open for 4% of the time, Pallas kernels for 21%

profile of v7, /device:TPU:17, one launch (start us, length us, event | category | flops | bytes accessed | tf_op | source)
XLA Modules:
  0.0 173.1 jit_solution(9238297897613258881)
XLA Ops:
  0.6 2.6 %collective-permute-start.6 = (bf16[64,2688]{1,0:T(8,128)(2,1)}, bf16[64,2688]{1,0:T(8,128)(2,1)S(1)}, u32[]{:S(2)}, u32[]{:S(2)}) collective-permute-start(bf16[64,2688]{1,0:T(8,128)(2,1)} %bitcast.36), channel_id=1, source_target_pairs={{2,0},{6,4},{8,10},{12,14},{18,16},{22,20},{24,26},{28,30},{3,1},{... | collective-permute-start | bytes 1032200 | tf_op jit(solution)/shard_map/ppermute | solution.py:177
  15.5 4.9 %collective-permute-done.3.refs_6_ = bf16[128,2688]{1,0:T(8,128)(2,1)} collective-permute-done((bf16[128,2688]{1,0:T(8,128)(2,1)}, bf16[128,2688]{1,0:T(8,128)(2,1)}, u32[]{:S(2)}, u32[]{:S(2)}) %collective-permute-start.3) | collective-permute-done | bytes 688160 | tf_op jit(solution)/shard_map/ppermute | solution.py:177
  21.6 3.0 %collective-permute-start.4 = (bf16[128,2688]{1,0:T(8,128)(2,1)}, bf16[128,2688]{1,0:T(8,128)(2,1)}, u32[]{:S(2)}, u32[]{:S(2)}) collective-permute-start(bf16[128,2688]{1,0:T(8,128)(2,1)} %collective-permute-done.2.refs_5_), channel_id=1, source_target_pairs={{8,16},{12,20},{18,10},{22,14},{9,17},{13,21},{19,11},{23,15}} | collective-permute-start | bytes 2064392 | tf_op jit(solution)/shard_map/ppermute | solution.py:177
  29.1 3.3 %collective-permute-start.11 = (bf16[128,2688]{1,0:T(8,128)(2,1)}, bf16[128,2688]{1,0:T(8,128)(2,1)}, u32[]{:S(2)}, u32[]{:S(2)}) collective-permute-start(bf16[128,2688]{1,0:T(8,128)(2,1)} %collective-permute-done.7.refs_5_), channel_id=1, source_target_pairs={{8,16},{12,20},{18,10},{22,14},{9,17},{13,21},{19,11},{23,15}} | collective-permute-start | bytes 2064392 | tf_op jit(solution)/shard_map/ppermute | solution.py:177
  40.9 6.2 %collective-permute-done.12.refs_8_ = bf16[128,2688]{1,0:T(8,128)(2,1)} collective-permute-done((bf16[128,2688]{1,0:T(8,128)(2,1)}, bf16[128,2688]{1,0:T(8,128)(2,1)}, u32[]{:S(2)}, u32[]{:S(2)}) %collective-permute-start.12) | collective-permute-done | bytes 688160 | tf_op jit(solution)/shard_map/ppermute | solution.py:177
  50.9 3.6 %project.2 = (bf16[1024,128]{1,0:T(8,128)(2,1)S(1)}, bf16[1024,128]{1,0:T(8,128)(2,1)S(1)}, bf16[256,2688]{1,0:T(8,128)(2,1)S(1)}) custom-call(s32[7]{0:T(128)S(1)} %stack.71.code, bf16[256,2688]{1,0:T(8,128)(2,1)S(1)} %copy-done, bf16[256,2688]{1,0:T(8,128)(2,1)S(1)} %collective-permute-done.9.refs_1_.a1, ...), custom_call_target="tpu_custom_call" | custom-call | tf_op jit(solution)/shard_map/project/pallas_call | solution.py:361
  55.8 5.7 %collective-permute-done.16 = bf16[4,256,256]{2,1,0:T(8,128)(2,1)S(1)} collective-permute-done((bf16[4,256,256]{2,1,0:T(8,128)(2,1)S(1)}, bf16[4,256,256]{2,1,0:T(8,128)(2,1)S(1)}, u32[]{:S(2)}, u32[]{:S(2)}) %collective-permute-start.16) | collective-permute-done | bytes 524320 | tf_op jit(solution)/shard_map/ppermute | solution.py:177
  61.5 3.6 %project.3 = (bf16[1024,128]{1,0:T(8,128)(2,1)S(1)}, bf16[1024,128]{1,0:T(8,128)(2,1)S(1)}, bf16[256,2688]{1,0:T(8,128)(2,1)S(1)}) custom-call(s32[7]{0:T(128)S(1)} %stack.71.code, bf16[256,2688]{1,0:T(8,128)(2,1)S(1)} %copy-done, bf16[256,2688]{1,0:T(8,128)(2,1)S(1)} %collective-permute-done.9.refs_1_.a1, ...), custom_call_target="tpu_custom_call" | custom-call | tf_op jit(solution)/shard_map/project/pallas_call | solution.py:361
  69.6 2.5 %collective-permute-done.15 = bf16[1024,128]{1,0:T(8,128)(2,1)S(1)} collective-permute-done((bf16[1024,128]{1,0:T(8,128)(2,1)S(1)}, bf16[1024,128]{1,0:T(8,128)(2,1)S(1)}, u32[]{:S(2)}, u32[]{:S(2)}) %collective-permute-start.15) | collective-permute-done | bytes 262176 | tf_op jit(solution)/shard_map/ppermute | solution.py:197
  74.2 2.7 %collective-permute-done.19.before_ref = bf16[1024,128]{1,0:T(8,128)(2,1)S(1)} collective-permute-done((bf16[1024,128]{1,0:T(8,128)(2,1)S(1)}, bf16[1024,128]{1,0:T(8,128)(2,1)S(1)}, u32[]{:S(2)}, u32[]{:S(2)}) %collective-permute-start.19) | collective-permute-done | bytes 262176 | tf_op jit(solution)/shard_map/ppermute | solution.py:177
  77.0 6.3 %attend_scores.1 = (bf16[4,1280,512]{2,1,0:T(8,128)(2,1)S(1)}, f32[4,8,512]{2,1,0:T(8,128)S(1)}, f32[1024,128]{1,0:T(8,128)S(1)}, bf16[1024,128]{1,0:T(8,128)(2,1)S(1)}) custom-call(s32[7]{0:T(128)S(1)} %stack.71.code, bf16[4,256,256]{2,1,0:T(8,128)(2,1)S(1)} %pad_maximum_fusion.4.q_ref, bf16[4,256,256]{2,1,0:T(8,128)(2,1)S(1)} %pad_maximum_fusion.5.go_ref, ...), custom_call_target="tpu_custom_call" | custom-call | tf_op jit(solution)/shard_map/attend_scores/pallas_call | solution.py:449
  83.3 3.3 %collective-permute-start.26 = (bf16[1024,128]{1,0:T(8,128)(2,1)S(1)}, bf16[1024,128]{1,0:T(8,128)(2,1)S(1)}, u32[]{:S(2)}, u32[]{:S(2)}) collective-permute-start(bf16[1024,128]{1,0:T(8,128)(2,1)S(1)} %get-tuple-element.108), channel_id=1, source_target_pairs={{8,0},{12,4},{10,2},{14,6},{16,8},{20,12},{18,10},{22,14},{24,16},... | collective-permute-start | bytes 786440 | tf_op jit(solution)/shard_map/ppermute | solution.py:177
  86.7 7.0 %attend_values.1 = (bf16[2,2,256,256]{3,2,1,0:T(8,128)(2,1)S(1)}, bf16[2,2,256,256]{3,2,1,0:T(8,128)(2,1)S(1)}, f32[1024,128]{1,0:T(8,128)S(1)}, bf16[1024,128]{1,0:T(8,128)(2,1)S(1)}) custom-call(s32[7]{0:T(128)S(1)} %stack.71.code, bf16[4,256,256]{2,1,0:T(8,128)(2,1)S(1)} %pad_maximum_fusion.4.q_ref, bf16[4,256,256]{2,1,0:T(8,128)(2,1)S(1)} %pad_maximum_fusion.5.go_ref, ...), custom_call_target="tpu_custom_call" | custom-call | tf_op jit(solution)/shard_map/attend_values/pallas_call | solution.py:546
  98.9 4.5 %collective-permute-done.27.theirs.refs_5_ = bf16[1024,128]{1,0:T(8,128)(2,1)S(1)} collective-permute-done((bf16[1024,128]{1,0:T(8,128)(2,1)S(1)}, bf16[1024,128]{1,0:T(8,128)(2,1)S(1)}, u32[]{:S(2)}, u32[]{:S(2)}) %collective-permute-start.27) | collective-permute-done | bytes 262176 | tf_op jit(solution)/shard_map/ppermute | solution.py:197
  103.4 2.4 %weight_grad.2 = (bf16[128,2688]{1,0:T(8,128)(2,1)S(1)}, bf16[128,2688]{1,0:T(8,128)(2,1)S(1)}) custom-call(s32[7]{0:T(128)S(1)} %stack.71.code, bf16[1024,128]{1,0:T(8,128)(2,1)S(1)} %add_convert_fusion.mine.refs_4_, bf16[1024,128]{1,0:T(8,128)(2,1)S(1)} %collective-permute-done.27.theirs.refs_5_, bf16[256,2688]{1,0:T(8,128)(2,1)S(1)} %copy-done, ...), custom_call_target="tpu_custom_call" | custom-call | tf_op jit(solution)/shard_map/weight_grad/pallas_call | solution.py:607
  110.6 2.9 %collective-permute-done.28.theirs.refs_1_ = bf16[1024,128]{1,0:T(8,128)(2,1)S(1)} collective-permute-done((bf16[1024,128]{1,0:T(8,128)(2,1)S(1)}, bf16[1024,128]{1,0:T(8,128)(2,1)S(1)}, u32[]{:S(2)}, u32[]{:S(2)}) %collective-permute-start.28) | collective-permute-done | bytes 262176 | tf_op jit(solution)/shard_map/ppermute | solution.py:197
  115.2 2.4 %weight_grad.3 = (bf16[128,2688]{1,0:T(8,128)(2,1)S(1)}, bf16[128,2688]{1,0:T(8,128)(2,1)S(1)}) custom-call(s32[7]{0:T(128)S(1)} %stack.71.code, bf16[1024,128]{1,0:T(8,128)(2,1)S(1)} %multiply_convert_fusion.mine.refs_0_, bf16[1024,128]{1,0:T(8,128)(2,1)S(1)} %collective-permute-done.28.theirs.refs_1_, bf16[256,2688]{1,0:T(8,128)(2,1)S(1)} %copy-done, ...), custom_call_target="tpu_custom_call" | custom-call | tf_op jit(solution)/shard_map/weight_grad/pallas_call | solution.py:607
  120.6 2.3 %input_grad.2 = bf16[256,2688]{1,0:T(8,128)(2,1)S(1)} custom-call(s32[7]{0:T(128)S(1)} %stack.71.code, bf16[1024,128]{1,0:T(8,128)(2,1)S(1)} %multiply_convert_fusion.mine.refs_0_, bf16[1024,128]{1,0:T(8,128)(2,1)S(1)} %collective-permute-done.28.theirs.refs_1_, bf16[1024,128]{1,0:T(8,128)(2,1)S(1)} %collective-permute-done.31.refs_2_, ...), custom_call_target="tpu_custom_call" | custom-call | tf_op jit(solution)/shard_map/input_grad/pallas_call | solution.py:635
  131.7 2.3 %input_grad.3.refs_0_ = bf16[256,2688]{1,0:T(8,128)(2,1)S(1)} custom-call(s32[7]{0:T(128)S(1)} %stack.71.code, bf16[1024,128]{1,0:T(8,128)(2,1)S(1)} %multiply_convert_fusion.mine.refs_0_, bf16[1024,128]{1,0:T(8,128)(2,1)S(1)} %collective-permute-done.28.theirs.refs_1_, bf16[1024,128]{1,0:T(8,128)(2,1)S(1)} %collective-permute-done.31.refs_2_, ...), custom_call_target="tpu_custom_call" | custom-call | tf_op jit(solution)/shard_map/input_grad/pallas_call | solution.py:635
  134.1 2.3 %collective-permute-done.36.b = bf16[128,2688]{1,0:T(8,128)(2,1)S(1)} collective-permute-done((bf16[128,2688]{1,0:T(8,128)(2,1)S(1)}, bf16[128,2688]{1,0:T(8,128)(2,1)S(1)}, u32[]{:S(2)}, u32[]{:S(2)}) %collective-permute-start.36) | collective-permute-done | bytes 688160 | tf_op jit(solution)/shard_map/ppermute | solution.py:177
  136.4 9.9 %collective-permute-done.35.refs_1_ = bf16[128,2688]{1,0:T(8,128)(2,1)S(1)} collective-permute-done((bf16[128,2688]{1,0:T(8,128)(2,1)S(1)}, bf16[128,2688]{1,0:T(8,128)(2,1)S(1)}, u32[]{:S(2)}, u32[]{:S(2)}) %collective-permute-start.35) | collective-permute-done | bytes 688160 | tf_op jit(solution)/shard_map/ppermute | solution.py:177
  149.5 4.9 %collective-permute-done.39.refs_1_ = bf16[128,2688]{1,0:T(8,128)(2,1)S(1)} collective-permute-done((bf16[128,2688]{1,0:T(8,128)(2,1)S(1)}, bf16[128,2688]{1,0:T(8,128)(2,1)S(1)}, u32[]{:S(2)}, u32[]{:S(2)}) %collective-permute-start.39) | collective-permute-done | bytes 688160 | tf_op jit(solution)/shard_map/ppermute | solution.py:177
  160.9 3.4 %collective-permute-done.44.other = bf16[64,2688]{1,0:T(8,128)(2,1)S(1)} collective-permute-done((bf16[64,2688]{1,0:T(8,128)(2,1)S(1)}, bf16[64,2688]{1,0:T(8,128)(2,1)S(1)}, u32[]{:S(2)}, u32[]{:S(2)}) %collective-permute-start.44) | collective-permute-done | bytes 344096 | tf_op jit(solution)/shard_map/ppermute | solution.py:177
  167.9 3.8 %collective-permute-done.45.other = bf16[64,2688]{1,0:T(8,128)(2,1)S(1)} collective-permute-done((bf16[64,2688]{1,0:T(8,128)(2,1)S(1)}, bf16[64,2688]{1,0:T(8,128)(2,1)S(1)}, u32[]{:S(2)}, u32[]{:S(2)}) %collective-permute-start.45) | collective-permute-done | bytes 344096 | tf_op jit(solution)/shard_map/ppermute | solution.py:177
  (125 shorter events, 75.9 us)
Async XLA Ops:
  4.6 32.4 %collective-permute-start = (bf16[256,2688]{1,0:T(8,128)(2,1)}, bf16[256,2688]{1,0:T(8,128)(2,1)S(1)}, u32[]{:S(2)}, u32[]{:S(2)}) collective-permute-start(bf16[256,2688]{1,0:T(8,128)(2,1)} %a0.3), channel_id=1, source_target_pairs={{0,4},{2,6},{4,0},{6,2},{8,12},{10,14},{12,8},{14,10},{16,20},{18,... | collective-permute-start | bytes 4128776 | tf_op jit(solution)/shard_map/ppermute | solution.py:177
  8.2 12.2 %collective-permute-start.3 = (bf16[128,2688]{1,0:T(8,128)(2,1)}, bf16[128,2688]{1,0:T(8,128)(2,1)}, u32[]{:S(2)}, u32[]{:S(2)}) collective-permute-start(bf16[128,2688]{1,0:T(8,128)(2,1)} %pad_maximum_fusion.refs_4_), channel_id=1, source_target_pairs={{10,18},{14,22},{16,8},{20,12},{11,19},{15,23},{17,9},{21,13}} | collective-permute-start | bytes 2064392 | tf_op jit(solution)/shard_map/ppermute | solution.py:177
  9.4 12.2 %collective-permute-start.2 = (bf16[128,2688]{1,0:T(8,128)(2,1)}, bf16[128,2688]{1,0:T(8,128)(2,1)}, u32[]{:S(2)}, u32[]{:S(2)}) collective-permute-start(bf16[128,2688]{1,0:T(8,128)(2,1)} %pad_maximum_fusion.refs_4_), channel_id=1, source_target_pairs={{0,8},{4,12},{26,18},{30,22},{10,2},{14,6},{16,24},{20,28},{1,9},{... | collective-permute-start | bytes 2064392 | tf_op jit(solution)/shard_map/ppermute | solution.py:177
  10.8 17.5 %collective-permute-start.8 = (bf16[128,2688]{1,0:T(8,128)(2,1)S(1)}, bf16[128,2688]{1,0:T(8,128)(2,1)}, u32[]{:S(2)}, u32[]{:S(2)}) collective-permute-start(bf16[128,2688]{1,0:T(8,128)(2,1)S(1)} %pad_maximum_fusion.1.refs_4_), channel_id=1, source_target_pairs={{10,18},{14,22},{16,8},{20,12},{11,19},{15,23},{17,9},{21,13}} | collective-permute-start | bytes 2064392 | tf_op jit(solution)/shard_map/ppermute | solution.py:177
  12.1 17.0 %collective-permute-start.7 = (bf16[128,2688]{1,0:T(8,128)(2,1)S(1)}, bf16[128,2688]{1,0:T(8,128)(2,1)}, u32[]{:S(2)}, u32[]{:S(2)}) collective-permute-start(bf16[128,2688]{1,0:T(8,128)(2,1)S(1)} %pad_maximum_fusion.1.refs_4_), channel_id=1, source_target_pairs={{0,8},{4,12},{26,18},{30,22},{10,2},{14,6},{16,24},{20,28},{1,9},{... | collective-permute-start | bytes 2064392 | tf_op jit(solution)/shard_map/ppermute | solution.py:177
  21.6 12.9 %collective-permute-start.4 = (bf16[128,2688]{1,0:T(8,128)(2,1)}, bf16[128,2688]{1,0:T(8,128)(2,1)}, u32[]{:S(2)}, u32[]{:S(2)}) collective-permute-start(bf16[128,2688]{1,0:T(8,128)(2,1)} %collective-permute-done.2.refs_5_), channel_id=1, source_target_pairs={{8,16},{12,20},{18,10},{22,14},{9,17},{13,21},{19,11},{23,15}} | collective-permute-start | bytes 2064392 | tf_op jit(solution)/shard_map/ppermute | solution.py:177
  32.4 14.8 %collective-permute-start.12 = (bf16[128,2688]{1,0:T(8,128)(2,1)}, bf16[128,2688]{1,0:T(8,128)(2,1)}, u32[]{:S(2)}, u32[]{:S(2)}) collective-permute-start(bf16[128,2688]{1,0:T(8,128)(2,1)} %collective-permute-done.8.refs_6_), channel_id=1, source_target_pairs={{8,0},{12,4},{18,26},{22,30},{9,1},{13,5},{19,27},{23,31}} | collective-permute-start | bytes 2064392 | tf_op jit(solution)/shard_map/ppermute | solution.py:177
  34.5 16.3 %collective-permute-start.9 = (bf16[256,2688]{1,0:T(8,128)(2,1)S(1)}, bf16[256,2688]{1,0:T(8,128)(2,1)S(1)}, u32[]{:S(2)}, u32[]{:S(2)}) collective-permute-start(bf16[256,2688]{1,0:T(8,128)(2,1)S(1)} %copy-done), channel_id=1, source_target_pairs={{0,2},{2,0},{4,6},{6,4},{8,10},{10,8},{12,14},{14,12},{16,18},{18,... | collective-permute-start | bytes 4128776 | tf_op jit(solution)/shard_map/ppermute | solution.py:177
  36.2 14.7 %collective-permute-start.14 = (bf16[128,2688]{1,0:T(8,128)(2,1)}, bf16[128,2688]{1,0:T(8,128)(2,1)S(1)}, u32[]{:S(2)}, u32[]{:S(2)}) collective-permute-start(bf16[128,2688]{1,0:T(8,128)(2,1)} %collective-permute-done.4.refs_7_), channel_id=1, source_target_pairs={{16,24},{20,28},{10,2},{14,6},{17,25},{21,29},{11,3},{15,7}} | collective-permute-start | bytes 2064392 | tf_op jit(solution)/shard_map/ppermute | solution.py:177
  36.9 13.9 %collective-permute-start.10 = (bf16[256,2688]{1,0:T(8,128)(2,1)S(1)}, bf16[256,2688]{1,0:T(8,128)(2,1)S(1)}, u32[]{:S(2)}, u32[]{:S(2)}) collective-permute-start(bf16[256,2688]{1,0:T(8,128)(2,1)S(1)} %collective-permute-done.refs_2_.a2), channel_id=1, source_target_pairs={{0,2},{2,0},{4,6},{6,4},{8,10},{10,8},{12,14},{14,12},{16,18},{18,... | collective-permute-start | bytes 4128776 | tf_op jit(solution)/shard_map/ppermute | solution.py:177
  47.1 14.3 %collective-permute-start.13 = (bf16[128,2688]{1,0:T(8,128)(2,1)}, bf16[128,2688]{1,0:T(8,128)(2,1)S(1)}, u32[]{:S(2)}, u32[]{:S(2)}) collective-permute-start(bf16[128,2688]{1,0:T(8,128)(2,1)} %collective-permute-done.11.refs_7_), channel_id=1, source_target_pairs={{16,24},{20,28},{10,2},{14,6},{17,25},{21,29},{11,3},{15,7}} | collective-permute-start | bytes 2064392 | tf_op jit(solution)/shard_map/ppermute | solution.py:177
  49.2 12.3 %collective-permute-start.16 = (bf16[4,256,256]{2,1,0:T(8,128)(2,1)S(1)}, bf16[4,256,256]{2,1,0:T(8,128)(2,1)S(1)}, u32[]{:S(2)}, u32[]{:S(2)}) collective-permute-start(bf16[4,256,256]{2,1,0:T(8,128)(2,1)S(1)} %pad_maximum_fusion.2), channel_id=1, source_target_pairs={{0,4},{2,6},{4,0},{6,2},{8,12},{10,14},{12,8},{14,10},{16,20},{18,... | collective-permute-start | bytes 1572872 | tf_op jit(solution)/shard_map/ppermute | solution.py:177
  54.5 12.7 %collective-permute-start.18 = (bf16[1024,128]{1,0:T(8,128)(2,1)S(1)}, bf16[1024,128]{1,0:T(8,128)(2,1)S(1)}, u32[]{:S(2)}, u32[]{:S(2)}) collective-permute-start(bf16[1024,128]{1,0:T(8,128)(2,1)S(1)} %get-tuple-element.86), channel_id=1, source_target_pairs={{0,1},{1,0},{2,3},{3,2},{4,5},{5,4},{6,7},{7,6},{8,9},{9,8},{10,11... | collective-permute-start | bytes 786440 | tf_op jit(solution)/shard_map/ppermute | solution.py:197
  66.6 20.1 %collective-permute-start.22 = (bf16[256,2688]{1,0:T(8,128)(2,1)S(1)}, bf16[256,2688]{1,0:T(8,128)(2,1)S(1)}, u32[]{:S(2)}, u32[]{:S(2)}) collective-permute-start(bf16[256,2688]{1,0:T(8,128)(2,1)S(1)} %get-tuple-element.100.refs_10_), channel_id=1, source_target_pairs={{0,2},{2,0},{4,6},{6,4},{8,10},{10,8},{12,14},{14,12},{16,18},{18,... | collective-permute-start | bytes 4128776 | tf_op jit(solution)/shard_map/ppermute | solution.py:177
  67.1 19.6 %collective-permute-start.21 = (bf16[256,2688]{1,0:T(8,128)(2,1)S(1)}, bf16[256,2688]{1,0:T(8,128)(2,1)S(1)}, u32[]{:S(2)}, u32[]{:S(2)}) collective-permute-start(bf16[256,2688]{1,0:T(8,128)(2,1)S(1)} %get-tuple-element.99.refs_8_), channel_id=1, source_target_pairs={{0,2},{2,0},{4,6},{6,4},{8,10},{10,8},{12,14},{14,12},{16,18},{18,... | collective-permute-start | bytes 4128776 | tf_op jit(solution)/shard_map/ppermute | solution.py:177
  72.2 14.5 %collective-permute-start.20 = (bf16[1024,128]{1,0:T(8,128)(2,1)S(1)}, bf16[1024,128]{1,0:T(8,128)(2,1)S(1)}, u32[]{:S(2)}, u32[]{:S(2)}) collective-permute-start(bf16[1024,128]{1,0:T(8,128)(2,1)S(1)} %add_convert_fusion.1.v_own), channel_id=1, source_target_pairs={{0,8},{4,12},{2,10},{6,14},{8,16},{12,20},{10,18},{14,22},{16,24},... | collective-permute-start | bytes 786440 | tf_op jit(solution)/shard_map/ppermute | solution.py:177
  97.9 20.5 %collective-permute-start.24 = (bf16[2,2,256,256]{3,2,1,0:T(8,128)(2,1)S(1)}, bf16[2,2,256,256]{3,2,1,0:T(8,128)(2,1)S(1)}, u32[]{:S(2)}, u32[]{:S(2)}) collective-permute-start(bf16[2,2,256,256]{3,2,1,0:T(8,128)(2,1)S(1)} %pack.1), channel_id=1, source_target_pairs={{0,4},{2,6},{4,0},{6,2},{8,12},{10,14},{12,8},{14,10},{16,20},{18,... | collective-permute-start | bytes 1572872 | tf_op jit(solution)/shard_map/ppermute | solution.py:177
  107.1 16.9 %collective-permute-start.29 = (bf16[128,2688]{1,0:T(8,128)(2,1)S(1)}, bf16[128,2688]{1,0:T(8,128)(2,1)S(1)}, u32[]{:S(2)}, u32[]{:S(2)}) collective-permute-start(bf16[128,2688]{1,0:T(8,128)(2,1)S(1)} %get-tuple-element.115.refs_2_.a), channel_id=1, source_target_pairs={{24,16},{28,20},{2,10},{6,14},{25,17},{29,21},{3,11},{7,15}} | collective-permute-start | bytes 2064392 | tf_op jit(solution)/shard_map/ppermute | solution.py:177
  107.8 18.2 %collective-permute-start.30 = (bf16[128,2688]{1,0:T(8,128)(2,1)S(1)}, bf16[128,2688]{1,0:T(8,128)(2,1)S(1)}, u32[]{:S(2)}, u32[]{:S(2)}) collective-permute-start(bf16[128,2688]{1,0:T(8,128)(2,1)S(1)} %get-tuple-element.111.refs_0_), channel_id=1, source_target_pairs={{0,8},{4,12},{26,18},{30,22},{1,9},{5,13},{27,19},{31,23}} | collective-permute-start | bytes 2064392 | tf_op jit(solution)/shard_map/ppermute | solution.py:177
  122.9 34.5 %collective-permute-start.38 = (bf16[256,2688]{1,0:T(8,128)(2,1)S(1)}, bf16[256,2688]{1,0:T(8,128)(2,1)S(1)}, u32[]{:S(2)}, u32[]{:S(2)}) collective-permute-start(bf16[256,2688]{1,0:T(8,128)(2,1)S(1)} %input_grad.2), channel_id=1, source_target_pairs={{0,4},{2,6},{4,0},{6,2},{8,12},{10,14},{12,8},{14,10},{16,20},{18,... | collective-permute-start | bytes 4128776 | tf_op jit(solution)/shard_map/ppermute | solution.py:177
  127.6 18.7 %collective-permute-start.35 = (bf16[128,2688]{1,0:T(8,128)(2,1)S(1)}, bf16[128,2688]{1,0:T(8,128)(2,1)S(1)}, u32[]{:S(2)}, u32[]{:S(2)}) collective-permute-start(bf16[128,2688]{1,0:T(8,128)(2,1)S(1)} %get-tuple-element.120), channel_id=1, source_target_pairs={{16,8},{20,12},{10,18},{14,22},{17,9},{21,13},{11,19},{15,23}} | collective-permute-start | bytes 2064392 | tf_op jit(solution)/shard_map/ppermute | solution.py:177
  129.1 25.2 %collective-permute-start.39 = (bf16[128,2688]{1,0:T(8,128)(2,1)S(1)}, bf16[128,2688]{1,0:T(8,128)(2,1)S(1)}, u32[]{:S(2)}, u32[]{:S(2)}) collective-permute-start(bf16[128,2688]{1,0:T(8,128)(2,1)S(1)} %sums.6), channel_id=1, source_target_pairs={{16,8},{20,12},{10,18},{14,22},{17,9},{21,13},{11,19},{15,23}} | collective-permute-start | bytes 2064392 | tf_op jit(solution)/shard_map/ppermute | solution.py:177
  130.4 23.9 %collective-permute-start.40 = (bf16[128,2688]{1,0:T(8,128)(2,1)S(1)}, bf16[128,2688]{1,0:T(8,128)(2,1)S(1)}, u32[]{:S(2)}, u32[]{:S(2)}) collective-permute-start(bf16[128,2688]{1,0:T(8,128)(2,1)S(1)} %get-tuple-element.129.refs_0_), channel_id=1, source_target_pairs={{0,8},{4,12},{26,18},{30,22},{1,9},{5,13},{27,19},{31,23}} | collective-permute-start | bytes 2064392 | tf_op jit(solution)/shard_map/ppermute | solution.py:177
  146.5 12.3 %collective-permute-start.43 = (bf16[128,2688]{1,0:T(8,128)(2,1)S(1)}, bf16[128,2688]{1,0:T(8,128)(2,1)S(1)}, u32[]{:S(2)}, u32[]{:S(2)}) collective-permute-start(bf16[128,2688]{1,0:T(8,128)(2,1)S(1)} %sums.7), channel_id=1, source_target_pairs={{8,0},{12,4},{18,26},{22,30},{2,10},{6,14},{24,16},{28,20},{9,1},{... | collective-permute-start | bytes 2064392 | tf_op jit(solution)/shard_map/ppermute | solution.py:177
  (28 other events, 259.8 us)
